TPU v7x, 32 devices: a whole 2x2x4 slice. The times are simulated.
32 devices in a mesh: row: 4 (over y, x), col: 8 (over z, core).
Axes of the slice: x: 2, y: 2, z: 4, core: 2. Of those that a mesh axis runs over, the one named last changes fastest.
Arguments:
- features: bfloat16 [4096, 256], P(('col', 'row')), may hold values from -6 to 6
- weight: bfloat16 [256, 256], replicated, may hold values from -0.375 to 0.375
- bias_term: float32 [256], replicated, may hold values from -3 to 3
- block_values: bfloat16 [4, 8, 16, 128, 128], P('row', 'col'), may hold values from -0.21875 to 0.21875
- block_rows: int32 [4, 8, 16], P('row', 'col'), may hold values from 0 to 7, as said below
- block_cols: int32 [4, 8, 16], P('row', 'col'), may hold values from 0 to 3, as said below
- counts: int32 [4, 8], P('row', 'col'), may hold values from 1 to 16, as said below
- cluster_order: int32 [4096], P('col'), may hold values from 0 to 511, as said below
- cotangent: bfloat16 [4096, 256], P(('row', 'col')), may hold values from -6 to 6
Outputs:
- activations: bfloat16 [4096, 256], P(('row', 'col'))
- grad_features: bfloat16 [4096, 256], P(('col', 'row'))
- grad_weight: float32 [256, 256], replicated
Inputs may be any that keep to these rules, and one draw needn't show every extreme that they name: Slots from counts on are ignored; some tile holds 16 live slots. `block_rows`: within one tile, the slots name distinct pairs of block row and block column. `block_cols`: paired with block_rows as stated there. `cluster_order`: each run of 512 entries that starts at a multiple of 512 is a permutation of 0 to 511.
All inputs are finite; a program needn't handle non-finite values.
Results may differ from a plain program's by a relative error of at most 0.015.
Values may be sent and summed in bfloat16 or wider, within the bound.
No kernel may reach another device: no remote copies, remote signals or barrier semaphores. Data moves between devices by JAX's collectives and lax.ppermute only.
A program may use at most 64 MiB of HBM per device.

v0:
```python
import math

import jax
import jax.numpy as jnp
from jax import lax
from jax.sharding import PartitionSpec as P


def silu_slope(preact):
    sigmoid_value = jax.nn.sigmoid(preact)
    return sigmoid_value * (1.0 + preact * (1.0 - sigmoid_value))


def shards(
    features,
    weight,
    bias_term,
    block_values,
    block_rows,
    block_cols,
    counts,
    cluster_order,
    cotangent,
):
    node_count, feature_dim = features.shape
    row_devices = lax.axis_size("row")
    col_devices = lax.axis_size("col")
    tile_values = block_values[0, 0]
    tile_rows = block_rows[0, 0]
    tile_cols = block_cols[0, 0]
    tile_count = counts[0, 0]
    capacity = tile_values.shape[0]
    block_size = tile_values.shape[1]
    stride = min(32, capacity)
    slot_ids = jnp.arange(stride, dtype=jnp.int32)
    hidden = jnp.dot(features, weight, preferred_element_type=jnp.float32).astype(jnp.bfloat16)
    group_rows = lax.all_gather(hidden, "row", axis=0, tiled=True)
    column_nodes = group_rows.shape[0]
    column_blocks = column_nodes // block_size
    row_nodes = node_count * col_devices
    row_blocks = row_nodes // block_size
    permuted_blocks = group_rows[cluster_order].reshape(column_blocks, block_size, feature_dim)

    def slot_group(first_slot):
        values_part = lax.dynamic_slice_in_dim(tile_values, first_slot, stride, 0)
        row_ids = lax.dynamic_slice_in_dim(tile_rows, first_slot, stride, 0)
        col_ids = lax.dynamic_slice_in_dim(tile_cols, first_slot, stride, 0)
        active = first_slot + slot_ids < tile_count
        return (values_part, row_ids, col_ids, active)

    def forward_step(step_index, running):
        values_part, row_ids, col_ids, active = slot_group(step_index * stride)
        gathered = permuted_blocks[col_ids]
        product = jnp.einsum(
            "sij,sjf->sif", values_part, gathered, preferred_element_type=jnp.float32
        )
        product = jnp.where(active[:, None, None], product, 0.0)
        return running.at[row_ids].add(product)

    steps_taken = capacity // stride
    forward_total = lax.fori_loop(
        0, steps_taken, forward_step, jnp.zeros((row_blocks, block_size, feature_dim), jnp.float32)
    )
    terms = forward_total.reshape(row_nodes, feature_dim).astype(jnp.bfloat16)
    summed = lax.psum_scatter(terms, "col", scatter_dimension=0, tiled=True).astype(jnp.float32)
    own_preact = summed + bias_term
    activations = jax.nn.silu(own_preact).astype(jnp.bfloat16)
    slopes = (cotangent.astype(jnp.float32) * silu_slope(own_preact)).astype(jnp.bfloat16)
    slope_group = lax.all_gather(slopes, "col", axis=0, tiled=True)
    slope_blocks = slope_group.reshape(row_blocks, block_size, feature_dim)

    def backward_step(step_index, running):
        values_part, row_ids, col_ids, active = slot_group(step_index * stride)
        gathered = slope_blocks[row_ids]
        product = jnp.einsum(
            "sij,sif->sjf", values_part, gathered, preferred_element_type=jnp.float32
        )
        product = jnp.where(active[:, None, None], product, 0.0)
        return running.at[col_ids].add(product)

    backward_total = lax.fori_loop(
        0,
        steps_taken,
        backward_step,
        jnp.zeros((column_blocks, block_size, feature_dim), jnp.float32),
    )
    cluster_terms = backward_total.reshape(column_nodes, feature_dim)
    node_terms = (
        jnp.zeros_like(cluster_terms).at[cluster_order].set(cluster_terms).astype(jnp.bfloat16)
    )
    grad_sum = lax.psum_scatter(node_terms, "row", scatter_dimension=0, tiled=True).astype(
        jnp.float32
    )
    grad_hidden = grad_sum.astype(jnp.bfloat16)
    grad_features = lax.dot_general(
        grad_hidden, weight, (((1,), (1,)), ((), ())), preferred_element_type=jnp.float32
    ).astype(jnp.bfloat16)
    weight_term = lax.dot_general(
        features, grad_hidden, (((0,), (0,)), ((), ())), preferred_element_type=jnp.float32
    )
    weight_total = lax.psum(weight_term, ("row", "col"))
    all_nodes = node_count * row_devices * col_devices
    grad_weight = weight_total / math.sqrt(all_nodes)
    return (activations, grad_features, grad_weight)


def solution(mesh):
    placed = (
        P(("col", "row"), None),
        P(),
        P(),
        P("row", "col", None, None, None),
        P("row", "col", None),
        P("row", "col", None),
        P("row", "col"),
        P("col"),
        P(("row", "col"), None),
    )
    return jax.shard_map(
        shards,
        mesh=mesh,
        in_specs=placed,
        out_specs=(P(("row", "col"), None), P(("col", "row"), None), P()),
        check_vma=False,
    )
```

profile of v0, /device:TPU:0, one launch (start us, length us, event | category | flops | bytes accessed | tf_op | source)
XLA Modules:
  0.0 252.3 jit_solution(15372613919844931661)
XLA Ops:
  7.2 0.7 compare_select_fusion
  8.0 1.1 convolution_convert_fusion.1
  9.1 10.4 %all_gather.6 = bf16[512,256]{1,0:T(8,128)(2,1)S(1)} all-gather(bf16[128,256]{1,0:T(8,128)(2,1)S(1)} %convolution_convert_fusion.1), channel_id=1, replica_groups=mesh['row'=4,'col'=8] {'row'}, dimensions={0}, use_global_device_ids=true | all-gather | bytes 327680 | tf_op jit(solution)/shard_map/all_gather | solution.py:37
  19.5 0.7 fusion.5
  20.9 2.0 gather_fusion
  22.8 1.6 gather_fusion.1
  24.4 1.7 select_bitcast_fusion.1
  26.2 1.9 copy.16
  28.1 3.5 %scatter_fusion = f32[8,128,256]{2,1,0:T(8,128)S(1)} fusion(f32[8,128,256]{2,1,0:T(8,128)S(1)} %broadcast_in_dim.50, s32[16]{0:T(128)S(1)} %fusion.4, f32[16,128,256]{2,1,0:T(8,128)} %copy.16), kind=kCustom, calls=%fused_computation.3 | custom fusion | flops 524288 | bytes 6291520 | tf_op jit(solution)/shard_map/while/body/eval_jaxpr/scatter-add | solution.py:58
  31.7 0.8 convert_element_type.30
  32.6 31.3 %reduce-scatter.3.cloned.1.call-done = bf16[128,256]{1,0:T(8,128)(2,1)} async-done(((bf16[1024,256]{1,0:T(8,128)(2,1)}), bf16[128,256]{1,0:T(8,128)(2,1)}) %reduce-scatter.3.cloned.1.call-update) | async-done | bytes 65552 | tf_op jit(solution)/shard_map/reduce_scatter | solution.py:65
  64.0 1.5 multiply_convert_fusion
  65.5 15.0 %all_gather.7 = bf16[1024,256]{1,0:T(8,128)(2,1)S(1)} all-gather(bf16[128,256]{1,0:T(8,128)(2,1)S(1)} %get-tuple-element.54), channel_id=1, replica_groups=mesh['row'=4,'col'=8] {'col'}, dimensions={0}, use_global_device_ids=true | all-gather | bytes 589824 | tf_op jit(solution)/shard_map/all_gather | solution.py:69
  81.1 1.9 select_bitcast_fusion
  83.0 1.9 copy.18
  85.0 2.2 scatter_fusion.1
  87.2 2.4 scatter_custom_fusion.2
  89.5 0.7 convert_element_type.36
  90.3 22.4 %reduce-scatter.5.cloned.1.call-done = bf16[128,256]{1,0:T(8,128)(2,1)} async-done(((bf16[512,256]{1,0:T(8,128)(2,1)}), bf16[128,256]{1,0:T(8,128)(2,1)}) %reduce-scatter.5.cloned.1.call-update) | async-done | bytes 65552 | tf_op jit(solution)/shard_map/reduce_scatter | solution.py:91
  112.8 1.8 convolution_bitcast_fusion
  114.6 1.7 convolution_convert_fusion
  116.2 127.7 %all-reduce.2.cloned.1.call-done = f32[256,256]{0,1:T(8,128)} async-done(((f32[256,256]{0,1:T(8,128)}), f32[256,256]{0,1:T(8,128)}) %all-reduce.2.cloned.1.call-update) | async-done | bytes 262160 | tf_op jit(solution)/shard_map/psum | solution.py:101
  244.0 1.0 broadcast_multiply_fusion
  244.9 0.8 copy.19
  (26 shorter events, 1.0 us)
Async XLA Ops:
  7.2 17.3 %copy-start = (bf16[1,1,16,128,128]{4,3,2,1,0:T(8,128)(2,1)S(1)}, bf16[1,1,16,128,128]{4,3,2,1,0:T(8,128)(2,1)}, u32[]{:S(2)}) copy-start(bf16[1,1,16,128,128]{4,3,2,1,0:T(8,128)(2,1)} %param.12) | copy-start | bytes 1572868
  7.2 56.8 %reduce-scatter.3.cloned.1.call-start = ((), (), s32[]{:S(2)}) async-start(), calls=%async_computation.2 | async-start | bytes 589824 | tf_op jit(solution)/shard_map/reduce_scatter | solution.py:65
  26.2 1.9 copy-start.5
  31.7 32.3 %copy-start.3 = (bf16[128,256]{1,0:T(8,128)(2,1)S(1)}, bf16[128,256]{1,0:T(8,128)(2,1)}, u32[]{:S(2)}) copy-start(bf16[128,256]{1,0:T(8,128)(2,1)} %param.17) | copy-start | bytes 196612
  31.7 32.3 %copy-start.4 = (f32[256]{0:T(256)S(1)}, f32[256]{0:T(256)}, u32[]{:S(2)}) copy-start(f32[256]{0:T(256)} %param.11) | copy-start | bytes 3076
  32.6 80.2 %reduce-scatter.5.cloned.1.call-start = ((), (), s32[]{:S(2)}) async-start(), calls=%async_computation.3 | async-start | bytes 327680 | tf_op jit(solution)/shard_map/reduce_scatter | solution.py:91
  84.9 27.8 %copy-start.2 = (bf16[128,256]{1,0:T(8,128)(2,1)S(1)}, bf16[128,256]{1,0:T(8,128)(2,1)}, u32[]{:S(2)}) copy-start(bf16[128,256]{1,0:T(8,128)(2,1)} %param.9) | copy-start | bytes 196612
  87.1 27.4 %copy-start.1 = (bf16[256,256]{1,0:T(8,128)(2,1)S(1)}, bf16[256,256]{1,0:T(8,128)(2,1)}, u32[]{:S(2)}) copy-start(bf16[256,256]{1,0:T(8,128)(2,1)} %param.10) | copy-start | bytes 393220
  90.3 153.7 %all-reduce.2.cloned.1.call-start = ((), (), s32[]{:S(2)}) async-start(), calls=%async_computation.4 | async-start | bytes 524288 | tf_op jit(solution)/shard_map/psum | solution.py:101
Sparse Core Ops, SparseCore 0:
  32.7 31.2 reduce-scatter.2
  90.4 22.3 reduce-scatter.4
  118.9 125.0 all-reduce.1
where the time goes:
time: 253 us; the launch traced here: 252 us
  waiting for transfers between devices  182 us (72%)
  blocking collectives  25.5 us (10%)
  between operations  14.6 us (6%)
  local copies, waits for them, and re-layouts  11.3 us (4%)
  other arithmetic  11.2 us (4%)
  matrix products  8.11 us (3%)
    psum x1, waiting for transfers between devices, shards(): weight_total = lax.psum(weight_term, ('row', 'col'))  128 us
    reduce_scatter x1, waiting for transfers between devices, shards(): lax.psum_scatter(terms, 'col', scatter_dimension=0, tiled=True)  31.3 us
    reduce_scatter x1, waiting for transfers between devices, shards(): lax.psum_scatter(node_terms, 'row', scatter_dimension=0, tiled=True)  22.4 us
    all_gather x1, blocking collectives, shards(): slope_group = lax.all_gather(slopes, 'col', axis=0, tiled=True)  15 us
    all_gather x1, blocking collectives, shards(): group_rows = lax.all_gather(hidden, 'row', axis=0, tiled=True)  10.4 us
  transfers between devices with their start and end apart: 3, of which 3 were waited for; matrix products, arithmetic and copies ran while one was open for 1% of the time, Pallas kernels for 0%

commit v1 on v0

v1 whole, which is shorter than its diff:
```python
import functools
import math

import jax
import jax.numpy as jnp
from jax import lax
from jax.experimental import pallas as pl
from jax.experimental.pallas import tpu as pltpu
from jax.sharding import PartitionSpec as P

F32 = jnp.float32
BF16 = jnp.bfloat16
VMEM_LIMIT = 48 * 1024 * 1024


def params():
    return pltpu.CompilerParams(vmem_limit_bytes=VMEM_LIMIT)


def cost(flops, nbytes, transcendentals=0):
    return pl.CostEstimate(flops=flops, bytes_accessed=nbytes, transcendentals=transcendentals)


def whole(shape):
    return pl.BlockSpec(shape, lambda *_: (0,) * len(shape))


def swap(value, axis, mask):
    size = lax.axis_size(axis)
    return lax.ppermute(value, axis, [(i, i ^ mask) for i in range(size)])


def tiled_dot(shape, store, lhs_rows, rhs_rows):
    rows, cols = shape
    row_step, col_step = min(rows, 512), min(cols, 512)

    def tile(i, j):
        left = lhs_rows(pl.multiple_of(i * row_step, row_step), row_step)
        right = rhs_rows(pl.multiple_of(j * col_step, col_step), col_step)
        return lax.dot_general(left, right, NT, preferred_element_type=F32)

    def step(t, carry):
        i, j = t // (cols // col_step), t % (cols // col_step)
        value = tile(i, j)
        rows_at = pl.ds(pl.multiple_of(i * row_step, row_step), row_step)
        store(rows_at, pl.ds(pl.multiple_of(j * col_step, col_step), col_step), value)
        return carry

    steps = (rows // row_step) * (cols // col_step)
    if steps <= 4:
        for t in range(steps):
            step(t, 0)
    else:
        lax.fori_loop(0, steps, step, 0)


NT = (((1,), (1,)), ((), ()))


def prep_kernel(per_step, rows_ref, cols_ref, count_ref, order_ref, values_ref, a_ref, at_ref, dense, select):
    block = values_ref.shape[1]
    nodes = select.shape[0]
    first = pl.program_id(0) * per_step
    row_blocks = pl.num_programs(0) * per_step
    row, col = lax.axis_index("row"), lax.axis_index("col")

    dense[...] = jnp.zeros_like(dense)
    local = lax.broadcasted_iota(jnp.int32, (block, block), 0)
    for chunk in range(nodes // block):
        node = (row ^ chunk) * block + local
        for part in range(nodes // block):
            hit = order_ref[part : part + 1, :] == node
            select[chunk * block : (chunk + 1) * block, part * block : (part + 1) * block] = jnp.where(
                hit, 1.0, 0.0
            ).astype(BF16)

    def slot(s, carry):
        turned = rows_ref[s] ^ col
        place = (turned & 1) * (row_blocks // 2) + (turned >> 1) - first

        @pl.when((place >= 0) & (place < per_step))
        def _():
            dense[
                pl.ds(pl.multiple_of(place * block, block), block),
                pl.ds(pl.multiple_of(cols_ref[s] * block, block), block),
            ] = values_ref[s]

        return carry

    lax.fori_loop(0, count_ref[0], slot, 0)

    def store_a(i, j, value):
        a_ref[i, j] = value.astype(BF16)

    def store_at(i, j, value):
        at_ref[i, j] = value.astype(BF16)

    dense_rows = lambda i, n: dense[pl.ds(i, n), :]
    select_rows = lambda i, n: select[pl.ds(i, n), :]
    tiled_dot((per_step * block, nodes), store_a, dense_rows, select_rows)
    tiled_dot((nodes, per_step * block), store_at, select_rows, dense_rows)


def prep(values, rows, cols, count, order, row_blocks):
    capacity, block, _ = values.shape
    nodes = order.shape[0]
    per_step = min(row_blocks, 8)
    smem = pl.BlockSpec(memory_space=pltpu.SMEM)
    return pl.pallas_call(
        functools.partial(prep_kernel, per_step),
        grid=(row_blocks // per_step,),
        out_shape=(
            jax.ShapeDtypeStruct((row_blocks * block, nodes), BF16),
            jax.ShapeDtypeStruct((nodes, row_blocks * block), BF16),
        ),
        in_specs=[smem, smem, smem, whole((nodes // block, block)), whole(values.shape)],
        out_specs=(
            pl.BlockSpec((per_step * block, nodes), lambda i: (i, 0)),
            pl.BlockSpec((nodes, per_step * block), lambda i: (0, i)),
        ),
        scratch_shapes=[
            pltpu.VMEM((per_step * block, nodes), BF16),
            pltpu.VMEM((nodes, nodes), BF16),
        ],
        compiler_params=params(),
        cost_estimate=cost(4 * row_blocks * block * nodes * nodes, 2 * values.size),
        name="prep",
    )(rows, cols, count, order.reshape(nodes // block, block), values)


def product_kernel(pieces, *refs):
    matrix, parts, outs, joined = refs[0], refs[1 : 1 + pieces], refs[1 + pieces : -1], refs[-1]
    run = parts[0].shape[0]

    @pl.when(pl.program_id(0) == 0)
    def _():
        for i, part in enumerate(parts):
            joined[i * run : (i + 1) * run, :] = part[...]

    total = lax.dot_general(matrix[...], joined[...], (((1,), (0,)), ((), ())), preferred_element_type=F32)
    start = 0
    for out in outs:
        out[...] = total[start : start + out.shape[0]].astype(out.dtype)
        start += out.shape[0]


def product(matrix, parts, sizes, name):
    rows, depth = matrix.shape
    width = parts[0].shape[1]
    step = min(rows, 1024)
    if step == rows:
        out_shape = [jax.ShapeDtypeStruct((n, width), BF16) for n in sizes]
        out_specs = [whole((n, width)) for n in sizes]
    else:
        out_shape = [jax.ShapeDtypeStruct((rows, width), BF16)]
        out_specs = [pl.BlockSpec((step, width), lambda i: (i, 0))]
    outs = pl.pallas_call(
        functools.partial(product_kernel, len(parts)),
        grid=(rows // step,),
        out_shape=out_shape,
        in_specs=[pl.BlockSpec((step, depth), lambda i: (i, 0))] + [whole(p.shape) for p in parts],
        out_specs=out_specs,
        scratch_shapes=[pltpu.VMEM((depth, width), BF16)],
        compiler_params=params(),
        cost_estimate=cost(2 * rows * depth * width, 2 * (rows * depth + depth * width + rows * width)),
        name=name,
    )(matrix, *parts)
    if step == rows:
        return list(outs)
    cuts, start = [], 0
    for n in sizes:
        cuts.append(outs[0][start : start + n])
        start += n
    return cuts


def pointwise_kernel(terms, *refs):
    weight, bias, cotangent = refs[terms : terms + 3]
    activations, slopes, kept, sent, whole_term = refs[terms + 3 :]
    mixed = refs[0][...].astype(F32)
    for ref in refs[1:terms]:
        mixed = mixed + ref[...].astype(F32)
    high = mixed.astype(BF16)
    low = (mixed - high.astype(F32)).astype(BF16)
    preact = (
        jnp.dot(high, weight[...], preferred_element_type=F32)
        + jnp.dot(low, weight[...], preferred_element_type=F32)
        + bias[...]
    )
    gate = 1.0 / (1.0 + jnp.exp(-preact))
    activations[...] = (preact * gate).astype(BF16)
    slope = (cotangent[...].astype(F32) * (gate * (1.0 + preact * (1.0 - gate)))).astype(BF16)
    slopes[...] = slope
    whole_term[...] = lax.dot_general(high, slope, (((0,), (0,)), ((), ())), preferred_element_type=F32)
    half = kept.shape[0]
    core = lax.axis_index("col") & 1
    kept[...] = whole_term[pl.ds(pl.multiple_of(core * half, half), half), :].astype(kept.dtype)
    sent[...] = whole_term[pl.ds(pl.multiple_of((1 - core) * half, half), half), :].astype(sent.dtype)


def pointwise(terms, weight, bias, cotangent):
    nodes, width = cotangent.shape
    depth = weight.shape[0]
    node_out = jax.ShapeDtypeStruct((nodes, width), BF16)
    half_out = jax.ShapeDtypeStruct((depth // 2, width), BF16)
    return pl.pallas_call(
        functools.partial(pointwise_kernel, len(terms)),
        out_shape=(node_out, node_out, half_out, half_out),
        scratch_shapes=[pltpu.VMEM((depth, width), F32)],
        compiler_params=params(),
        cost_estimate=cost(6 * nodes * depth * width, 2 * nodes * width * (len(terms) + 5), nodes * width),
        name="pointwise",
    )(*terms, weight, bias.reshape(1, width), cotangent)


def feature_kernel(terms, *refs):
    total = refs[0][...].astype(F32)
    for ref in refs[1:terms]:
        total = total + ref[...].astype(F32)
    weight, out = refs[terms:]
    out[...] = lax.dot_general(total.astype(BF16), weight[...], NT, preferred_element_type=F32).astype(BF16)


def feature_gradient(terms, weight):
    nodes, width = terms[0].shape
    depth = weight.shape[0]
    return pl.pallas_call(
        functools.partial(feature_kernel, len(terms)),
        out_shape=jax.ShapeDtypeStruct((nodes, depth), BF16),
        compiler_params=params(),
        cost_estimate=cost(2 * nodes * depth * width, 2 * nodes * width * (len(terms) + 2)),
        name="feature_gradient",
    )(*terms, weight)


def add(left, right):
    return (left.astype(F32) + right.astype(F32)).astype(BF16)


def shards(
    features,
    weight,
    bias_term,
    block_values,
    block_rows,
    block_cols,
    counts,
    cluster_order,
    cotangent,
):
    node_count, width = features.shape
    row_devices = lax.axis_size("row")
    col_devices = lax.axis_size("col")
    levels = col_devices // 2
    values = block_values[0, 0]
    block = values.shape[1]
    row_blocks = node_count * col_devices // block

    with jax.named_scope("gather_features"):
        pieces = [features] + [swap(features, "row", m) for m in range(1, row_devices)]
    tile, tile_turned = prep(
        values, block_rows[0, 0], block_cols[0, 0], counts[0], cluster_order, row_blocks
    )

    with jax.named_scope("forward"):
        own = [node_count] * levels
        *kept, other = product(tile, pieces, own + [node_count * levels], "forward_tile")
        arrived = swap(other, "col", 1)
        pairs = [add(k, arrived[i * node_count : (i + 1) * node_count]) for i, k in enumerate(kept)]
        terms = [pairs[0]] + [swap(pairs[m], "col", 2 * m) for m in range(1, levels)]
        activations, slopes, weight_kept, weight_sent = pointwise(terms, weight, bias_term, cotangent)

    with jax.named_scope("gather_slopes"):
        slope_own = [slopes] + [swap(slopes, "col", 2 * m) for m in range(1, levels)]
    with jax.named_scope("weight_rows"):
        term = add(weight_kept, swap(weight_sent, "col", 1))
        mask = 1
        while mask < row_devices:
            term = add(term, swap(term, "row", mask))
            mask *= 2

    with jax.named_scope("backward"):
        slope_half = jnp.concatenate(slope_own)
        slope_other = swap(slope_half, "col", 1)
        node_terms = product(tile_turned, [slope_half, slope_other], [node_count] * row_devices, "backward_tile")
        node_sum = [node_terms[0]] + [swap(node_terms[m], "row", m) for m in range(1, row_devices)]
        grad_features = feature_gradient(node_sum, weight)

    with jax.named_scope("weight_levels"):
        mask = 2
        while mask < col_devices:
            term = add(term, swap(term, "col", mask))
            mask *= 2
        partner = swap(term, "col", 1)
        core = lax.axis_index("col") & 1
        scale = 1.0 / math.sqrt(node_count * row_devices * col_devices)
        both = jnp.where(
            core == 0, jnp.concatenate([term, partner]), jnp.concatenate([partner, term])
        )
        grad_weight = both.astype(F32) * scale
    return (activations, grad_features, grad_weight)


def solution(mesh):
    placed = (
        P(("col", "row"), None),
        P(),
        P(),
        P("row", "col", None, None, None),
        P("row", "col", None),
        P("row", "col", None),
        P("row", "col"),
        P("col"),
        P(("row", "col"), None),
    )
    return jax.shard_map(
        shards,
        mesh=mesh,
        in_specs=placed,
        out_specs=(P(("row", "col"), None), P(("col", "row"), None), P()),
        check_vma=False,
    )
```

time: 253 us -> 57 us (0.23)
  waiting for transfers between devices: 182 us -> 26.1 us
  blocking collectives: 25.5 us -> 0 us
  starting transfers between devices: 0.12 us -> 21.1 us
  between operations: 14.6 us -> 1.46 us
  other arithmetic: 11.2 us -> 0.89 us
  local copies, waits for them, and re-layouts: 11.3 us -> 2.41 us
  matrix products: 8.11 us -> 0 us
  Pallas kernels: 0 us -> 4.94 us
    psum x1 -> x0, waiting for transfers between devices: 128 us -> none  [shards(): weight_total = lax.psum(weight_term, ('row', 'col'))]
    reduce_scatter x2 -> x0, waiting for transfers between devices: 53.8 us -> none  [the longest x1 31.3 us: shards(): lax.psum_scatter(terms, 'col', scatter_dimension=0, tiled=True)]
    ppermute x0 -> x20, waiting for transfers between devices: none -> 26.1 us  [swap(): return lax.ppermute(value, axis, [(i, i ^ mask) for i in range(size)])]
    all_gather x2 -> x0, blocking collectives: 25.5 us -> none  [the longest x1 15 us: shards(): slope_group = lax.all_gather(slopes, 'col', axis=0, tiled=True)]
    ppermute x0 -> x20, starting transfers between devices: none -> 21.1 us  [swap(): return lax.ppermute(value, axis, [(i, i ^ mask) for i in range(size)])]
    dot_general x5 -> x0, matrix products: 8.11 us -> none  [the longest x1 1.86 us: backward_step(): jnp.einsum('sij,sif->sjf', values_part, gathered, preferred_element_type=...]
    scatter-add x2 -> x0, other arithmetic: 5.69 us -> none  [the longest x1 3.51 us: forward_step(): return running.at[row_ids].add(product)]
    pallas_call x0 -> x5, Pallas kernels: none -> 4.94 us  [the longest x1 2.35 us: prep(): pl.pallas_call(functools.partial(prep_kernel, per_step), grid=(row_blocks...]
  transfers between devices with their start and end apart: 3 -> 20, of which waited for: 3 -> 11; matrix products, arithmetic and copies ran while one was open for 1% -> 1% of each run, Pallas kernels for 0% -> 5%
where the time goes in v1:
time: 57 us; the launch traced here: 56.9 us
  waiting for transfers between devices  26.1 us (46%)
  starting transfers between devices  21.1 us (37%)
  Pallas kernels  4.94 us (9%)
  local copies, waits for them, and re-layouts  2.41 us (4%)
  between operations  1.46 us (3%)
  other arithmetic  0.89 us (2%)
    ppermute x20, waiting for transfers between devices, swap(): return lax.ppermute(value, axis, [(i, i ^ mask) for i in range(size)])  26.1 us
    ppermute x20, starting transfers between devices, swap(): return lax.ppermute(value, axis, [(i, i ^ mask) for i in range(size)])  21.1 us
    unnamed x19, local copies, waits for them, and re-layouts  2.41 us
    pallas_call x1, Pallas kernels, prep(): pl.pallas_call(functools.partial(prep_kernel, per_step), grid=(row_blocks...  2.35 us
  transfers between devices with their start and end apart: 20, of which 11 were waited for; matrix products, arithmetic and copies ran while one was open for 1% of the time, Pallas kernels for 5%

profile of v1, /device:TPU:0, one launch (start us, length us, event | category | flops | bytes accessed | tf_op | source)
XLA Modules:
  0.0 56.9 jit_solution(7603168504635371996)
XLA Ops:
  0.6 3.0 %collective-permute-start = (bf16[128,256]{1,0:T(8,128)(2,1)}, bf16[128,256]{1,0:T(8,128)(2,1)S(1)}, u32[]{:S(2)}, u32[]{:S(2)}) collective-permute-start(bf16[128,256]{1,0:T(8,128)(2,1)} %refs_1_.1), channel_id=1, source_target_pairs={{0,8},{8,0},{16,24},{24,16},{1,9},{9,1},{17,25},{25,17},{2,10},{10... | collective-permute-start | bytes 196616 | tf_op jit(solution)/shard_map/gather_features/ppermute | solution.py:30
  3.6 1.5 %collective-permute-start.1 = (bf16[128,256]{1,0:T(8,128)(2,1)}, bf16[128,256]{1,0:T(8,128)(2,1)S(1)}, u32[]{:S(2)}, u32[]{:S(2)}) collective-permute-start(bf16[128,256]{1,0:T(8,128)(2,1)} %refs_1_.1), channel_id=1, source_target_pairs={{0,16},{8,24},{16,0},{24,8},{1,17},{9,25},{17,1},{25,9},{2,18},{10... | collective-permute-start | bytes 196616 | tf_op jit(solution)/shard_map/gather_features/ppermute | solution.py:30
  6.5 1.0 %copy-done.4 = bf16[1,1,16,128,128]{4,3,2,1,0:T(8,128)(2,1)S(1)} copy-done((bf16[1,1,16,128,128]{4,3,2,1,0:T(8,128)(2,1)S(1)}, bf16[1,1,16,128,128]{4,3,2,1,0:T(8,128)(2,1)}, u32[]{:S(2)}) %copy-start.4) | copy-done | bytes 524312
  7.6 2.4 %prep.1 = (bf16[1024,512]{1,0:T(8,128)(2,1)S(1)}, bf16[512,1024]{1,0:T(8,128)(2,1)S(1)}) custom-call(s32[16]{0:T(128)S(1)} %bitcast.10, s32[16]{0:T(128)S(1)} %bitcast.11, s32[1]{0:T(128)} %bitcast.6.count_ref, s32[4,128]{1,0:T(4,128)S(1)} %bitcast.9, bf16[16,128,128]{2,1,0:T(8,128)(2,1)S(1)} %bitcast.8), custom_call_target="tpu_custom_call" | custom-call | flops 1073741824 | bytes 524288 | tf_op jit(solution)/shard_map/prep/pallas_call | solution.py:109
  11.1 1.5 %collective-permute-done.3 = bf16[512,256]{1,0:T(8,128)(2,1)S(1)} collective-permute-done((bf16[512,256]{1,0:T(8,128)(2,1)S(1)}, bf16[512,256]{1,0:T(8,128)(2,1)S(1)}, u32[]{:S(2)}, u32[]{:S(2)}) %collective-permute-start.3) | collective-permute-done | bytes 262176 | tf_op jit(solution)/shard_map/forward/ppermute | solution.py:30
  12.6 1.6 %collective-permute-start.4 = (bf16[128,256]{1,0:T(8,128)(2,1)S(1)}, bf16[128,256]{1,0:T(8,128)(2,1)S(1)}, u32[]{:S(2)}, u32[]{:S(2)}) collective-permute-start(bf16[128,256]{1,0:T(8,128)(2,1)S(1)} %get-tuple-element.35), channel_id=1, source_target_pairs={{0,2},{1,3},{2,0},{3,1},{4,6},{5,7},{6,4},{7,5},{8,10},{9,11},{10,... | collective-permute-start | bytes 196616 | tf_op jit(solution)/shard_map/forward/ppermute | solution.py:30
  14.3 2.6 %collective-permute-start.5 = (bf16[128,256]{1,0:T(8,128)(2,1)S(1)}, bf16[128,256]{1,0:T(8,128)(2,1)S(1)}, u32[]{:S(2)}, u32[]{:S(2)}) collective-permute-start(bf16[128,256]{1,0:T(8,128)(2,1)S(1)} %get-tuple-element.34), channel_id=1, source_target_pairs={{0,4},{1,5},{2,6},{3,7},{4,0},{5,1},{6,2},{7,3},{8,12},{9,13},{10,... | collective-permute-start | bytes 196616 | tf_op jit(solution)/shard_map/forward/ppermute | solution.py:30
  17.1 4.7 %collective-permute-done.5.refs_2_ = bf16[128,256]{1,0:T(8,128)(2,1)S(1)} collective-permute-done((bf16[128,256]{1,0:T(8,128)(2,1)S(1)}, bf16[128,256]{1,0:T(8,128)(2,1)S(1)}, u32[]{:S(2)}, u32[]{:S(2)}) %collective-permute-start.5) | collective-permute-done | bytes 65568 | tf_op jit(solution)/shard_map/forward/ppermute | solution.py:30
  21.8 1.2 %collective-permute-done.6.refs_3_ = bf16[128,256]{1,0:T(8,128)(2,1)S(1)} collective-permute-done((bf16[128,256]{1,0:T(8,128)(2,1)S(1)}, bf16[128,256]{1,0:T(8,128)(2,1)S(1)}, u32[]{:S(2)}, u32[]{:S(2)}) %collective-permute-start.6) | collective-permute-done | bytes 65568 | tf_op jit(solution)/shard_map/forward/ppermute | solution.py:30
  23.7 0.9 %pointwise.1 = (bf16[128,256]{1,0:T(8,128)(2,1)}, bf16[128,256]{1,0:T(8,128)(2,1)S(1)}, bf16[128,256]{1,0:T(8,128)(2,1)S(1)}, bf16[128,256]{1,0:T(8,128)(2,1)S(1)}) custom-call(bf16[128,256]{1,0:T(8,128)(2,1)S(1)} %get-tuple-element.36.refs_0_, bf16[128,256]{1,0:T(8,128)(2,1)S(1)} %collective-permute-done.4.refs_1_, ...), custom_call_target="tpu_custom_call" | custom-call | flops 50331648 | bytes 589824 | tf_op jit(solution)/shard_map/forward/pointwise/pallas_call | solution.py:206
  24.6 0.8 %collective-permute-start.7 = (bf16[128,256]{1,0:T(8,128)(2,1)S(1)}, bf16[128,256]{1,0:T(8,128)(2,1)S(1)}, u32[]{:S(2)}, u32[]{:S(2)}) collective-permute-start(bf16[128,256]{1,0:T(8,128)(2,1)S(1)} %get-tuple-element.26), channel_id=1, source_target_pairs={{0,2},{1,3},{2,0},{3,1},{4,6},{5,7},{6,4},{7,5},{8,10},{9,11},{10,... | collective-permute-start | bytes 196616 | tf_op jit(solution)/shard_map/gather_slopes/ppermute | solution.py:30
  25.5 1.7 %collective-permute-start.8 = (bf16[128,256]{1,0:T(8,128)(2,1)S(1)}, bf16[128,256]{1,0:T(8,128)(2,1)S(1)}, u32[]{:S(2)}, u32[]{:S(2)}) collective-permute-start(bf16[128,256]{1,0:T(8,128)(2,1)S(1)} %get-tuple-element.26), channel_id=1, source_target_pairs={{0,4},{1,5},{2,6},{3,7},{4,0},{5,1},{6,2},{7,3},{8,12},{9,13},{10,... | collective-permute-start | bytes 196616 | tf_op jit(solution)/shard_map/gather_slopes/ppermute | solution.py:30
  27.2 1.8 %collective-permute-start.9 = (bf16[128,256]{1,0:T(8,128)(2,1)S(1)}, bf16[128,256]{1,0:T(8,128)(2,1)S(1)}, u32[]{:S(2)}, u32[]{:S(2)}) collective-permute-start(bf16[128,256]{1,0:T(8,128)(2,1)S(1)} %get-tuple-element.26), channel_id=1, source_target_pairs={{0,6},{1,7},{2,4},{3,5},{4,2},{5,3},{6,0},{7,1},{8,14},{9,15},{10,... | collective-permute-start | bytes 196616 | tf_op jit(solution)/shard_map/gather_slopes/ppermute | solution.py:30
  29.0 1.1 %collective-permute-start.15 = (bf16[128,256]{1,0:T(8,128)(2,1)S(1)}, bf16[128,256]{1,0:T(8,128)(2,1)S(1)}, u32[]{:S(2)}, u32[]{:S(2)}) collective-permute-start(bf16[128,256]{1,0:T(8,128)(2,1)S(1)} %add_convert_fusion.4), channel_id=1, source_target_pairs={{0,8},{8,0},{16,24},{24,16},{1,9},{9,1},{17,25},{25,17},{2,10},{10... | collective-permute-start | bytes 196616 | tf_op jit(solution)/shard_map/weight_rows/ppermute | solution.py:30
  30.2 3.2 %collective-permute-done.15 = bf16[128,256]{1,0:T(8,128)(2,1)S(1)} collective-permute-done((bf16[128,256]{1,0:T(8,128)(2,1)S(1)}, bf16[128,256]{1,0:T(8,128)(2,1)S(1)}, u32[]{:S(2)}, u32[]{:S(2)}) %collective-permute-start.15) | collective-permute-done | bytes 65568 | tf_op jit(solution)/shard_map/weight_rows/ppermute | solution.py:30
  33.4 1.3 %collective-permute-start.16 = (bf16[128,256]{1,0:T(8,128)(2,1)S(1)}, bf16[128,256]{1,0:T(8,128)(2,1)S(1)}, u32[]{:S(2)}, u32[]{:S(2)}) collective-permute-start(bf16[128,256]{1,0:T(8,128)(2,1)S(1)} %add_convert_fusion.3), channel_id=1, source_target_pairs={{0,16},{8,24},{16,0},{24,8},{1,17},{9,25},{17,1},{25,9},{2,18},{10... | collective-permute-start | bytes 196616 | tf_op jit(solution)/shard_map/weight_rows/ppermute | solution.py:30
  34.7 3.0 %collective-permute-done.16 = bf16[128,256]{1,0:T(8,128)(2,1)S(1)} collective-permute-done((bf16[128,256]{1,0:T(8,128)(2,1)S(1)}, bf16[128,256]{1,0:T(8,128)(2,1)S(1)}, u32[]{:S(2)}, u32[]{:S(2)}) %collective-permute-start.16) | collective-permute-done | bytes 65568 | tf_op jit(solution)/shard_map/weight_rows/ppermute | solution.py:30
  37.8 4.2 %collective-permute-done.17 = bf16[128,256]{1,0:T(8,128)(2,1)S(1)} collective-permute-done((bf16[128,256]{1,0:T(8,128)(2,1)S(1)}, bf16[128,256]{1,0:T(8,128)(2,1)S(1)}, u32[]{:S(2)}, u32[]{:S(2)}) %collective-permute-start.17) | collective-permute-done | bytes 65568 | tf_op jit(solution)/shard_map/weight_levels/ppermute | solution.py:30
  42.1 1.5 %collective-permute-start.18 = (bf16[128,256]{1,0:T(8,128)(2,1)S(1)}, bf16[128,256]{1,0:T(8,128)(2,1)S(1)}, u32[]{:S(2)}, u32[]{:S(2)}) collective-permute-start(bf16[128,256]{1,0:T(8,128)(2,1)S(1)} %add_convert_fusion.1), channel_id=1, source_target_pairs={{0,4},{1,5},{2,6},{3,7},{4,0},{5,1},{6,2},{7,3},{8,12},{9,13},{10,... | collective-permute-start | bytes 196616 | tf_op jit(solution)/shard_map/weight_levels/ppermute | solution.py:30
  43.6 3.8 %collective-permute-done.18 = bf16[128,256]{1,0:T(8,128)(2,1)S(1)} collective-permute-done((bf16[128,256]{1,0:T(8,128)(2,1)S(1)}, bf16[128,256]{1,0:T(8,128)(2,1)S(1)}, u32[]{:S(2)}, u32[]{:S(2)}) %collective-permute-start.18) | collective-permute-done | bytes 65568 | tf_op jit(solution)/shard_map/weight_levels/ppermute | solution.py:30
  48.0 1.1 %collective-permute-start.11 = (bf16[128,256]{1,0:T(8,128)(2,1)S(1)}, bf16[128,256]{1,0:T(8,128)(2,1)S(1)}, u32[]{:S(2)}, u32[]{:S(2)}) collective-permute-start(bf16[128,256]{1,0:T(8,128)(2,1)S(1)} %get-tuple-element.28), channel_id=1, source_target_pairs={{0,8},{8,0},{16,24},{24,16},{1,9},{9,1},{17,25},{25,17},{2,10},{10... | collective-permute-start | bytes 196616 | tf_op jit(solution)/shard_map/backward/ppermute | solution.py:30
  49.1 1.7 %collective-permute-start.12 = (bf16[128,256]{1,0:T(8,128)(2,1)S(1)}, bf16[128,256]{1,0:T(8,128)(2,1)S(1)}, u32[]{:S(2)}, u32[]{:S(2)}) collective-permute-start(bf16[128,256]{1,0:T(8,128)(2,1)S(1)} %get-tuple-element.29), channel_id=1, source_target_pairs={{0,16},{8,24},{16,0},{24,8},{1,17},{9,25},{17,1},{25,9},{2,18},{10... | collective-permute-start | bytes 196616 | tf_op jit(solution)/shard_map/backward/ppermute | solution.py:30
  52.6 1.2 %collective-permute-done.12.refs_2_ = bf16[128,256]{1,0:T(8,128)(2,1)S(1)} collective-permute-done((bf16[128,256]{1,0:T(8,128)(2,1)S(1)}, bf16[128,256]{1,0:T(8,128)(2,1)S(1)}, u32[]{:S(2)}, u32[]{:S(2)}) %collective-permute-start.12) | collective-permute-done | bytes 65568 | tf_op jit(solution)/shard_map/backward/ppermute | solution.py:30
  53.7 2.3 %collective-permute-done.13.refs_3_ = bf16[128,256]{1,0:T(8,128)(2,1)S(1)} collective-permute-done((bf16[128,256]{1,0:T(8,128)(2,1)S(1)}, bf16[128,256]{1,0:T(8,128)(2,1)S(1)}, u32[]{:S(2)}, u32[]{:S(2)}) %collective-permute-start.13) | collective-permute-done | bytes 65568 | tf_op jit(solution)/shard_map/backward/ppermute | solution.py:30
  (48 shorter events, 6.1 us)
Async XLA Ops:
  0.6 9.3 %collective-permute-start = (bf16[128,256]{1,0:T(8,128)(2,1)}, bf16[128,256]{1,0:T(8,128)(2,1)S(1)}, u32[]{:S(2)}, u32[]{:S(2)}) collective-permute-start(bf16[128,256]{1,0:T(8,128)(2,1)} %refs_1_.1), channel_id=1, source_target_pairs={{0,8},{8,0},{16,24},{24,16},{1,9},{9,1},{17,25},{25,17},{2,10},{10... | collective-permute-start | bytes 196616 | tf_op jit(solution)/shard_map/gather_features/ppermute | solution.py:30
  3.6 6.3 %collective-permute-start.1 = (bf16[128,256]{1,0:T(8,128)(2,1)}, bf16[128,256]{1,0:T(8,128)(2,1)S(1)}, u32[]{:S(2)}, u32[]{:S(2)}) collective-permute-start(bf16[128,256]{1,0:T(8,128)(2,1)} %refs_1_.1), channel_id=1, source_target_pairs={{0,16},{8,24},{16,0},{24,8},{1,17},{9,25},{17,1},{25,9},{2,18},{10... | collective-permute-start | bytes 196616 | tf_op jit(solution)/shard_map/gather_features/ppermute | solution.py:30
  5.2 5.4 %collective-permute-start.2 = (bf16[128,256]{1,0:T(8,128)(2,1)}, bf16[128,256]{1,0:T(8,128)(2,1)S(1)}, u32[]{:S(2)}, u32[]{:S(2)}) collective-permute-start(bf16[128,256]{1,0:T(8,128)(2,1)} %refs_1_.1), channel_id=1, source_target_pairs={{0,24},{8,16},{16,8},{24,0},{1,25},{9,17},{17,9},{25,1},{2,26},{10... | collective-permute-start | bytes 196616 | tf_op jit(solution)/shard_map/gather_features/ppermute | solution.py:30
  6.5 1.0 %copy-start.4 = (bf16[1,1,16,128,128]{4,3,2,1,0:T(8,128)(2,1)S(1)}, bf16[1,1,16,128,128]{4,3,2,1,0:T(8,128)(2,1)}, u32[]{:S(2)}) copy-start(bf16[1,1,16,128,128]{4,3,2,1,0:T(8,128)(2,1)} %param.12) | copy-start | bytes 1572868
  7.6 3.0 %copy-start.1 = (bf16[128,256]{1,0:T(8,128)(2,1)S(1)}, bf16[128,256]{1,0:T(8,128)(2,1)}, u32[]{:S(2)}) copy-start(bf16[128,256]{1,0:T(8,128)(2,1)} %refs_1_.1) | copy-start | bytes 196612
  11.0 1.6 %collective-permute-start.3 = (bf16[512,256]{1,0:T(8,128)(2,1)S(1)}, bf16[512,256]{1,0:T(8,128)(2,1)S(1)}, u32[]{:S(2)}, u32[]{:S(2)}) collective-permute-start(bf16[512,256]{1,0:T(8,128)(2,1)S(1)} %get-tuple-element.20), channel_id=1, source_target_pairs={{0,1},{1,0},{2,3},{3,2},{4,5},{5,4},{6,7},{7,6},{8,9},{9,8},{10,11... | collective-permute-start | bytes 786440 | tf_op jit(solution)/shard_map/forward/ppermute | solution.py:30
  12.6 10.5 %copy-start = (bf16[256,256]{1,0:T(8,128)(2,1)S(1)}, bf16[256,256]{1,0:T(8,128)(2,1)}, u32[]{:S(2)}) copy-start(bf16[256,256]{1,0:T(8,128)(2,1)} %refs_4_.3) | copy-start | bytes 393220
  12.6 10.5 %copy-start.2 = (bf16[128,256]{1,0:T(8,128)(2,1)S(1)}, bf16[128,256]{1,0:T(8,128)(2,1)}, u32[]{:S(2)}) copy-start(bf16[128,256]{1,0:T(8,128)(2,1)} %refs_6_.1) | copy-start | bytes 196612
  12.6 4.5 %collective-permute-start.4 = (bf16[128,256]{1,0:T(8,128)(2,1)S(1)}, bf16[128,256]{1,0:T(8,128)(2,1)S(1)}, u32[]{:S(2)}, u32[]{:S(2)}) collective-permute-start(bf16[128,256]{1,0:T(8,128)(2,1)S(1)} %get-tuple-element.35), channel_id=1, source_target_pairs={{0,2},{1,3},{2,0},{3,1},{4,6},{5,7},{6,4},{7,5},{8,10},{9,11},{10,... | collective-permute-start | bytes 196616 | tf_op jit(solution)/shard_map/forward/ppermute | solution.py:30
  14.3 7.5 %collective-permute-start.5 = (bf16[128,256]{1,0:T(8,128)(2,1)S(1)}, bf16[128,256]{1,0:T(8,128)(2,1)S(1)}, u32[]{:S(2)}, u32[]{:S(2)}) collective-permute-start(bf16[128,256]{1,0:T(8,128)(2,1)S(1)} %get-tuple-element.34), channel_id=1, source_target_pairs={{0,4},{1,5},{2,6},{3,7},{4,0},{5,1},{6,2},{7,3},{8,12},{9,13},{10,... | collective-permute-start | bytes 196616 | tf_op jit(solution)/shard_map/forward/ppermute | solution.py:30
  16.9 6.2 %collective-permute-start.6 = (bf16[128,256]{1,0:T(8,128)(2,1)S(1)}, bf16[128,256]{1,0:T(8,128)(2,1)S(1)}, u32[]{:S(2)}, u32[]{:S(2)}) collective-permute-start(bf16[128,256]{1,0:T(8,128)(2,1)S(1)} %get-tuple-element.33), channel_id=1, source_target_pairs={{0,6},{1,7},{2,4},{3,5},{4,2},{5,3},{6,0},{7,1},{8,14},{9,15},{10,... | collective-permute-start | bytes 196616 | tf_op jit(solution)/shard_map/forward/ppermute | solution.py:30
  24.6 4.4 %collective-permute-start.14 = (bf16[128,256]{1,0:T(8,128)(2,1)S(1)}, bf16[128,256]{1,0:T(8,128)(2,1)S(1)}, u32[]{:S(2)}, u32[]{:S(2)}) collective-permute-start(bf16[128,256]{1,0:T(8,128)(2,1)S(1)} %get-tuple-element.32), channel_id=1, source_target_pairs={{0,1},{1,0},{2,3},{3,2},{4,5},{5,4},{6,7},{7,6},{8,9},{9,8},{10,11... | collective-permute-start | bytes 196616 | tf_op jit(solution)/shard_map/weight_rows/ppermute | solution.py:30
  24.6 10.1 %collective-permute-start.7 = (bf16[128,256]{1,0:T(8,128)(2,1)S(1)}, bf16[128,256]{1,0:T(8,128)(2,1)S(1)}, u32[]{:S(2)}, u32[]{:S(2)}) collective-permute-start(bf16[128,256]{1,0:T(8,128)(2,1)S(1)} %get-tuple-element.26), channel_id=1, source_target_pairs={{0,2},{1,3},{2,0},{3,1},{4,6},{5,7},{6,4},{7,5},{8,10},{9,11},{10,... | collective-permute-start | bytes 196616 | tf_op jit(solution)/shard_map/gather_slopes/ppermute | solution.py:30
  25.5 12.4 %collective-permute-start.8 = (bf16[128,256]{1,0:T(8,128)(2,1)S(1)}, bf16[128,256]{1,0:T(8,128)(2,1)S(1)}, u32[]{:S(2)}, u32[]{:S(2)}) collective-permute-start(bf16[128,256]{1,0:T(8,128)(2,1)S(1)} %get-tuple-element.26), channel_id=1, source_target_pairs={{0,4},{1,5},{2,6},{3,7},{4,0},{5,1},{6,2},{7,3},{8,12},{9,13},{10,... | collective-permute-start | bytes 196616 | tf_op jit(solution)/shard_map/gather_slopes/ppermute | solution.py:30
  27.2 16.4 %collective-permute-start.9 = (bf16[128,256]{1,0:T(8,128)(2,1)S(1)}, bf16[128,256]{1,0:T(8,128)(2,1)S(1)}, u32[]{:S(2)}, u32[]{:S(2)}) collective-permute-start(bf16[128,256]{1,0:T(8,128)(2,1)S(1)} %get-tuple-element.26), channel_id=1, source_target_pairs={{0,6},{1,7},{2,4},{3,5},{4,2},{5,3},{6,0},{7,1},{8,14},{9,15},{10,... | collective-permute-start | bytes 196616 | tf_op jit(solution)/shard_map/gather_slopes/ppermute | solution.py:30
  29.0 4.3 %collective-permute-start.15 = (bf16[128,256]{1,0:T(8,128)(2,1)S(1)}, bf16[128,256]{1,0:T(8,128)(2,1)S(1)}, u32[]{:S(2)}, u32[]{:S(2)}) collective-permute-start(bf16[128,256]{1,0:T(8,128)(2,1)S(1)} %add_convert_fusion.4), channel_id=1, source_target_pairs={{0,8},{8,0},{16,24},{24,16},{1,9},{9,1},{17,25},{25,17},{2,10},{10... | collective-permute-start | bytes 196616 | tf_op jit(solution)/shard_map/weight_rows/ppermute | solution.py:30
  33.4 4.3 %collective-permute-start.16 = (bf16[128,256]{1,0:T(8,128)(2,1)S(1)}, bf16[128,256]{1,0:T(8,128)(2,1)S(1)}, u32[]{:S(2)}, u32[]{:S(2)}) collective-permute-start(bf16[128,256]{1,0:T(8,128)(2,1)S(1)} %add_convert_fusion.3), channel_id=1, source_target_pairs={{0,16},{8,24},{16,0},{24,8},{1,17},{9,25},{17,1},{25,9},{2,18},{10... | collective-permute-start | bytes 196616 | tf_op jit(solution)/shard_map/weight_rows/ppermute | solution.py:30
  37.7 4.3 %collective-permute-start.17 = (bf16[128,256]{1,0:T(8,128)(2,1)S(1)}, bf16[128,256]{1,0:T(8,128)(2,1)S(1)}, u32[]{:S(2)}, u32[]{:S(2)}) collective-permute-start(bf16[128,256]{1,0:T(8,128)(2,1)S(1)} %add_convert_fusion.2), channel_id=1, source_target_pairs={{0,2},{1,3},{2,0},{3,1},{4,6},{5,7},{6,4},{7,5},{8,10},{9,11},{10,... | collective-permute-start | bytes 196616 | tf_op jit(solution)/shard_map/weight_levels/ppermute | solution.py:30
  42.1 5.4 %collective-permute-start.18 = (bf16[128,256]{1,0:T(8,128)(2,1)S(1)}, bf16[128,256]{1,0:T(8,128)(2,1)S(1)}, u32[]{:S(2)}, u32[]{:S(2)}) collective-permute-start(bf16[128,256]{1,0:T(8,128)(2,1)S(1)} %add_convert_fusion.1), channel_id=1, source_target_pairs={{0,4},{1,5},{2,6},{3,7},{4,0},{5,1},{6,2},{7,3},{8,12},{9,13},{10,... | collective-permute-start | bytes 196616 | tf_op jit(solution)/shard_map/weight_levels/ppermute | solution.py:30
  43.6 4.0 %collective-permute-start.10 = (bf16[512,256]{1,0:T(8,128)(2,1)S(1)}, bf16[512,256]{1,0:T(8,128)(2,1)S(1)}, u32[]{:S(2)}, u32[]{:S(2)}) collective-permute-start(bf16[512,256]{1,0:T(8,128)(2,1)S(1)} %constant_dynamic-update-slice_fusion.refs_1_), channel_id=1, source_target_pairs={{0,1},{1,0},{2,3},{3,2},{4,5},{5,4},{6,7},{7,6},{8,9},{9,8},{10,11... | collective-permute-start | bytes 786440 | tf_op jit(solution)/shard_map/backward/ppermute | solution.py:30
  47.5 4.1 %collective-permute-start.19 = (bf16[128,256]{1,0:T(8,128)(2,1)S(1)}, bf16[128,256]{1,0:T(8,128)(2,1)S(1)}, u32[]{:S(2)}, u32[]{:S(2)}) collective-permute-start(bf16[128,256]{1,0:T(8,128)(2,1)S(1)} %add_convert_fusion), channel_id=1, source_target_pairs={{0,1},{1,0},{2,3},{3,2},{4,5},{5,4},{6,7},{7,6},{8,9},{9,8},{10,11... | collective-permute-start | bytes 196616 | tf_op jit(solution)/shard_map/weight_levels/ppermute | solution.py:30
  48.0 4.5 %collective-permute-start.11 = (bf16[128,256]{1,0:T(8,128)(2,1)S(1)}, bf16[128,256]{1,0:T(8,128)(2,1)S(1)}, u32[]{:S(2)}, u32[]{:S(2)}) collective-permute-start(bf16[128,256]{1,0:T(8,128)(2,1)S(1)} %get-tuple-element.28), channel_id=1, source_target_pairs={{0,8},{8,0},{16,24},{24,16},{1,9},{9,1},{17,25},{25,17},{2,10},{10... | collective-permute-start | bytes 196616 | tf_op jit(solution)/shard_map/backward/ppermute | solution.py:30
  49.1 4.6 %collective-permute-start.12 = (bf16[128,256]{1,0:T(8,128)(2,1)S(1)}, bf16[128,256]{1,0:T(8,128)(2,1)S(1)}, u32[]{:S(2)}, u32[]{:S(2)}) collective-permute-start(bf16[128,256]{1,0:T(8,128)(2,1)S(1)} %get-tuple-element.29), channel_id=1, source_target_pairs={{0,16},{8,24},{16,0},{24,8},{1,17},{9,25},{17,1},{25,9},{2,18},{10... | collective-permute-start | bytes 196616 | tf_op jit(solution)/shard_map/backward/ppermute | solution.py:30
  50.9 5.2 %collective-permute-start.13 = (bf16[128,256]{1,0:T(8,128)(2,1)S(1)}, bf16[128,256]{1,0:T(8,128)(2,1)S(1)}, u32[]{:S(2)}, u32[]{:S(2)}) collective-permute-start(bf16[128,256]{1,0:T(8,128)(2,1)S(1)} %get-tuple-element.30), channel_id=1, source_target_pairs={{0,24},{8,16},{16,8},{24,0},{1,25},{9,17},{17,9},{25,1},{2,26},{10... | collective-permute-start | bytes 196616 | tf_op jit(solution)/shard_map/backward/ppermute | solution.py:30
  (4 other events, 2.7 us)

commit v2 on v1

--- a/solution.py
+++ b/solution.py
@@ -57,37 +57,58 @@
 NT = (((1,), (1,)), ((), ()))
 
 
-def prep_kernel(per_step, rows_ref, cols_ref, count_ref, order_ref, values_ref, a_ref, at_ref, dense, select):
-    block = values_ref.shape[1]
+def prep_kernel(
+    per_step, count, rows_hbm, cols_hbm, order_hbm, values_hbm, weight_hbm, bias_hbm, cotangent_hbm,
+    a_ref, at_ref, weight_ref, bias_ref, cotangent_ref,
+    dense, select, values, order, rows, cols, sems,
+):
+    block = values.shape[1]
     nodes = select.shape[0]
     first = pl.program_id(0) * per_step
     row_blocks = pl.num_programs(0) * per_step
     row, col = lax.axis_index("row"), lax.axis_index("col")
+    pairs = (
+        (order_hbm, order), (rows_hbm, rows), (cols_hbm, cols), (values_hbm, values),
+        (weight_hbm, weight_ref), (bias_hbm, bias_ref), (cotangent_hbm, cotangent_ref),
+    )
+    copies = [pltpu.make_async_copy(src, dst, sems.at[i]) for i, (src, dst) in enumerate(pairs)]
+    once = pl.program_id(0) == 0
+
+    @pl.when(once)
+    def _():
+        for copy in copies:
+            copy.start()
 
     dense[...] = jnp.zeros_like(dense)
-    local = lax.broadcasted_iota(jnp.int32, (block, block), 0)
-    for chunk in range(nodes // block):
-        node = (row ^ chunk) * block + local
-        for part in range(nodes // block):
-            hit = order_ref[part : part + 1, :] == node
-            select[chunk * block : (chunk + 1) * block, part * block : (part + 1) * block] = jnp.where(
-                hit, 1.0, 0.0
-            ).astype(BF16)
+
+    @pl.when(once)
+    def _():
+        copies[0].wait()
+        local = lax.broadcasted_iota(jnp.int32, (block, block), 0)
+        for chunk in range(nodes // block):
+            node = (row ^ chunk) * block + local
+            for part in range(nodes // block):
+                hit = order[part : part + 1, :] == node
+                select[chunk * block : (chunk + 1) * block, part * block : (part + 1) * block] = jnp.where(
+                    hit, 1.0, 0.0
+                ).astype(BF16)
+        for copy in copies[1:]:
+            copy.wait()
 
     def slot(s, carry):
-        turned = rows_ref[s] ^ col
+        turned = rows[0, 0, s] ^ col
         place = (turned & 1) * (row_blocks // 2) + (turned >> 1) - first
 
         @pl.when((place >= 0) & (place < per_step))
         def _():
             dense[
                 pl.ds(pl.multiple_of(place * block, block), block),
-                pl.ds(pl.multiple_of(cols_ref[s] * block, block), block),
-            ] = values_ref[s]
+                pl.ds(pl.multiple_of(cols[0, 0, s] * block, block), block),
+            ] = values[s]
 
         return carry
 
-    lax.fori_loop(0, count_ref[0], slot, 0)
+    lax.fori_loop(0, count[0, 0], slot, 0)
 
     def store_a(i, j, value):
         a_ref[i, j] = value.astype(BF16)
@@ -101,31 +122,40 @@
     tiled_dot((nodes, per_step * block), store_at, select_rows, dense_rows)
 
 
-def prep(values, rows, cols, count, order, row_blocks):
+def prep(values, rows, cols, count, order, weight, bias, cotangent, row_blocks):
     capacity, block, _ = values.shape
     nodes = order.shape[0]
     per_step = min(row_blocks, 8)
-    smem = pl.BlockSpec(memory_space=pltpu.SMEM)
+    order = order.reshape(nodes // block, block)
+    bias = bias.reshape(1, bias.shape[0])
+    passed = (weight, bias, cotangent)
     return pl.pallas_call(
         functools.partial(prep_kernel, per_step),
         grid=(row_blocks // per_step,),
         out_shape=(
             jax.ShapeDtypeStruct((row_blocks * block, nodes), BF16),
             jax.ShapeDtypeStruct((nodes, row_blocks * block), BF16),
-        ),
-        in_specs=[smem, smem, smem, whole((nodes // block, block)), whole(values.shape)],
+        )
+        + tuple(jax.ShapeDtypeStruct(p.shape, p.dtype) for p in passed),
+        in_specs=[pl.BlockSpec(memory_space=pltpu.SMEM)] + [pl.BlockSpec(memory_space=pltpu.HBM)] * 7,
         out_specs=(
             pl.BlockSpec((per_step * block, nodes), lambda i: (i, 0)),
             pl.BlockSpec((nodes, per_step * block), lambda i: (0, i)),
-        ),
+        )
+        + tuple(whole(p.shape) for p in passed),
         scratch_shapes=[
             pltpu.VMEM((per_step * block, nodes), BF16),
             pltpu.VMEM((nodes, nodes), BF16),
+            pltpu.VMEM(values.shape, BF16),
+            pltpu.VMEM(order.shape, jnp.int32),
+            pltpu.SMEM(rows.shape, jnp.int32),
+            pltpu.SMEM(cols.shape, jnp.int32),
+            pltpu.SemaphoreType.DMA((7,)),
         ],
         compiler_params=params(),
         cost_estimate=cost(4 * row_blocks * block * nodes * nodes, 2 * values.size),
         name="prep",
-    )(rows, cols, count, order.reshape(nodes // block, block), values)
+    )(count, *(pltpu.with_memory_space_constraint(x, pltpu.HBM) for x in (rows, cols, order, values, *passed)))
 
 
 def product_kernel(pieces, *refs):
@@ -174,9 +204,9 @@
     return cuts
 
 
-def pointwise_kernel(terms, *refs):
+def slopes_kernel(terms, *refs):
     weight, bias, cotangent = refs[terms : terms + 3]
-    activations, slopes, kept, sent, whole_term = refs[terms + 3 :]
+    preact_ref, slopes, kept, sent, whole_term = refs[terms + 3 :]
     mixed = refs[0][...].astype(F32)
     for ref in refs[1:terms]:
         mixed = mixed + ref[...].astype(F32)
@@ -187,8 +217,8 @@
         + jnp.dot(low, weight[...], preferred_element_type=F32)
         + bias[...]
     )
+    preact_ref[...] = preact
     gate = 1.0 / (1.0 + jnp.exp(-preact))
-    activations[...] = (preact * gate).astype(BF16)
     slope = (cotangent[...].astype(F32) * (gate * (1.0 + preact * (1.0 - gate)))).astype(BF16)
     slopes[...] = slope
     whole_term[...] = lax.dot_general(high, slope, (((0,), (0,)), ((), ())), preferred_element_type=F32)
@@ -198,19 +228,38 @@
     sent[...] = whole_term[pl.ds(pl.multiple_of((1 - core) * half, half), half), :].astype(sent.dtype)
 
 
-def pointwise(terms, weight, bias, cotangent):
+def slopes_of(terms, weight, bias, cotangent):
     nodes, width = cotangent.shape
     depth = weight.shape[0]
-    node_out = jax.ShapeDtypeStruct((nodes, width), BF16)
     half_out = jax.ShapeDtypeStruct((depth // 2, width), BF16)
     return pl.pallas_call(
-        functools.partial(pointwise_kernel, len(terms)),
-        out_shape=(node_out, node_out, half_out, half_out),
+        functools.partial(slopes_kernel, len(terms)),
+        out_shape=(
+            jax.ShapeDtypeStruct((nodes, width), F32),
+            jax.ShapeDtypeStruct((nodes, width), BF16),
+            half_out,
+            half_out,
+        ),
         scratch_shapes=[pltpu.VMEM((depth, width), F32)],
         compiler_params=params(),
         cost_estimate=cost(6 * nodes * depth * width, 2 * nodes * width * (len(terms) + 5), nodes * width),
-        name="pointwise",
-    )(*terms, weight, bias.reshape(1, width), cotangent)
+        name="slopes",
+    )(*terms, weight, bias, cotangent)
+
+
+def activation_kernel(preact_ref, out):
+    preact = preact_ref[...]
+    out[...] = (preact / (1.0 + jnp.exp(-preact))).astype(BF16)
+
+
+def activation(preact):
+    return pl.pallas_call(
+        activation_kernel,
+        out_shape=jax.ShapeDtypeStruct(preact.shape, BF16),
+        compiler_params=params(),
+        cost_estimate=cost(4 * preact.size, 6 * preact.size, preact.size),
+        name="activation",
+    )(preact)
 
 
 def feature_kernel(terms, *refs):
@@ -252,14 +301,13 @@
     row_devices = lax.axis_size("row")
     col_devices = lax.axis_size("col")
     levels = col_devices // 2
-    values = block_values[0, 0]
-    block = values.shape[1]
+    block = block_values.shape[3]
     row_blocks = node_count * col_devices // block
 
     with jax.named_scope("gather_features"):
         pieces = [features] + [swap(features, "row", m) for m in range(1, row_devices)]
-    tile, tile_turned = prep(
-        values, block_rows[0, 0], block_cols[0, 0], counts[0], cluster_order, row_blocks
+    tile, tile_turned, weight_near, bias_near, cotangent_near = prep(
+        block_values[0, 0], block_rows, block_cols, counts, cluster_order, weight, bias_term, cotangent, row_blocks
     )
 
     with jax.named_scope("forward"):
@@ -268,29 +316,43 @@
         arrived = swap(other, "col", 1)
         pairs = [add(k, arrived[i * node_count : (i + 1) * node_count]) for i, k in enumerate(kept)]
         terms = [pairs[0]] + [swap(pairs[m], "col", 2 * m) for m in range(1, levels)]
-        activations, slopes, weight_kept, weight_sent = pointwise(terms, weight, bias_term, cotangent)
+        preact, slopes, weight_kept, weight_sent = slopes_of(terms, weight_near, bias_near, cotangent_near)
 
     with jax.named_scope("gather_slopes"):
         slope_own = [slopes] + [swap(slopes, "col", 2 * m) for m in range(1, levels)]
+    activations = activation(preact)
+
     with jax.named_scope("weight_rows"):
         term = add(weight_kept, swap(weight_sent, "col", 1))
-        mask = 1
-        while mask < row_devices:
+        masks = [1 << i for i in range((row_devices - 1).bit_length())]
+        for mask in masks[:-1]:
             term = add(term, swap(term, "row", mask))
-            mask *= 2
+        last = swap(term, "row", masks[-1])
 
     with jax.named_scope("backward"):
         slope_half = jnp.concatenate(slope_own)
+        slope_half, last = lax.optimization_barrier((slope_half, last))
         slope_other = swap(slope_half, "col", 1)
-        node_terms = product(tile_turned, [slope_half, slope_other], [node_count] * row_devices, "backward_tile")
+        node_terms = product(
+            tile_turned, [slope_half, slope_other], [node_count] * row_devices, "backward_tile"
+        )
+
+    with jax.named_scope("weight_levels"):
+        term = add(term, last)
+        masks = [2 << i for i in range((levels - 1).bit_length())]
+        for mask in masks[:-1]:
+            other = swap(term, "col", mask)
+            if mask == 2:
+                other, node_terms[0] = lax.optimization_barrier((other, node_terms[0]))
+            term = add(term, other)
+        last = swap(term, "col", masks[-1])
+
+    with jax.named_scope("backward"):
         node_sum = [node_terms[0]] + [swap(node_terms[m], "row", m) for m in range(1, row_devices)]
-        grad_features = feature_gradient(node_sum, weight)
+        grad_features = feature_gradient(node_sum, weight_near)
 
     with jax.named_scope("weight_levels"):
-        mask = 2
-        while mask < col_devices:
-            term = add(term, swap(term, "col", mask))
-            mask *= 2
+        term = add(term, last)
         partner = swap(term, "col", 1)
         core = lax.axis_index("col") & 1
         scale = 1.0 / math.sqrt(node_count * row_devices * col_devices)

time: 57 us -> 49.6 us (0.87)
  waiting for transfers between devices: 26.1 us -> 21.4 us
  local copies, waits for them, and re-layouts: 2.41 us -> 0.01 us
  starting transfers between devices: 21.1 us -> 20.3 us
    ppermute x20, waiting for transfers between devices: 26.1 us -> 21.4 us  [swap(): return lax.ppermute(value, axis, [(i, i ^ mask) for i in range(size)])]
    unnamed x19 -> x2, local copies, waits for them, and re-layouts: 2.41 us -> 0.01 us
    ppermute x20, starting transfers between devices: 21.1 us -> 20.3 us  [swap(): return lax.ppermute(value, axis, [(i, i ^ mask) for i in range(size)])]
    pallas_call x1 -> x2, Pallas kernels: 0.89 us -> 1.15 us  [the longest x1 0.68 us: activation(): pl.pallas_call(activation_kernel, out_shape=jax.ShapeDtypeStruct(preact.s...]
  transfers between devices with their start and end apart: 20 -> 20, of which waited for: 11 -> 13; matrix products, arithmetic and copies ran while one was open for 1% -> 0% of each run, Pallas kernels for 5% -> 9%
where the time goes in v2:
time: 49.6 us; the launch traced here: 49.4 us
  waiting for transfers between devices  21.4 us (43%)
  starting transfers between devices  20.3 us (41%)
  Pallas kernels  5.34 us (11%)
  between operations  1.43 us (3%)
  other arithmetic  0.91 us (2%)
    ppermute x20, waiting for transfers between devices, swap(): return lax.ppermute(value, axis, [(i, i ^ mask) for i in range(size)])  21.4 us
    ppermute x20, starting transfers between devices, swap(): return lax.ppermute(value, axis, [(i, i ^ mask) for i in range(size)])  20.3 us
    pallas_call x1, Pallas kernels, prep(): pl.pallas_call(functools.partial(prep_kernel, per_step), grid=(row_blocks...  2.49 us
  transfers between devices with their start and end apart: 20, of which 13 were waited for; matrix products, arithmetic and copies ran while one was open for 0% of the time, Pallas kernels for 9%

profile of v2, /device:TPU:0, one launch (start us, length us, event | category | flops | bytes accessed | tf_op | source)
XLA Modules:
  0.0 49.4 jit_solution(16047256528234979972)
XLA Ops:
  0.6 3.0 %collective-permute-start = (bf16[128,256]{1,0:T(8,128)(2,1)}, bf16[128,256]{1,0:T(8,128)(2,1)S(1)}, u32[]{:S(2)}, u32[]{:S(2)}) collective-permute-start(bf16[128,256]{1,0:T(8,128)(2,1)} %refs_1_.1), channel_id=1, source_target_pairs={{0,8},{8,0},{16,24},{24,16},{1,9},{9,1},{17,25},{25,17},{2,10},{10... | collective-permute-start | bytes 196616 | tf_op jit(solution)/shard_map/gather_features/ppermute | solution.py:30
  3.6 1.5 %collective-permute-start.1 = (bf16[128,256]{1,0:T(8,128)(2,1)}, bf16[128,256]{1,0:T(8,128)(2,1)S(1)}, u32[]{:S(2)}, u32[]{:S(2)}) collective-permute-start(bf16[128,256]{1,0:T(8,128)(2,1)} %refs_1_.1), channel_id=1, source_target_pairs={{0,16},{8,24},{16,0},{24,8},{1,17},{9,25},{17,1},{25,9},{2,18},{10... | collective-permute-start | bytes 196616 | tf_op jit(solution)/shard_map/gather_features/ppermute | solution.py:30
  5.8 2.5 %prep.1 = (bf16[1024,512]{1,0:T(8,128)(2,1)S(1)}, bf16[512,1024]{1,0:T(8,128)(2,1)S(1)}, bf16[256,256]{1,0:T(8,128)(2,1)S(1)}, f32[1,256]{1,0:T(1,128)S(1)}, bf16[128,256]{1,0:T(8,128)(2,1)S(1)}) custom-call(s32[1,1]{1,0:T(1,128)S(6)} %copy.12.count, s32[1,1,16]{2,1,0:T(1,128)} %rows_hbm.1, s32[1,1,16]{2,1,0:T(1,128)} %cols_hbm.1, s32[4,128]{1,0:T(4,128)} %bitcast.4, ...), custom_call_target="tpu_custom_call" | custom-call | flops 1073741824 | bytes 524288 | tf_op jit(solution)/shard_map/prep/pallas_call | solution.py:132
  8.4 2.2 %collective-permute-done.2.refs_4_ = bf16[128,256]{1,0:T(8,128)(2,1)S(1)} collective-permute-done((bf16[128,256]{1,0:T(8,128)(2,1)}, bf16[128,256]{1,0:T(8,128)(2,1)S(1)}, u32[]{:S(2)}, u32[]{:S(2)}) %collective-permute-start.2) | collective-permute-done | bytes 65568 | tf_op jit(solution)/shard_map/gather_features/ppermute | solution.py:30
  11.1 1.5 %collective-permute-done.3 = bf16[512,256]{1,0:T(8,128)(2,1)S(1)} collective-permute-done((bf16[512,256]{1,0:T(8,128)(2,1)S(1)}, bf16[512,256]{1,0:T(8,128)(2,1)S(1)}, u32[]{:S(2)}, u32[]{:S(2)}) %collective-permute-start.3) | collective-permute-done | bytes 262176 | tf_op jit(solution)/shard_map/forward/ppermute | solution.py:30
  12.6 1.6 %collective-permute-start.4 = (bf16[128,256]{1,0:T(8,128)(2,1)S(1)}, bf16[128,256]{1,0:T(8,128)(2,1)S(1)}, u32[]{:S(2)}, u32[]{:S(2)}) collective-permute-start(bf16[128,256]{1,0:T(8,128)(2,1)S(1)} %get-tuple-element.49), channel_id=1, source_target_pairs={{0,2},{1,3},{2,0},{3,1},{4,6},{5,7},{6,4},{7,5},{8,10},{9,11},{10,... | collective-permute-start | bytes 196616 | tf_op jit(solution)/shard_map/forward/ppermute | solution.py:30
  14.3 2.6 %collective-permute-start.5 = (bf16[128,256]{1,0:T(8,128)(2,1)S(1)}, bf16[128,256]{1,0:T(8,128)(2,1)S(1)}, u32[]{:S(2)}, u32[]{:S(2)}) collective-permute-start(bf16[128,256]{1,0:T(8,128)(2,1)S(1)} %get-tuple-element.48), channel_id=1, source_target_pairs={{0,4},{1,5},{2,6},{3,7},{4,0},{5,1},{6,2},{7,3},{8,12},{9,13},{10,... | collective-permute-start | bytes 196616 | tf_op jit(solution)/shard_map/forward/ppermute | solution.py:30
  17.1 4.7 %collective-permute-done.5.refs_2_ = bf16[128,256]{1,0:T(8,128)(2,1)S(1)} collective-permute-done((bf16[128,256]{1,0:T(8,128)(2,1)S(1)}, bf16[128,256]{1,0:T(8,128)(2,1)S(1)}, u32[]{:S(2)}, u32[]{:S(2)}) %collective-permute-start.5) | collective-permute-done | bytes 65568 | tf_op jit(solution)/shard_map/forward/ppermute | solution.py:30
  21.8 1.2 %collective-permute-done.6.refs_3_ = bf16[128,256]{1,0:T(8,128)(2,1)S(1)} collective-permute-done((bf16[128,256]{1,0:T(8,128)(2,1)S(1)}, bf16[128,256]{1,0:T(8,128)(2,1)S(1)}, u32[]{:S(2)}, u32[]{:S(2)}) %collective-permute-start.6) | collective-permute-done | bytes 65568 | tf_op jit(solution)/shard_map/forward/ppermute | solution.py:30
  23.6 1.2 %collective-permute-done.7 = bf16[128,256]{1,0:T(8,128)(2,1)S(1)} collective-permute-done((bf16[128,256]{1,0:T(8,128)(2,1)S(1)}, bf16[128,256]{1,0:T(8,128)(2,1)S(1)}, u32[]{:S(2)}, u32[]{:S(2)}) %collective-permute-start.7) | collective-permute-done | bytes 65568 | tf_op jit(solution)/shard_map/weight_rows/ppermute | solution.py:30
  25.5 1.8 %collective-permute-start.10 = (bf16[128,256]{1,0:T(8,128)(2,1)S(1)}, bf16[128,256]{1,0:T(8,128)(2,1)S(1)}, u32[]{:S(2)}, u32[]{:S(2)}) collective-permute-start(bf16[128,256]{1,0:T(8,128)(2,1)S(1)} %get-tuple-element.37), channel_id=1, source_target_pairs={{0,4},{1,5},{2,6},{3,7},{4,0},{5,1},{6,2},{7,3},{8,12},{9,13},{10,... | collective-permute-start | bytes 196616 | tf_op jit(solution)/shard_map/gather_slopes/ppermute | solution.py:30
  27.2 1.4 %collective-permute-start.11 = (bf16[128,256]{1,0:T(8,128)(2,1)S(1)}, bf16[128,256]{1,0:T(8,128)(2,1)S(1)}, u32[]{:S(2)}, u32[]{:S(2)}) collective-permute-start(bf16[128,256]{1,0:T(8,128)(2,1)S(1)} %get-tuple-element.37), channel_id=1, source_target_pairs={{0,6},{1,7},{2,4},{3,5},{4,2},{5,3},{6,0},{7,1},{8,14},{9,15},{10,... | collective-permute-start | bytes 196616 | tf_op jit(solution)/shard_map/gather_slopes/ppermute | solution.py:30
  29.9 3.7 %collective-permute-done.10 = bf16[128,256]{1,0:T(8,128)(2,1)S(1)} collective-permute-done((bf16[128,256]{1,0:T(8,128)(2,1)S(1)}, bf16[128,256]{1,0:T(8,128)(2,1)S(1)}, u32[]{:S(2)}, u32[]{:S(2)}) %collective-permute-start.10) | collective-permute-done | bytes 65568 | tf_op jit(solution)/shard_map/gather_slopes/ppermute | solution.py:30
  34.3 1.0 %collective-permute-start.13 = (bf16[128,256]{1,0:T(8,128)(2,1)S(1)}, bf16[128,256]{1,0:T(8,128)(2,1)S(1)}, u32[]{:S(2)}, u32[]{:S(2)}) collective-permute-start(bf16[128,256]{1,0:T(8,128)(2,1)S(1)} %add_convert_fusion.2), channel_id=1, source_target_pairs={{0,2},{1,3},{2,0},{3,1},{4,6},{5,7},{6,4},{7,5},{8,10},{9,11},{10,... | collective-permute-start | bytes 196616 | tf_op jit(solution)/shard_map/weight_levels/ppermute | solution.py:30
  36.2 2.6 %collective-permute-done.13 = bf16[128,256]{1,0:T(8,128)(2,1)S(1)} collective-permute-done((bf16[128,256]{1,0:T(8,128)(2,1)S(1)}, bf16[128,256]{1,0:T(8,128)(2,1)S(1)}, u32[]{:S(2)}, u32[]{:S(2)}) %collective-permute-start.13) | collective-permute-done | bytes 65568 | tf_op jit(solution)/shard_map/weight_levels/ppermute | solution.py:30
  38.8 1.8 %collective-permute-start.18 = (bf16[128,256]{1,0:T(8,128)(2,1)S(1)}, bf16[128,256]{1,0:T(8,128)(2,1)S(1)}, u32[]{:S(2)}, u32[]{:S(2)}) collective-permute-start(bf16[128,256]{1,0:T(8,128)(2,1)S(1)} %add_convert_fusion.1), channel_id=1, source_target_pairs={{0,4},{1,5},{2,6},{3,7},{4,0},{5,1},{6,2},{7,3},{8,12},{9,13},{10,... | collective-permute-start | bytes 196616 | tf_op jit(solution)/shard_map/weight_levels/ppermute | solution.py:30
  40.7 1.5 %collective-permute-start.15 = (bf16[128,256]{1,0:T(8,128)(2,1)S(1)}, bf16[128,256]{1,0:T(8,128)(2,1)S(1)}, u32[]{:S(2)}, u32[]{:S(2)}) collective-permute-start(bf16[128,256]{1,0:T(8,128)(2,1)S(1)} %get-tuple-element.43), channel_id=1, source_target_pairs={{0,8},{8,0},{16,24},{24,16},{1,9},{9,1},{17,25},{25,17},{2,10},{10... | collective-permute-start | bytes 196616 | tf_op jit(solution)/shard_map/backward/ppermute | solution.py:30
  42.7 1.5 %collective-permute-start.17 = (bf16[128,256]{1,0:T(8,128)(2,1)S(1)}, bf16[128,256]{1,0:T(8,128)(2,1)S(1)}, u32[]{:S(2)}, u32[]{:S(2)}) collective-permute-start(bf16[128,256]{1,0:T(8,128)(2,1)S(1)} %get-tuple-element.45), channel_id=1, source_target_pairs={{0,24},{8,16},{16,8},{24,0},{1,25},{9,17},{17,9},{25,1},{2,26},{10... | collective-permute-start | bytes 196616 | tf_op jit(solution)/shard_map/backward/ppermute | solution.py:30
  44.2 0.8 %collective-permute-done.18 = bf16[128,256]{1,0:T(8,128)(2,1)S(1)} collective-permute-done((bf16[128,256]{1,0:T(8,128)(2,1)S(1)}, bf16[128,256]{1,0:T(8,128)(2,1)S(1)}, u32[]{:S(2)}, u32[]{:S(2)}) %collective-permute-start.18) | collective-permute-done | bytes 65568 | tf_op jit(solution)/shard_map/weight_levels/ppermute | solution.py:30
  45.0 0.7 %activation.1 = bf16[128,256]{1,0:T(8,128)(2,1)} custom-call(f32[128,256]{1,0:T(8,128)S(1)} %get-tuple-element.34.preact_ref), custom_call_target="tpu_custom_call" | custom-call | flops 131072 | bytes 196608 | tf_op jit(solution)/shard_map/activation/pallas_call | solution.py:256
  45.7 1.0 %collective-permute-done.16.refs_2_ = bf16[128,256]{1,0:T(8,128)(2,1)S(1)} collective-permute-done((bf16[128,256]{1,0:T(8,128)(2,1)S(1)}, bf16[128,256]{1,0:T(8,128)(2,1)S(1)}, u32[]{:S(2)}, u32[]{:S(2)}) %collective-permute-start.16) | collective-permute-done | bytes 65568 | tf_op jit(solution)/shard_map/backward/ppermute | solution.py:30
  46.7 1.1 %collective-permute-done.17.refs_3_ = bf16[128,256]{1,0:T(8,128)(2,1)S(1)} collective-permute-done((bf16[128,256]{1,0:T(8,128)(2,1)S(1)}, bf16[128,256]{1,0:T(8,128)(2,1)S(1)}, u32[]{:S(2)}, u32[]{:S(2)}) %collective-permute-start.17) | collective-permute-done | bytes 65568 | tf_op jit(solution)/shard_map/backward/ppermute | solution.py:30
  47.8 0.8 %feature_gradient.1 = bf16[128,256]{1,0:T(8,128)(2,1)} custom-call(bf16[128,256]{1,0:T(8,128)(2,1)S(1)} %get-tuple-element.42.refs_0_, bf16[128,256]{1,0:T(8,128)(2,1)S(1)} %collective-permute-done.15.refs_1_, bf16[128,256]{1,0:T(8,128)(2,1)S(1)} %collective-permute-done.16.refs_2_, bf16[128,256]{1,0:T(8,128)(2,1)S(1)} %collective-permute-done.17.refs_3_, ...), custom_call_target="tpu_custom_call" | custom-call | flops 16777216 | bytes 393216 | tf_op jit(solution)/shard_map/backward/feature_gradient/pallas_call | solution.py:276
  48.7 0.7 %convert_multiply_fusion = f32[256,256]{1,0:T(8,128)} fusion(bf16[128,256]{1,0:T(8,128)(2,1)S(1)} %collective-permute-done.19, bf16[128,256]{1,0:T(8,128)(2,1)S(1)} %add_convert_fusion, pred[]{:T(512)S(6)} %eq.3), kind=kLoop, calls=%fused_computation.1 | loop fusion | flops 720896 | bytes 393217 | tf_op jit(solution)/shard_map/weight_levels/mul | solution.py:362
  (32 shorter events, 5.4 us)
Async XLA Ops:
  0.6 7.7 %collective-permute-start = (bf16[128,256]{1,0:T(8,128)(2,1)}, bf16[128,256]{1,0:T(8,128)(2,1)S(1)}, u32[]{:S(2)}, u32[]{:S(2)}) collective-permute-start(bf16[128,256]{1,0:T(8,128)(2,1)} %refs_1_.1), channel_id=1, source_target_pairs={{0,8},{8,0},{16,24},{24,16},{1,9},{9,1},{17,25},{25,17},{2,10},{10... | collective-permute-start | bytes 196616 | tf_op jit(solution)/shard_map/gather_features/ppermute | solution.py:30
  3.6 4.7 %collective-permute-start.1 = (bf16[128,256]{1,0:T(8,128)(2,1)}, bf16[128,256]{1,0:T(8,128)(2,1)S(1)}, u32[]{:S(2)}, u32[]{:S(2)}) collective-permute-start(bf16[128,256]{1,0:T(8,128)(2,1)} %refs_1_.1), channel_id=1, source_target_pairs={{0,16},{8,24},{16,0},{24,8},{1,17},{9,25},{17,1},{25,9},{2,18},{10... | collective-permute-start | bytes 196616 | tf_op jit(solution)/shard_map/gather_features/ppermute | solution.py:30
  5.2 5.4 %collective-permute-start.2 = (bf16[128,256]{1,0:T(8,128)(2,1)}, bf16[128,256]{1,0:T(8,128)(2,1)S(1)}, u32[]{:S(2)}, u32[]{:S(2)}) collective-permute-start(bf16[128,256]{1,0:T(8,128)(2,1)} %refs_1_.1), channel_id=1, source_target_pairs={{0,24},{8,16},{16,8},{24,0},{1,25},{9,17},{17,9},{25,1},{2,26},{10... | collective-permute-start | bytes 196616 | tf_op jit(solution)/shard_map/gather_features/ppermute | solution.py:30
  5.8 4.7 %copy-start = (bf16[128,256]{1,0:T(8,128)(2,1)S(1)}, bf16[128,256]{1,0:T(8,128)(2,1)}, u32[]{:S(2)}) copy-start(bf16[128,256]{1,0:T(8,128)(2,1)} %refs_1_.1) | copy-start | bytes 196612
  11.0 1.6 %collective-permute-start.3 = (bf16[512,256]{1,0:T(8,128)(2,1)S(1)}, bf16[512,256]{1,0:T(8,128)(2,1)S(1)}, u32[]{:S(2)}, u32[]{:S(2)}) collective-permute-start(bf16[512,256]{1,0:T(8,128)(2,1)S(1)} %get-tuple-element.27), channel_id=1, source_target_pairs={{0,1},{1,0},{2,3},{3,2},{4,5},{5,4},{6,7},{7,6},{8,9},{9,8},{10,11... | collective-permute-start | bytes 786440 | tf_op jit(solution)/shard_map/forward/ppermute | solution.py:30
  12.6 4.5 %collective-permute-start.4 = (bf16[128,256]{1,0:T(8,128)(2,1)S(1)}, bf16[128,256]{1,0:T(8,128)(2,1)S(1)}, u32[]{:S(2)}, u32[]{:S(2)}) collective-permute-start(bf16[128,256]{1,0:T(8,128)(2,1)S(1)} %get-tuple-element.49), channel_id=1, source_target_pairs={{0,2},{1,3},{2,0},{3,1},{4,6},{5,7},{6,4},{7,5},{8,10},{9,11},{10,... | collective-permute-start | bytes 196616 | tf_op jit(solution)/shard_map/forward/ppermute | solution.py:30
  14.3 7.5 %collective-permute-start.5 = (bf16[128,256]{1,0:T(8,128)(2,1)S(1)}, bf16[128,256]{1,0:T(8,128)(2,1)S(1)}, u32[]{:S(2)}, u32[]{:S(2)}) collective-permute-start(bf16[128,256]{1,0:T(8,128)(2,1)S(1)} %get-tuple-element.48), channel_id=1, source_target_pairs={{0,4},{1,5},{2,6},{3,7},{4,0},{5,1},{6,2},{7,3},{8,12},{9,13},{10,... | collective-permute-start | bytes 196616 | tf_op jit(solution)/shard_map/forward/ppermute | solution.py:30
  16.9 6.2 %collective-permute-start.6 = (bf16[128,256]{1,0:T(8,128)(2,1)S(1)}, bf16[128,256]{1,0:T(8,128)(2,1)S(1)}, u32[]{:S(2)}, u32[]{:S(2)}) collective-permute-start(bf16[128,256]{1,0:T(8,128)(2,1)S(1)} %get-tuple-element.47), channel_id=1, source_target_pairs={{0,6},{1,7},{2,4},{3,5},{4,2},{5,3},{6,0},{7,1},{8,14},{9,15},{10,... | collective-permute-start | bytes 196616 | tf_op jit(solution)/shard_map/forward/ppermute | solution.py:30
  23.5 1.3 %collective-permute-start.7 = (bf16[128,256]{1,0:T(8,128)(2,1)S(1)}, bf16[128,256]{1,0:T(8,128)(2,1)S(1)}, u32[]{:S(2)}, u32[]{:S(2)}) collective-permute-start(bf16[128,256]{1,0:T(8,128)(2,1)S(1)} %get-tuple-element.36), channel_id=1, source_target_pairs={{0,1},{1,0},{2,3},{3,2},{4,5},{5,4},{6,7},{7,6},{8,9},{9,8},{10,11... | collective-permute-start | bytes 196616 | tf_op jit(solution)/shard_map/weight_rows/ppermute | solution.py:30
  24.9 4.3 %collective-permute-start.8 = (bf16[128,256]{1,0:T(8,128)(2,1)S(1)}, bf16[128,256]{1,0:T(8,128)(2,1)S(1)}, u32[]{:S(2)}, u32[]{:S(2)}) collective-permute-start(bf16[128,256]{1,0:T(8,128)(2,1)S(1)} %add_convert_fusion.4), channel_id=1, source_target_pairs={{0,8},{8,0},{16,24},{24,16},{1,9},{9,1},{17,25},{25,17},{2,10},{10... | collective-permute-start | bytes 196616 | tf_op jit(solution)/shard_map/weight_rows/ppermute | solution.py:30
  25.5 8.1 %collective-permute-start.10 = (bf16[128,256]{1,0:T(8,128)(2,1)S(1)}, bf16[128,256]{1,0:T(8,128)(2,1)S(1)}, u32[]{:S(2)}, u32[]{:S(2)}) collective-permute-start(bf16[128,256]{1,0:T(8,128)(2,1)S(1)} %get-tuple-element.37), channel_id=1, source_target_pairs={{0,4},{1,5},{2,6},{3,7},{4,0},{5,1},{6,2},{7,3},{8,12},{9,13},{10,... | collective-permute-start | bytes 196616 | tf_op jit(solution)/shard_map/gather_slopes/ppermute | solution.py:30
  27.2 6.3 %collective-permute-start.11 = (bf16[128,256]{1,0:T(8,128)(2,1)S(1)}, bf16[128,256]{1,0:T(8,128)(2,1)S(1)}, u32[]{:S(2)}, u32[]{:S(2)}) collective-permute-start(bf16[128,256]{1,0:T(8,128)(2,1)S(1)} %get-tuple-element.37), channel_id=1, source_target_pairs={{0,6},{1,7},{2,4},{3,5},{4,2},{5,3},{6,0},{7,1},{8,14},{9,15},{10,... | collective-permute-start | bytes 196616 | tf_op jit(solution)/shard_map/gather_slopes/ppermute | solution.py:30
  28.7 5.5 %collective-permute-start.9 = (bf16[128,256]{1,0:T(8,128)(2,1)S(1)}, bf16[128,256]{1,0:T(8,128)(2,1)S(1)}, u32[]{:S(2)}, u32[]{:S(2)}) collective-permute-start(bf16[128,256]{1,0:T(8,128)(2,1)S(1)} %get-tuple-element.37), channel_id=1, source_target_pairs={{0,2},{1,3},{2,0},{3,1},{4,6},{5,7},{6,4},{7,5},{8,10},{9,11},{10,... | collective-permute-start | bytes 196616 | tf_op jit(solution)/shard_map/gather_slopes/ppermute | solution.py:30
  29.2 4.9 %collective-permute-start.12 = (bf16[128,256]{1,0:T(8,128)(2,1)S(1)}, bf16[128,256]{1,0:T(8,128)(2,1)S(1)}, u32[]{:S(2)}, u32[]{:S(2)}) collective-permute-start(bf16[128,256]{1,0:T(8,128)(2,1)S(1)} %add_convert_fusion.3), channel_id=1, source_target_pairs={{0,16},{8,24},{16,0},{24,8},{1,17},{9,25},{17,1},{25,9},{2,18},{10... | collective-permute-start | bytes 196616 | tf_op jit(solution)/shard_map/weight_rows/ppermute | solution.py:30
  34.2 1.6 %collective-permute-start.14 = (bf16[512,256]{1,0:T(8,128)(2,1)S(1)}, bf16[512,256]{1,0:T(8,128)(2,1)S(1)}, u32[]{:S(2)}, u32[]{:S(2)}) collective-permute-start(bf16[512,256]{1,0:T(8,128)(2,1)S(1)} %pad_maximum_fusion.refs_1_), channel_id=1, source_target_pairs={{0,1},{1,0},{2,3},{3,2},{4,5},{5,4},{6,7},{7,6},{8,9},{9,8},{10,11... | collective-permute-start | bytes 786440 | tf_op jit(solution)/shard_map/backward/ppermute | solution.py:30
  34.3 4.6 %collective-permute-start.13 = (bf16[128,256]{1,0:T(8,128)(2,1)S(1)}, bf16[128,256]{1,0:T(8,128)(2,1)S(1)}, u32[]{:S(2)}, u32[]{:S(2)}) collective-permute-start(bf16[128,256]{1,0:T(8,128)(2,1)S(1)} %add_convert_fusion.2), channel_id=1, source_target_pairs={{0,2},{1,3},{2,0},{3,1},{4,6},{5,7},{6,4},{7,5},{8,10},{9,11},{10,... | collective-permute-start | bytes 196616 | tf_op jit(solution)/shard_map/weight_levels/ppermute | solution.py:30
  38.8 6.1 %collective-permute-start.18 = (bf16[128,256]{1,0:T(8,128)(2,1)S(1)}, bf16[128,256]{1,0:T(8,128)(2,1)S(1)}, u32[]{:S(2)}, u32[]{:S(2)}) collective-permute-start(bf16[128,256]{1,0:T(8,128)(2,1)S(1)} %add_convert_fusion.1), channel_id=1, source_target_pairs={{0,4},{1,5},{2,6},{3,7},{4,0},{5,1},{6,2},{7,3},{8,12},{9,13},{10,... | collective-permute-start | bytes 196616 | tf_op jit(solution)/shard_map/weight_levels/ppermute | solution.py:30
  40.7 5.0 %collective-permute-start.15 = (bf16[128,256]{1,0:T(8,128)(2,1)S(1)}, bf16[128,256]{1,0:T(8,128)(2,1)S(1)}, u32[]{:S(2)}, u32[]{:S(2)}) collective-permute-start(bf16[128,256]{1,0:T(8,128)(2,1)S(1)} %get-tuple-element.43), channel_id=1, source_target_pairs={{0,8},{8,0},{16,24},{24,16},{1,9},{9,1},{17,25},{25,17},{2,10},{10... | collective-permute-start | bytes 196616 | tf_op jit(solution)/shard_map/backward/ppermute | solution.py:30
  42.2 4.6 %collective-permute-start.16 = (bf16[128,256]{1,0:T(8,128)(2,1)S(1)}, bf16[128,256]{1,0:T(8,128)(2,1)S(1)}, u32[]{:S(2)}, u32[]{:S(2)}) collective-permute-start(bf16[128,256]{1,0:T(8,128)(2,1)S(1)} %get-tuple-element.44), channel_id=1, source_target_pairs={{0,16},{8,24},{16,0},{24,8},{1,17},{9,25},{17,1},{25,9},{2,18},{10... | collective-permute-start | bytes 196616 | tf_op jit(solution)/shard_map/backward/ppermute | solution.py:30
  42.7 5.2 %collective-permute-start.17 = (bf16[128,256]{1,0:T(8,128)(2,1)S(1)}, bf16[128,256]{1,0:T(8,128)(2,1)S(1)}, u32[]{:S(2)}, u32[]{:S(2)}) collective-permute-start(bf16[128,256]{1,0:T(8,128)(2,1)S(1)} %get-tuple-element.45), channel_id=1, source_target_pairs={{0,24},{8,16},{16,8},{24,0},{1,25},{9,17},{17,9},{25,1},{2,26},{10... | collective-permute-start | bytes 196616 | tf_op jit(solution)/shard_map/backward/ppermute | solution.py:30
  44.9 3.7 %collective-permute-start.19 = (bf16[128,256]{1,0:T(8,128)(2,1)S(1)}, bf16[128,256]{1,0:T(8,128)(2,1)S(1)}, u32[]{:S(2)}, u32[]{:S(2)}) collective-permute-start(bf16[128,256]{1,0:T(8,128)(2,1)S(1)} %add_convert_fusion), channel_id=1, source_target_pairs={{0,1},{1,0},{2,3},{3,2},{4,5},{5,4},{6,7},{7,6},{8,9},{9,8},{10,11... | collective-permute-start | bytes 196616 | tf_op jit(solution)/shard_map/weight_levels/ppermute | solution.py:30

commit v3 on v2

--- a/solution.py
+++ b/solution.py
@@ -10,11 +10,11 @@
 
 F32 = jnp.float32
 BF16 = jnp.bfloat16
-VMEM_LIMIT = 48 * 1024 * 1024
-
-
-def params():
-    return pltpu.CompilerParams(vmem_limit_bytes=VMEM_LIMIT)
+MIB = 1024 * 1024
+
+
+def params(tile_bytes=0):
+    return pltpu.CompilerParams(vmem_limit_bytes=(8 if tile_bytes <= MIB else 48) * MIB)
 
 
 def cost(flops, nbytes, transcendentals=0):
@@ -28,6 +28,25 @@
 def swap(value, axis, mask):
     size = lax.axis_size(axis)
     return lax.ppermute(value, axis, [(i, i ^ mask) for i in range(size)])
+
+
+def exchange(values, axis, unit):
+    out = list(values)
+    for m in reversed(range(1, len(values))):
+        out[m] = swap(values[m], axis, m * unit)
+    return out
+
+
+def far_first(count):
+    return list(reversed(range(count)))
+
+
+def ordered(values, order):
+    return [values[i] for i in order]
+
+
+def runs_of(order, size):
+    return [(order.index(i), 0, size) for i in range(len(order))]
 
 
 def tiled_dot(shape, store, lhs_rows, rhs_rows):
@@ -152,20 +171,21 @@
             pltpu.SMEM(cols.shape, jnp.int32),
             pltpu.SemaphoreType.DMA((7,)),
         ],
-        compiler_params=params(),
+        compiler_params=params(2 * row_blocks * block * nodes),
         cost_estimate=cost(4 * row_blocks * block * nodes * nodes, 2 * values.size),
         name="prep",
     )(count, *(pltpu.with_memory_space_constraint(x, pltpu.HBM) for x in (rows, cols, order, values, *passed)))
 
 
-def product_kernel(pieces, *refs):
-    matrix, parts, outs, joined = refs[0], refs[1 : 1 + pieces], refs[1 + pieces : -1], refs[-1]
-    run = parts[0].shape[0]
+def product_kernel(count, runs, *refs):
+    matrix, parts, outs, joined = refs[0], refs[1 : 1 + count], refs[1 + count : -1], refs[-1]
 
     @pl.when(pl.program_id(0) == 0)
     def _():
-        for i, part in enumerate(parts):
-            joined[i * run : (i + 1) * run, :] = part[...]
+        start = 0
+        for part, first, size in runs:
+            joined[start : start + size, :] = parts[part][first : first + size, :]
+            start += size
 
     total = lax.dot_general(matrix[...], joined[...], (((1,), (0,)), ((), ())), preferred_element_type=F32)
     start = 0
@@ -174,7 +194,7 @@
         start += out.shape[0]
 
 
-def product(matrix, parts, sizes, name):
+def product(matrix, parts, runs, sizes, name):
     rows, depth = matrix.shape
     width = parts[0].shape[1]
     step = min(rows, 1024)
@@ -185,13 +205,13 @@
         out_shape = [jax.ShapeDtypeStruct((rows, width), BF16)]
         out_specs = [pl.BlockSpec((step, width), lambda i: (i, 0))]
     outs = pl.pallas_call(
-        functools.partial(product_kernel, len(parts)),
+        functools.partial(product_kernel, len(parts), tuple(runs)),
         grid=(rows // step,),
         out_shape=out_shape,
         in_specs=[pl.BlockSpec((step, depth), lambda i: (i, 0))] + [whole(p.shape) for p in parts],
         out_specs=out_specs,
         scratch_shapes=[pltpu.VMEM((depth, width), BF16)],
-        compiler_params=params(),
+        compiler_params=params(2 * rows * depth),
         cost_estimate=cost(2 * rows * depth * width, 2 * (rows * depth + depth * width + rows * width)),
         name=name,
     )(matrix, *parts)
@@ -263,10 +283,11 @@
 
 
 def feature_kernel(terms, *refs):
+    weight, out = refs[terms:]
+    nodes = out.shape[0]
     total = refs[0][...].astype(F32)
     for ref in refs[1:terms]:
-        total = total + ref[...].astype(F32)
-    weight, out = refs[terms:]
+        total = total + ref[:nodes, :].astype(F32)
     out[...] = lax.dot_general(total.astype(BF16), weight[...], NT, preferred_element_type=F32).astype(BF16)
 
 
@@ -304,55 +325,62 @@
     block = block_values.shape[3]
     row_blocks = node_count * col_devices // block
 
+    row_masks = [1 << i for i in range((row_devices - 1).bit_length())]
+    level_masks = [2 << i for i in reversed(range((levels - 1).bit_length()))]
+    row_order, level_order = far_first(row_devices), far_first(levels)
     with jax.named_scope("gather_features"):
-        pieces = [features] + [swap(features, "row", m) for m in range(1, row_devices)]
+        pieces = exchange([features] * row_devices, "row", 1)
     tile, tile_turned, weight_near, bias_near, cotangent_near = prep(
         block_values[0, 0], block_rows, block_cols, counts, cluster_order, weight, bias_term, cotangent, row_blocks
     )
 
     with jax.named_scope("forward"):
-        own = [node_count] * levels
-        *kept, other = product(tile, pieces, own + [node_count * levels], "forward_tile")
+        *kept, other = product(
+            tile,
+            ordered(pieces, row_order),
+            runs_of(row_order, node_count),
+            [node_count] * levels + [node_count * levels],
+            "forward_tile",
+        )
         arrived = swap(other, "col", 1)
         pairs = [add(k, arrived[i * node_count : (i + 1) * node_count]) for i, k in enumerate(kept)]
-        terms = [pairs[0]] + [swap(pairs[m], "col", 2 * m) for m in range(1, levels)]
-        preact, slopes, weight_kept, weight_sent = slopes_of(terms, weight_near, bias_near, cotangent_near)
+        terms = exchange(pairs, "col", 2)
+        preact, slopes, weight_kept, weight_sent = slopes_of(
+            ordered(terms, level_order), weight_near, bias_near, cotangent_near
+        )
+    activations = activation(preact)
 
     with jax.named_scope("gather_slopes"):
-        slope_own = [slopes] + [swap(slopes, "col", 2 * m) for m in range(1, levels)]
-    activations = activation(preact)
+        slope_own = exchange([slopes] * levels, "col", 2)
 
     with jax.named_scope("weight_rows"):
         term = add(weight_kept, swap(weight_sent, "col", 1))
-        masks = [1 << i for i in range((row_devices - 1).bit_length())]
-        for mask in masks[:-1]:
-            term = add(term, swap(term, "row", mask))
-        last = swap(term, "row", masks[-1])
+        for mask in row_masks:
+            other = swap(term, "row", mask)
+            if mask == row_masks[-1]:
+                other, _ = lax.optimization_barrier((other, slope_own[1:]))
+            term = add(term, other)
 
     with jax.named_scope("backward"):
-        slope_half = jnp.concatenate(slope_own)
-        slope_half, last = lax.optimization_barrier((slope_half, last))
-        slope_other = swap(slope_half, "col", 1)
+        far = ordered(slope_own, level_order)
+        slope_other = swap(jnp.concatenate(far), "col", 1)
+        runs = runs_of(level_order, node_count)
         node_terms = product(
-            tile_turned, [slope_half, slope_other], [node_count] * row_devices, "backward_tile"
-        )
+            tile_turned,
+            far + [slope_other],
+            runs + [(levels, part * node_count, node_count) for part, _, _ in runs],
+            [node_count] * row_devices,
+            "backward_tile",
+        )
+        node_sum = exchange(node_terms, "row", 1)
+        grad_features = feature_gradient(ordered(node_sum, row_order), weight_near)
 
     with jax.named_scope("weight_levels"):
-        term = add(term, last)
-        masks = [2 << i for i in range((levels - 1).bit_length())]
-        for mask in masks[:-1]:
+        for mask in level_masks:
             other = swap(term, "col", mask)
-            if mask == 2:
-                other, node_terms[0] = lax.optimization_barrier((other, node_terms[0]))
+            if mask == level_masks[-1]:
+                other, _ = lax.optimization_barrier((other, grad_features))
             term = add(term, other)
-        last = swap(term, "col", masks[-1])
-
-    with jax.named_scope("backward"):
-        node_sum = [node_terms[0]] + [swap(node_terms[m], "row", m) for m in range(1, row_devices)]
-        grad_features = feature_gradient(node_sum, weight_near)
-
-    with jax.named_scope("weight_levels"):
-        term = add(term, last)
         partner = swap(term, "col", 1)
         core = lax.axis_index("col") & 1
         scale = 1.0 / math.sqrt(node_count * row_devices * col_devices)

time: 49.6 us -> 46.1 us (0.929)
  waiting for transfers between devices: 21.4 us -> 17.5 us
    ppermute x20, waiting for transfers between devices: 21.4 us -> 17.5 us  [swap(): return lax.ppermute(value, axis, [(i, i ^ mask) for i in range(size)])]
  transfers between devices with their start and end apart: 20 -> 20, of which waited for: 13 -> 15; matrix products, arithmetic and copies ran while one was open for 0% -> 0% of each run, Pallas kernels for 9% -> 10%
where the time goes in v3:
time: 46.1 us; the launch traced here: 45.9 us
  starting transfers between devices  20.6 us (45%)
  waiting for transfers between devices  17.5 us (38%)
  Pallas kernels  5.42 us (12%)
  between operations  1.42 us (3%)
  other arithmetic  0.91 us (2%)
    ppermute x20, starting transfers between devices, swap(): return lax.ppermute(value, axis, [(i, i ^ mask) for i in range(size)])  20.6 us
    ppermute x20, waiting for transfers between devices, swap(): return lax.ppermute(value, axis, [(i, i ^ mask) for i in range(size)])  17.5 us
    pallas_call x1, Pallas kernels, prep(): pl.pallas_call(functools.partial(prep_kernel, per_step), grid=(row_blocks...  2.56 us
  transfers between devices with their start and end apart: 20, of which 15 were waited for; matrix products, arithmetic and copies ran while one was open for 0% of the time, Pallas kernels for 10%

profile of v3, /device:TPU:0, one launch (start us, length us, event | category | flops | bytes accessed | tf_op | source)
XLA Modules:
  0.0 45.9 jit_solution(1507679663535785451)
XLA Ops:
  0.6 4.0 %collective-permute-start = (bf16[128,256]{1,0:T(8,128)(2,1)}, bf16[128,256]{1,0:T(8,128)(2,1)S(1)}, u32[]{:S(2)}, u32[]{:S(2)}) collective-permute-start(bf16[128,256]{1,0:T(8,128)(2,1)} %refs_4_.1), channel_id=1, source_target_pairs={{0,24},{8,16},{16,8},{24,0},{1,25},{9,17},{17,9},{25,1},{2,26},{10... | collective-permute-start | bytes 196616 | tf_op jit(solution)/shard_map/gather_features/ppermute | solution.py:30
  5.9 2.6 %prep.1 = (bf16[1024,512]{1,0:T(8,128)(2,1)S(1)}, bf16[512,1024]{1,0:T(8,128)(2,1)S(1)}, bf16[256,256]{1,0:T(8,128)(2,1)S(1)}, f32[1,256]{1,0:T(1,128)S(1)}, bf16[128,256]{1,0:T(8,128)(2,1)S(1)}) custom-call(s32[1,1]{1,0:T(1,128)S(6)} %copy.12.count, s32[1,1,16]{2,1,0:T(1,128)} %rows_hbm.1, s32[1,1,16]{2,1,0:T(1,128)} %cols_hbm.1, s32[4,128]{1,0:T(4,128)} %bitcast.4, ...), custom_call_target="tpu_custom_call" | custom-call | flops 1073741824 | bytes 524288 | tf_op jit(solution)/shard_map/prep/pallas_call | solution.py:151
  10.1 1.5 %collective-permute-done.3 = bf16[512,256]{1,0:T(8,128)(2,1)S(1)} collective-permute-done((bf16[512,256]{1,0:T(8,128)(2,1)S(1)}, bf16[512,256]{1,0:T(8,128)(2,1)S(1)}, u32[]{:S(2)}, u32[]{:S(2)}) %collective-permute-start.3) | collective-permute-done | bytes 262176 | tf_op jit(solution)/shard_map/forward/ppermute | solution.py:30
  11.7 3.7 %collective-permute-start.4 = (bf16[128,256]{1,0:T(8,128)(2,1)S(1)}, bf16[128,256]{1,0:T(8,128)(2,1)S(1)}, u32[]{:S(2)}, u32[]{:S(2)}) collective-permute-start(bf16[128,256]{1,0:T(8,128)(2,1)S(1)} %get-tuple-element.46), channel_id=1, source_target_pairs={{0,6},{1,7},{2,4},{3,5},{4,2},{5,3},{6,0},{7,1},{8,14},{9,15},{10,... | collective-permute-start | bytes 196616 | tf_op jit(solution)/shard_map/forward/ppermute | solution.py:30
  15.4 0.8 %collective-permute-start.6 = (bf16[128,256]{1,0:T(8,128)(2,1)S(1)}, bf16[128,256]{1,0:T(8,128)(2,1)S(1)}, u32[]{:S(2)}, u32[]{:S(2)}) collective-permute-start(bf16[128,256]{1,0:T(8,128)(2,1)S(1)} %get-tuple-element.44), channel_id=1, source_target_pairs={{0,2},{1,3},{2,0},{3,1},{4,6},{5,7},{6,4},{7,5},{8,10},{9,11},{10,... | collective-permute-start | bytes 196616 | tf_op jit(solution)/shard_map/forward/ppermute | solution.py:30
  16.1 1.9 %collective-permute-done.4.refs_0_ = bf16[128,256]{1,0:T(8,128)(2,1)S(1)} collective-permute-done((bf16[128,256]{1,0:T(8,128)(2,1)S(1)}, bf16[128,256]{1,0:T(8,128)(2,1)S(1)}, u32[]{:S(2)}, u32[]{:S(2)}) %collective-permute-start.4) | collective-permute-done | bytes 65568 | tf_op jit(solution)/shard_map/forward/ppermute | solution.py:30
  18.1 3.2 %collective-permute-done.5.refs_1_ = bf16[128,256]{1,0:T(8,128)(2,1)S(1)} collective-permute-done((bf16[128,256]{1,0:T(8,128)(2,1)S(1)}, bf16[128,256]{1,0:T(8,128)(2,1)S(1)}, u32[]{:S(2)}, u32[]{:S(2)}) %collective-permute-start.5) | collective-permute-done | bytes 65568 | tf_op jit(solution)/shard_map/forward/ppermute | solution.py:30
  21.8 1.2 %collective-permute-done.14 = bf16[128,256]{1,0:T(8,128)(2,1)S(1)} collective-permute-done((bf16[128,256]{1,0:T(8,128)(2,1)S(1)}, bf16[128,256]{1,0:T(8,128)(2,1)S(1)}, u32[]{:S(2)}, u32[]{:S(2)}) %collective-permute-start.14) | collective-permute-done | bytes 65568 | tf_op jit(solution)/shard_map/weight_rows/ppermute | solution.py:30
  23.1 1.0 %collective-permute-start.15 = (bf16[128,256]{1,0:T(8,128)(2,1)S(1)}, bf16[128,256]{1,0:T(8,128)(2,1)S(1)}, u32[]{:S(2)}, u32[]{:S(2)}) collective-permute-start(bf16[128,256]{1,0:T(8,128)(2,1)S(1)} %add_convert_fusion.4), channel_id=1, source_target_pairs={{0,8},{8,0},{16,24},{24,16},{1,9},{9,1},{17,25},{25,17},{2,10},{10... | collective-permute-start | bytes 196616 | tf_op jit(solution)/shard_map/weight_rows/ppermute | solution.py:30
  24.1 2.3 %collective-permute-start.7 = (bf16[128,256]{1,0:T(8,128)(2,1)S(1)}, bf16[128,256]{1,0:T(8,128)(2,1)S(1)}, u32[]{:S(2)}, u32[]{:S(2)}) collective-permute-start(bf16[128,256]{1,0:T(8,128)(2,1)S(1)} %get-tuple-element.34.refs_4_), channel_id=1, source_target_pairs={{0,6},{1,7},{2,4},{3,5},{4,2},{5,3},{6,0},{7,1},{8,14},{9,15},{10,... | collective-permute-start | bytes 196616 | tf_op jit(solution)/shard_map/gather_slopes/ppermute | solution.py:30
  26.6 1.8 %collective-permute-start.9 = (bf16[128,256]{1,0:T(8,128)(2,1)S(1)}, bf16[128,256]{1,0:T(8,128)(2,1)S(1)}, u32[]{:S(2)}, u32[]{:S(2)}) collective-permute-start(bf16[128,256]{1,0:T(8,128)(2,1)S(1)} %get-tuple-element.34.refs_4_), channel_id=1, source_target_pairs={{0,2},{1,3},{2,0},{3,1},{4,6},{5,7},{6,4},{7,5},{8,10},{9,11},{10,... | collective-permute-start | bytes 196616 | tf_op jit(solution)/shard_map/gather_slopes/ppermute | solution.py:30
  28.5 1.5 %collective-permute-start.16 = (bf16[128,256]{1,0:T(8,128)(2,1)S(1)}, bf16[128,256]{1,0:T(8,128)(2,1)S(1)}, u32[]{:S(2)}, u32[]{:S(2)}) collective-permute-start(bf16[128,256]{1,0:T(8,128)(2,1)S(1)} %add_convert_fusion.3), channel_id=1, source_target_pairs={{0,16},{8,24},{16,0},{24,8},{1,17},{9,25},{17,1},{25,9},{2,18},{10... | collective-permute-start | bytes 196616 | tf_op jit(solution)/shard_map/weight_rows/ppermute | solution.py:30
  29.9 0.6 %collective-permute-done.7.refs_1_ = bf16[128,256]{1,0:T(8,128)(2,1)S(1)} collective-permute-done((bf16[128,256]{1,0:T(8,128)(2,1)S(1)}, bf16[128,256]{1,0:T(8,128)(2,1)S(1)}, u32[]{:S(2)}, u32[]{:S(2)}) %collective-permute-start.7) | collective-permute-done | bytes 65568 | tf_op jit(solution)/shard_map/gather_slopes/ppermute | solution.py:30
  30.6 2.5 %collective-permute-done.8.refs_2_ = bf16[128,256]{1,0:T(8,128)(2,1)S(1)} collective-permute-done((bf16[128,256]{1,0:T(8,128)(2,1)S(1)}, bf16[128,256]{1,0:T(8,128)(2,1)S(1)}, u32[]{:S(2)}, u32[]{:S(2)}) %collective-permute-start.8) | collective-permute-done | bytes 65568 | tf_op jit(solution)/shard_map/gather_slopes/ppermute | solution.py:30
  33.7 0.9 %collective-permute-done.10.refs_5_ = bf16[512,256]{1,0:T(8,128)(2,1)S(1)} collective-permute-done((bf16[512,256]{1,0:T(8,128)(2,1)S(1)}, bf16[512,256]{1,0:T(8,128)(2,1)S(1)}, u32[]{:S(2)}, u32[]{:S(2)}) %collective-permute-start.10) | collective-permute-done | bytes 262176 | tf_op jit(solution)/shard_map/backward/ppermute | solution.py:30
  35.1 2.1 %collective-permute-start.11 = (bf16[128,256]{1,0:T(8,128)(2,1)S(1)}, bf16[128,256]{1,0:T(8,128)(2,1)S(1)}, u32[]{:S(2)}, u32[]{:S(2)}) collective-permute-start(bf16[128,256]{1,0:T(8,128)(2,1)S(1)} %get-tuple-element.35), channel_id=1, source_target_pairs={{0,24},{8,16},{16,8},{24,0},{1,25},{9,17},{17,9},{25,1},{2,26},{10... | collective-permute-start | bytes 196616 | tf_op jit(solution)/shard_map/backward/ppermute | solution.py:30
  37.8 0.9 %collective-permute-start.13 = (bf16[128,256]{1,0:T(8,128)(2,1)S(1)}, bf16[128,256]{1,0:T(8,128)(2,1)S(1)}, u32[]{:S(2)}, u32[]{:S(2)}) collective-permute-start(bf16[128,256]{1,0:T(8,128)(2,1)S(1)} %get-tuple-element.37), channel_id=1, source_target_pairs={{0,8},{8,0},{16,24},{24,16},{1,9},{9,1},{17,25},{25,17},{2,10},{10... | collective-permute-start | bytes 196616 | tf_op jit(solution)/shard_map/backward/ppermute | solution.py:30
  38.7 0.8 %collective-permute-done.17 = bf16[128,256]{1,0:T(8,128)(2,1)S(1)} collective-permute-done((bf16[128,256]{1,0:T(8,128)(2,1)S(1)}, bf16[128,256]{1,0:T(8,128)(2,1)S(1)}, u32[]{:S(2)}, u32[]{:S(2)}) %collective-permute-start.17) | collective-permute-done | bytes 65568 | tf_op jit(solution)/shard_map/weight_levels/ppermute | solution.py:30
  39.8 0.6 %collective-permute-done.11.refs_0_ = bf16[128,256]{1,0:T(8,128)(2,1)S(1)} collective-permute-done((bf16[128,256]{1,0:T(8,128)(2,1)S(1)}, bf16[128,256]{1,0:T(8,128)(2,1)S(1)}, u32[]{:S(2)}, u32[]{:S(2)}) %collective-permute-start.11) | collective-permute-done | bytes 65568 | tf_op jit(solution)/shard_map/backward/ppermute | solution.py:30
  40.4 1.3 %collective-permute-done.12.refs_1_ = bf16[128,256]{1,0:T(8,128)(2,1)S(1)} collective-permute-done((bf16[128,256]{1,0:T(8,128)(2,1)S(1)}, bf16[128,256]{1,0:T(8,128)(2,1)S(1)}, u32[]{:S(2)}, u32[]{:S(2)}) %collective-permute-start.12) | collective-permute-done | bytes 65568 | tf_op jit(solution)/shard_map/backward/ppermute | solution.py:30
  42.0 0.8 %feature_gradient.1 = bf16[128,256]{1,0:T(8,128)(2,1)} custom-call(bf16[128,256]{1,0:T(8,128)(2,1)S(1)} %collective-permute-done.11.refs_0_, bf16[128,256]{1,0:T(8,128)(2,1)S(1)} %collective-permute-done.12.refs_1_, bf16[128,256]{1,0:T(8,128)(2,1)S(1)} %collective-permute-done.13.refs_2_, bf16[128,256]{1,0:T(8,128)(2,1)S(1)} %get-tuple-element.38.refs_3_, ...), custom_call_target="tpu_custom_call" | custom-call | flops 16777216 | bytes 393216 | tf_op jit(solution)/shard_map/backward/feature_gradient/pallas_call | solution.py:297
  42.9 0.9 %collective-permute-done.18 = bf16[128,256]{1,0:T(8,128)(2,1)S(1)} collective-permute-done((bf16[128,256]{1,0:T(8,128)(2,1)S(1)}, bf16[128,256]{1,0:T(8,128)(2,1)S(1)}, u32[]{:S(2)}, u32[]{:S(2)}) %collective-permute-start.18) | collective-permute-done | bytes 65568 | tf_op jit(solution)/shard_map/weight_levels/ppermute | solution.py:30
  43.9 0.7 %activation.1 = bf16[128,256]{1,0:T(8,128)(2,1)} custom-call(f32[128,256]{1,0:T(8,128)S(1)} %get-tuple-element.32.preact_ref), custom_call_target="tpu_custom_call" | custom-call | flops 131072 | bytes 196608 | tf_op jit(solution)/shard_map/activation/pallas_call | solution.py:276
  45.1 0.7 %convert_multiply_fusion = f32[256,256]{1,0:T(8,128)} fusion(bf16[128,256]{1,0:T(8,128)(2,1)S(1)} %collective-permute-done.19, bf16[128,256]{1,0:T(8,128)(2,1)S(1)} %add_convert_fusion, pred[]{:T(512)S(6)} %eq.3), kind=kLoop, calls=%fused_computation.1 | loop fusion | flops 720896 | bytes 393217 | tf_op jit(solution)/shard_map/weight_levels/mul | solution.py:390
  (32 shorter events, 6.1 us)
Async XLA Ops:
  0.6 7.8 %collective-permute-start = (bf16[128,256]{1,0:T(8,128)(2,1)}, bf16[128,256]{1,0:T(8,128)(2,1)S(1)}, u32[]{:S(2)}, u32[]{:S(2)}) collective-permute-start(bf16[128,256]{1,0:T(8,128)(2,1)} %refs_4_.1), channel_id=1, source_target_pairs={{0,24},{8,16},{16,8},{24,0},{1,25},{9,17},{17,9},{25,1},{2,26},{10... | collective-permute-start | bytes 196616 | tf_op jit(solution)/shard_map/gather_features/ppermute | solution.py:30
  4.6 4.5 %collective-permute-start.1 = (bf16[128,256]{1,0:T(8,128)(2,1)}, bf16[128,256]{1,0:T(8,128)(2,1)S(1)}, u32[]{:S(2)}, u32[]{:S(2)}) collective-permute-start(bf16[128,256]{1,0:T(8,128)(2,1)} %refs_4_.1), channel_id=1, source_target_pairs={{0,16},{8,24},{16,0},{24,8},{1,17},{9,25},{17,1},{25,9},{2,18},{10... | collective-permute-start | bytes 196616 | tf_op jit(solution)/shard_map/gather_features/ppermute | solution.py:30
  5.1 4.5 %collective-permute-start.2 = (bf16[128,256]{1,0:T(8,128)(2,1)}, bf16[128,256]{1,0:T(8,128)(2,1)S(1)}, u32[]{:S(2)}, u32[]{:S(2)}) collective-permute-start(bf16[128,256]{1,0:T(8,128)(2,1)} %refs_4_.1), channel_id=1, source_target_pairs={{0,8},{8,0},{16,24},{24,16},{1,9},{9,1},{17,25},{25,17},{2,10},{10... | collective-permute-start | bytes 196616 | tf_op jit(solution)/shard_map/gather_features/ppermute | solution.py:30
  5.9 3.7 %copy-start = (bf16[128,256]{1,0:T(8,128)(2,1)S(1)}, bf16[128,256]{1,0:T(8,128)(2,1)}, u32[]{:S(2)}) copy-start(bf16[128,256]{1,0:T(8,128)(2,1)} %refs_4_.1) | copy-start | bytes 196612
  10.0 1.6 %collective-permute-start.3 = (bf16[512,256]{1,0:T(8,128)(2,1)S(1)}, bf16[512,256]{1,0:T(8,128)(2,1)S(1)}, u32[]{:S(2)}, u32[]{:S(2)}) collective-permute-start(bf16[512,256]{1,0:T(8,128)(2,1)S(1)} %get-tuple-element.25), channel_id=1, source_target_pairs={{0,1},{1,0},{2,3},{3,2},{4,5},{5,4},{6,7},{7,6},{8,9},{9,8},{10,11... | collective-permute-start | bytes 786440 | tf_op jit(solution)/shard_map/forward/ppermute | solution.py:30
  11.7 6.4 %collective-permute-start.4 = (bf16[128,256]{1,0:T(8,128)(2,1)S(1)}, bf16[128,256]{1,0:T(8,128)(2,1)S(1)}, u32[]{:S(2)}, u32[]{:S(2)}) collective-permute-start(bf16[128,256]{1,0:T(8,128)(2,1)S(1)} %get-tuple-element.46), channel_id=1, source_target_pairs={{0,6},{1,7},{2,4},{3,5},{4,2},{5,3},{6,0},{7,1},{8,14},{9,15},{10,... | collective-permute-start | bytes 196616 | tf_op jit(solution)/shard_map/forward/ppermute | solution.py:30
  15.4 5.9 %collective-permute-start.5 = (bf16[128,256]{1,0:T(8,128)(2,1)S(1)}, bf16[128,256]{1,0:T(8,128)(2,1)S(1)}, u32[]{:S(2)}, u32[]{:S(2)}) collective-permute-start(bf16[128,256]{1,0:T(8,128)(2,1)S(1)} %get-tuple-element.45), channel_id=1, source_target_pairs={{0,4},{1,5},{2,6},{3,7},{4,0},{5,1},{6,2},{7,3},{8,12},{9,13},{10,... | collective-permute-start | bytes 196616 | tf_op jit(solution)/shard_map/forward/ppermute | solution.py:30
  15.4 5.9 %collective-permute-start.6 = (bf16[128,256]{1,0:T(8,128)(2,1)S(1)}, bf16[128,256]{1,0:T(8,128)(2,1)S(1)}, u32[]{:S(2)}, u32[]{:S(2)}) collective-permute-start(bf16[128,256]{1,0:T(8,128)(2,1)S(1)} %get-tuple-element.44), channel_id=1, source_target_pairs={{0,2},{1,3},{2,0},{3,1},{4,6},{5,7},{6,4},{7,5},{8,10},{9,11},{10,... | collective-permute-start | bytes 196616 | tf_op jit(solution)/shard_map/forward/ppermute | solution.py:30
  21.7 1.3 %collective-permute-start.14 = (bf16[128,256]{1,0:T(8,128)(2,1)S(1)}, bf16[128,256]{1,0:T(8,128)(2,1)S(1)}, u32[]{:S(2)}, u32[]{:S(2)}) collective-permute-start(bf16[128,256]{1,0:T(8,128)(2,1)S(1)} %get-tuple-element.40), channel_id=1, source_target_pairs={{0,1},{1,0},{2,3},{3,2},{4,5},{5,4},{6,7},{7,6},{8,9},{9,8},{10,11... | collective-permute-start | bytes 196616 | tf_op jit(solution)/shard_map/weight_rows/ppermute | solution.py:30
  23.1 5.4 %collective-permute-start.15 = (bf16[128,256]{1,0:T(8,128)(2,1)S(1)}, bf16[128,256]{1,0:T(8,128)(2,1)S(1)}, u32[]{:S(2)}, u32[]{:S(2)}) collective-permute-start(bf16[128,256]{1,0:T(8,128)(2,1)S(1)} %add_convert_fusion.4), channel_id=1, source_target_pairs={{0,8},{8,0},{16,24},{24,16},{1,9},{9,1},{17,25},{25,17},{2,10},{10... | collective-permute-start | bytes 196616 | tf_op jit(solution)/shard_map/weight_rows/ppermute | solution.py:30
  24.1 6.5 %collective-permute-start.7 = (bf16[128,256]{1,0:T(8,128)(2,1)S(1)}, bf16[128,256]{1,0:T(8,128)(2,1)S(1)}, u32[]{:S(2)}, u32[]{:S(2)}) collective-permute-start(bf16[128,256]{1,0:T(8,128)(2,1)S(1)} %get-tuple-element.34.refs_4_), channel_id=1, source_target_pairs={{0,6},{1,7},{2,4},{3,5},{4,2},{5,3},{6,0},{7,1},{8,14},{9,15},{10,... | collective-permute-start | bytes 196616 | tf_op jit(solution)/shard_map/gather_slopes/ppermute | solution.py:30
  26.3 6.7 %collective-permute-start.8 = (bf16[128,256]{1,0:T(8,128)(2,1)S(1)}, bf16[128,256]{1,0:T(8,128)(2,1)S(1)}, u32[]{:S(2)}, u32[]{:S(2)}) collective-permute-start(bf16[128,256]{1,0:T(8,128)(2,1)S(1)} %get-tuple-element.34.refs_4_), channel_id=1, source_target_pairs={{0,4},{1,5},{2,6},{3,7},{4,0},{5,1},{6,2},{7,3},{8,12},{9,13},{10,... | collective-permute-start | bytes 196616 | tf_op jit(solution)/shard_map/gather_slopes/ppermute | solution.py:30
  26.6 6.5 %collective-permute-start.9 = (bf16[128,256]{1,0:T(8,128)(2,1)S(1)}, bf16[128,256]{1,0:T(8,128)(2,1)S(1)}, u32[]{:S(2)}, u32[]{:S(2)}) collective-permute-start(bf16[128,256]{1,0:T(8,128)(2,1)S(1)} %get-tuple-element.34.refs_4_), channel_id=1, source_target_pairs={{0,2},{1,3},{2,0},{3,1},{4,6},{5,7},{6,4},{7,5},{8,10},{9,11},{10,... | collective-permute-start | bytes 196616 | tf_op jit(solution)/shard_map/gather_slopes/ppermute | solution.py:30
  28.5 4.7 %collective-permute-start.16 = (bf16[128,256]{1,0:T(8,128)(2,1)S(1)}, bf16[128,256]{1,0:T(8,128)(2,1)S(1)}, u32[]{:S(2)}, u32[]{:S(2)}) collective-permute-start(bf16[128,256]{1,0:T(8,128)(2,1)S(1)} %add_convert_fusion.3), channel_id=1, source_target_pairs={{0,16},{8,24},{16,0},{24,8},{1,17},{9,25},{17,1},{25,9},{2,18},{10... | collective-permute-start | bytes 196616 | tf_op jit(solution)/shard_map/weight_rows/ppermute | solution.py:30
  33.1 1.6 %collective-permute-start.10 = (bf16[512,256]{1,0:T(8,128)(2,1)S(1)}, bf16[512,256]{1,0:T(8,128)(2,1)S(1)}, u32[]{:S(2)}, u32[]{:S(2)}) collective-permute-start(bf16[512,256]{1,0:T(8,128)(2,1)S(1)} %pad_maximum_fusion), channel_id=1, source_target_pairs={{0,1},{1,0},{2,3},{3,2},{4,5},{5,4},{6,7},{7,6},{8,9},{9,8},{10,11... | collective-permute-start | bytes 786440 | tf_op jit(solution)/shard_map/backward/ppermute | solution.py:30
  33.2 6.3 %collective-permute-start.17 = (bf16[128,256]{1,0:T(8,128)(2,1)S(1)}, bf16[128,256]{1,0:T(8,128)(2,1)S(1)}, u32[]{:S(2)}, u32[]{:S(2)}) collective-permute-start(bf16[128,256]{1,0:T(8,128)(2,1)S(1)} %add_convert_fusion.2), channel_id=1, source_target_pairs={{0,4},{1,5},{2,6},{3,7},{4,0},{5,1},{6,2},{7,3},{8,12},{9,13},{10,... | collective-permute-start | bytes 196616 | tf_op jit(solution)/shard_map/weight_levels/ppermute | solution.py:30
  35.1 5.3 %collective-permute-start.11 = (bf16[128,256]{1,0:T(8,128)(2,1)S(1)}, bf16[128,256]{1,0:T(8,128)(2,1)S(1)}, u32[]{:S(2)}, u32[]{:S(2)}) collective-permute-start(bf16[128,256]{1,0:T(8,128)(2,1)S(1)} %get-tuple-element.35), channel_id=1, source_target_pairs={{0,24},{8,16},{16,8},{24,0},{1,25},{9,17},{17,9},{25,1},{2,26},{10... | collective-permute-start | bytes 196616 | tf_op jit(solution)/shard_map/backward/ppermute | solution.py:30
  37.3 4.5 %collective-permute-start.12 = (bf16[128,256]{1,0:T(8,128)(2,1)S(1)}, bf16[128,256]{1,0:T(8,128)(2,1)S(1)}, u32[]{:S(2)}, u32[]{:S(2)}) collective-permute-start(bf16[128,256]{1,0:T(8,128)(2,1)S(1)} %get-tuple-element.36), channel_id=1, source_target_pairs={{0,16},{8,24},{16,0},{24,8},{1,17},{9,25},{17,1},{25,9},{2,18},{10... | collective-permute-start | bytes 196616 | tf_op jit(solution)/shard_map/backward/ppermute | solution.py:30
  37.8 4.3 %collective-permute-start.13 = (bf16[128,256]{1,0:T(8,128)(2,1)S(1)}, bf16[128,256]{1,0:T(8,128)(2,1)S(1)}, u32[]{:S(2)}, u32[]{:S(2)}) collective-permute-start(bf16[128,256]{1,0:T(8,128)(2,1)S(1)} %get-tuple-element.37), channel_id=1, source_target_pairs={{0,8},{8,0},{16,24},{24,16},{1,9},{9,1},{17,25},{25,17},{2,10},{10... | collective-permute-start | bytes 196616 | tf_op jit(solution)/shard_map/backward/ppermute | solution.py:30
  39.5 4.3 %collective-permute-start.18 = (bf16[128,256]{1,0:T(8,128)(2,1)S(1)}, bf16[128,256]{1,0:T(8,128)(2,1)S(1)}, u32[]{:S(2)}, u32[]{:S(2)}) collective-permute-start(bf16[128,256]{1,0:T(8,128)(2,1)S(1)} %add_convert_fusion.1), channel_id=1, source_target_pairs={{0,2},{1,3},{2,0},{3,1},{4,6},{5,7},{6,4},{7,5},{8,10},{9,11},{10,... | collective-permute-start | bytes 196616 | tf_op jit(solution)/shard_map/weight_levels/ppermute | solution.py:30
  43.8 1.3 %collective-permute-start.19 = (bf16[128,256]{1,0:T(8,128)(2,1)S(1)}, bf16[128,256]{1,0:T(8,128)(2,1)S(1)}, u32[]{:S(2)}, u32[]{:S(2)}) collective-permute-start(bf16[128,256]{1,0:T(8,128)(2,1)S(1)} %add_convert_fusion), channel_id=1, source_target_pairs={{0,1},{1,0},{2,3},{3,2},{4,5},{5,4},{6,7},{7,6},{8,9},{9,8},{10,11... | collective-permute-start | bytes 196616 | tf_op jit(solution)/shard_map/weight_levels/ppermute | solution.py:30

commit v4 on v3

--- a/solution.py
+++ b/solution.py
@@ -177,7 +177,7 @@
     )(count, *(pltpu.with_memory_space_constraint(x, pltpu.HBM) for x in (rows, cols, order, values, *passed)))
 
 
-def product_kernel(count, runs, *refs):
+def product_kernel(count, runs, top, *refs):
     matrix, parts, outs, joined = refs[0], refs[1 : 1 + count], refs[1 + count : -1], refs[-1]
 
     @pl.when(pl.program_id(0) == 0)
@@ -187,35 +187,42 @@
             joined[start : start + size, :] = parts[part][first : first + size, :]
             start += size
 
-    total = lax.dot_general(matrix[...], joined[...], (((1,), (0,)), ((), ())), preferred_element_type=F32)
+    rows = sum(out.shape[0] for out in outs)
+    total = lax.dot_general(
+        matrix[top : top + rows, :], joined[...], (((1,), (0,)), ((), ())), preferred_element_type=F32
+    )
     start = 0
     for out in outs:
         out[...] = total[start : start + out.shape[0]].astype(out.dtype)
         start += out.shape[0]
 
 
-def product(matrix, parts, runs, sizes, name):
-    rows, depth = matrix.shape
+def product(matrix, parts, runs, sizes, name, top=0):
+    rows, depth = sum(sizes), matrix.shape[1]
     width = parts[0].shape[1]
-    step = min(rows, 1024)
-    if step == rows:
+    small = matrix.size <= MIB
+    if small:
+        step = rows
+        matrix_spec = whole(matrix.shape)
         out_shape = [jax.ShapeDtypeStruct((n, width), BF16) for n in sizes]
         out_specs = [whole((n, width)) for n in sizes]
     else:
+        step = math.gcd(math.gcd(rows, top), 1024)
+        matrix_spec = pl.BlockSpec((step, depth), lambda i: (top // step + i, 0))
         out_shape = [jax.ShapeDtypeStruct((rows, width), BF16)]
         out_specs = [pl.BlockSpec((step, width), lambda i: (i, 0))]
     outs = pl.pallas_call(
-        functools.partial(product_kernel, len(parts), tuple(runs)),
+        functools.partial(product_kernel, len(parts), tuple(runs), top if small else 0),
         grid=(rows // step,),
         out_shape=out_shape,
-        in_specs=[pl.BlockSpec((step, depth), lambda i: (i, 0))] + [whole(p.shape) for p in parts],
+        in_specs=[matrix_spec] + [whole(p.shape) for p in parts],
         out_specs=out_specs,
         scratch_shapes=[pltpu.VMEM((depth, width), BF16)],
-        compiler_params=params(2 * rows * depth),
+        compiler_params=params(2 * matrix.size),
         cost_estimate=cost(2 * rows * depth * width, 2 * (rows * depth + depth * width + rows * width)),
         name=name,
     )(matrix, *parts)
-    if step == rows:
+    if small:
         return list(outs)
     cuts, start = [], 0
     for n in sizes:
@@ -335,15 +342,14 @@
     )
 
     with jax.named_scope("forward"):
-        *kept, other = product(
-            tile,
-            ordered(pieces, row_order),
-            runs_of(row_order, node_count),
-            [node_count] * levels + [node_count * levels],
-            "forward_tile",
-        )
-        arrived = swap(other, "col", 1)
-        pairs = [add(k, arrived[i * node_count : (i + 1) * node_count]) for i, k in enumerate(kept)]
+        far, runs = ordered(pieces, row_order), runs_of(row_order, node_count)
+        near = levels // 2
+        (other_far,) = product(tile, far, runs, [node_count * (levels - near)], "forward_far", node_count * (levels + near))
+        *kept, other_near = product(tile, far, runs, [node_count] * levels + [node_count * near], "forward_near")
+        pairs = []
+        for group, sent in ((kept[:near], other_near), (kept[near:], other_far)):
+            arrived = swap(sent, "col", 1)
+            pairs += [add(k, arrived[i * node_count : (i + 1) * node_count]) for i, k in enumerate(group)]
         terms = exchange(pairs, "col", 2)
         preact, slopes, weight_kept, weight_sent = slopes_of(
             ordered(terms, level_order), weight_near, bias_near, cotangent_near
@@ -376,12 +382,11 @@
         grad_features = feature_gradient(ordered(node_sum, row_order), weight_near)
 
     with jax.named_scope("weight_levels"):
-        for mask in level_masks:
-            other = swap(term, "col", mask)
-            if mask == level_masks[-1]:
-                other, _ = lax.optimization_barrier((other, grad_features))
-            term = add(term, other)
-        partner = swap(term, "col", 1)
+        for mask in level_masks[:-1]:
+            term = add(term, swap(term, "col", mask))
+        others = [swap(term, "col", mask) for mask in (level_masks[-1], level_masks[-1] | 1, 1)]
+        others, _ = lax.optimization_barrier((others, grad_features))
+        term, partner = add(term, others[0]), add(others[1], others[2])
         core = lax.axis_index("col") & 1
         scale = 1.0 / math.sqrt(node_count * row_devices * col_devices)
         both = jnp.where(

time: 46.1 us -> 44.9 us (0.974)
  waiting for transfers between devices: 17.5 us -> 13.5 us
  starting transfers between devices: 20.6 us -> 23.4 us
    ppermute x20 -> x22, waiting for transfers between devices: 17.5 us -> 13.5 us  [swap(): return lax.ppermute(value, axis, [(i, i ^ mask) for i in range(size)])]
    ppermute x20 -> x22, starting transfers between devices: 20.6 us -> 23.4 us  [swap(): return lax.ppermute(value, axis, [(i, i ^ mask) for i in range(size)])]
    pallas_call x2 -> x3, Pallas kernels: 0.87 us -> 1.03 us  [product(): pl.pallas_call(functools.partial(product_kernel, len(parts), tuple(runs),...]
  transfers between devices with their start and end apart: 20 -> 22, of which waited for: 15 -> 11; matrix products, arithmetic and copies ran while one was open for 0% -> 0% of each run, Pallas kernels for 10% -> 11%
where the time goes in v4:
time: 44.9 us; the launch traced here: 44.7 us
  starting transfers between devices  23.4 us (52%)
  waiting for transfers between devices  13.5 us (30%)
  Pallas kernels  5.48 us (12%)
  between operations  1.43 us (3%)
  other arithmetic  0.93 us (2%)
    ppermute x22, starting transfers between devices, swap(): return lax.ppermute(value, axis, [(i, i ^ mask) for i in range(size)])  23.4 us
    ppermute x22, waiting for transfers between devices, swap(): return lax.ppermute(value, axis, [(i, i ^ mask) for i in range(size)])  13.5 us
    pallas_call x1, Pallas kernels, prep(): pl.pallas_call(functools.partial(prep_kernel, per_step), grid=(row_blocks...  2.47 us
    pallas_call x3, Pallas kernels, product(): pl.pallas_call(functools.partial(product_kernel, len(parts), tuple(runs),...  1.03 us
  transfers between devices with their start and end apart: 22, of which 11 were waited for; matrix products, arithmetic and copies ran while one was open for 0% of the time, Pallas kernels for 11%

profile of v4, /device:TPU:0, one launch (start us, length us, event | category | flops | bytes accessed | tf_op | source)
XLA Modules:
  0.0 44.7 jit_solution(3339680470113925115)
XLA Ops:
  0.6 4.0 %collective-permute-start = (bf16[128,256]{1,0:T(8,128)(2,1)}, bf16[128,256]{1,0:T(8,128)(2,1)S(1)}, u32[]{:S(2)}, u32[]{:S(2)}) collective-permute-start(bf16[128,256]{1,0:T(8,128)(2,1)} %refs_4_.3), channel_id=1, source_target_pairs={{0,24},{8,16},{16,8},{24,0},{1,25},{9,17},{17,9},{25,1},{2,26},{10... | collective-permute-start | bytes 196616 | tf_op jit(solution)/shard_map/gather_features/ppermute | solution.py:30
  5.9 2.5 %prep.1 = (bf16[1024,512]{1,0:T(8,128)(2,1)S(1)}, bf16[512,1024]{1,0:T(8,128)(2,1)S(1)}, bf16[256,256]{1,0:T(8,128)(2,1)S(1)}, f32[1,256]{1,0:T(1,128)S(1)}, bf16[128,256]{1,0:T(8,128)(2,1)S(1)}) custom-call(s32[1,1]{1,0:T(1,128)S(6)} %copy.12.count, s32[1,1,16]{2,1,0:T(1,128)} %rows_hbm.1, s32[1,1,16]{2,1,0:T(1,128)} %cols_hbm.1, s32[4,128]{1,0:T(4,128)} %bitcast.4, ...), custom_call_target="tpu_custom_call" | custom-call | flops 1073741824 | bytes 524288 | tf_op jit(solution)/shard_map/prep/pallas_call | solution.py:151
  8.4 0.7 %collective-permute-done.1.refs_2_ = bf16[128,256]{1,0:T(8,128)(2,1)S(1)} collective-permute-done((bf16[128,256]{1,0:T(8,128)(2,1)}, bf16[128,256]{1,0:T(8,128)(2,1)S(1)}, u32[]{:S(2)}, u32[]{:S(2)}) %collective-permute-start.1) | collective-permute-done | bytes 65568 | tf_op jit(solution)/shard_map/gather_features/ppermute | solution.py:30
  11.3 3.7 %collective-permute-start.4 = (bf16[128,256]{1,0:T(8,128)(2,1)S(1)}, bf16[128,256]{1,0:T(8,128)(2,1)S(1)}, u32[]{:S(2)}, u32[]{:S(2)}) collective-permute-start(bf16[128,256]{1,0:T(8,128)(2,1)S(1)} %get-tuple-element.50), channel_id=1, source_target_pairs={{0,6},{1,7},{2,4},{3,5},{4,2},{5,3},{6,0},{7,1},{8,14},{9,15},{10,... | collective-permute-start | bytes 196616 | tf_op jit(solution)/shard_map/forward/ppermute | solution.py:30
  15.0 0.8 %collective-permute-start.7 = (bf16[128,256]{1,0:T(8,128)(2,1)S(1)}, bf16[128,256]{1,0:T(8,128)(2,1)S(1)}, u32[]{:S(2)}, u32[]{:S(2)}) collective-permute-start(bf16[128,256]{1,0:T(8,128)(2,1)S(1)} %get-tuple-element.48), channel_id=1, source_target_pairs={{0,2},{1,3},{2,0},{3,1},{4,6},{5,7},{6,4},{7,5},{8,10},{9,11},{10,... | collective-permute-start | bytes 196616 | tf_op jit(solution)/shard_map/forward/ppermute | solution.py:30
  15.8 1.8 %collective-permute-done.4.refs_0_ = bf16[128,256]{1,0:T(8,128)(2,1)S(1)} collective-permute-done((bf16[128,256]{1,0:T(8,128)(2,1)S(1)}, bf16[128,256]{1,0:T(8,128)(2,1)S(1)}, u32[]{:S(2)}, u32[]{:S(2)}) %collective-permute-start.4) | collective-permute-done | bytes 65568 | tf_op jit(solution)/shard_map/forward/ppermute | solution.py:30
  17.6 3.2 %collective-permute-done.5.refs_1_ = bf16[128,256]{1,0:T(8,128)(2,1)S(1)} collective-permute-done((bf16[128,256]{1,0:T(8,128)(2,1)S(1)}, bf16[128,256]{1,0:T(8,128)(2,1)S(1)}, u32[]{:S(2)}, u32[]{:S(2)}) %collective-permute-start.5) | collective-permute-done | bytes 65568 | tf_op jit(solution)/shard_map/forward/ppermute | solution.py:30
  21.4 1.2 %collective-permute-done.15 = bf16[128,256]{1,0:T(8,128)(2,1)S(1)} collective-permute-done((bf16[128,256]{1,0:T(8,128)(2,1)S(1)}, bf16[128,256]{1,0:T(8,128)(2,1)S(1)}, u32[]{:S(2)}, u32[]{:S(2)}) %collective-permute-start.15) | collective-permute-done | bytes 65568 | tf_op jit(solution)/shard_map/weight_rows/ppermute | solution.py:30
  22.6 1.0 %collective-permute-start.16 = (bf16[128,256]{1,0:T(8,128)(2,1)S(1)}, bf16[128,256]{1,0:T(8,128)(2,1)S(1)}, u32[]{:S(2)}, u32[]{:S(2)}) collective-permute-start(bf16[128,256]{1,0:T(8,128)(2,1)S(1)} %add_convert_fusion.5), channel_id=1, source_target_pairs={{0,8},{8,0},{16,24},{24,16},{1,9},{9,1},{17,25},{25,17},{2,10},{10... | collective-permute-start | bytes 196616 | tf_op jit(solution)/shard_map/weight_rows/ppermute | solution.py:30
  23.7 2.3 %collective-permute-start.8 = (bf16[128,256]{1,0:T(8,128)(2,1)S(1)}, bf16[128,256]{1,0:T(8,128)(2,1)S(1)}, u32[]{:S(2)}, u32[]{:S(2)}) collective-permute-start(bf16[128,256]{1,0:T(8,128)(2,1)S(1)} %get-tuple-element.36.refs_4_), channel_id=1, source_target_pairs={{0,6},{1,7},{2,4},{3,5},{4,2},{5,3},{6,0},{7,1},{8,14},{9,15},{10,... | collective-permute-start | bytes 196616 | tf_op jit(solution)/shard_map/gather_slopes/ppermute | solution.py:30
  26.0 2.0 %collective-permute-start.10 = (bf16[128,256]{1,0:T(8,128)(2,1)S(1)}, bf16[128,256]{1,0:T(8,128)(2,1)S(1)}, u32[]{:S(2)}, u32[]{:S(2)}) collective-permute-start(bf16[128,256]{1,0:T(8,128)(2,1)S(1)} %get-tuple-element.36.refs_4_), channel_id=1, source_target_pairs={{0,2},{1,3},{2,0},{3,1},{4,6},{5,7},{6,4},{7,5},{8,10},{9,11},{10,... | collective-permute-start | bytes 196616 | tf_op jit(solution)/shard_map/gather_slopes/ppermute | solution.py:30
  28.1 1.6 %collective-permute-start.17 = (bf16[128,256]{1,0:T(8,128)(2,1)S(1)}, bf16[128,256]{1,0:T(8,128)(2,1)S(1)}, u32[]{:S(2)}, u32[]{:S(2)}) collective-permute-start(bf16[128,256]{1,0:T(8,128)(2,1)S(1)} %add_convert_fusion.4), channel_id=1, source_target_pairs={{0,16},{8,24},{16,0},{24,8},{1,17},{9,25},{17,1},{25,9},{2,18},{10... | collective-permute-start | bytes 196616 | tf_op jit(solution)/shard_map/weight_rows/ppermute | solution.py:30
  30.2 2.3 %collective-permute-done.9.refs_2_ = bf16[128,256]{1,0:T(8,128)(2,1)S(1)} collective-permute-done((bf16[128,256]{1,0:T(8,128)(2,1)S(1)}, bf16[128,256]{1,0:T(8,128)(2,1)S(1)}, u32[]{:S(2)}, u32[]{:S(2)}) %collective-permute-start.9) | collective-permute-done | bytes 65568 | tf_op jit(solution)/shard_map/gather_slopes/ppermute | solution.py:30
  32.6 0.7 %collective-permute-start.18 = (bf16[128,256]{1,0:T(8,128)(2,1)S(1)}, bf16[128,256]{1,0:T(8,128)(2,1)S(1)}, u32[]{:S(2)}, u32[]{:S(2)}) collective-permute-start(bf16[128,256]{1,0:T(8,128)(2,1)S(1)} %add_convert_fusion.3), channel_id=1, source_target_pairs={{0,4},{1,5},{2,6},{3,7},{4,0},{5,1},{6,2},{7,3},{8,12},{9,13},{10,... | collective-permute-start | bytes 196616 | tf_op jit(solution)/shard_map/weight_levels/ppermute | solution.py:30
  33.3 0.8 %collective-permute-done.11.refs_5_ = bf16[512,256]{1,0:T(8,128)(2,1)S(1)} collective-permute-done((bf16[512,256]{1,0:T(8,128)(2,1)S(1)}, bf16[512,256]{1,0:T(8,128)(2,1)S(1)}, u32[]{:S(2)}, u32[]{:S(2)}) %collective-permute-start.11) | collective-permute-done | bytes 262176 | tf_op jit(solution)/shard_map/backward/ppermute | solution.py:30
  34.5 2.3 %collective-permute-start.12 = (bf16[128,256]{1,0:T(8,128)(2,1)S(1)}, bf16[128,256]{1,0:T(8,128)(2,1)S(1)}, u32[]{:S(2)}, u32[]{:S(2)}) collective-permute-start(bf16[128,256]{1,0:T(8,128)(2,1)S(1)} %get-tuple-element.37), channel_id=1, source_target_pairs={{0,24},{8,16},{16,8},{24,0},{1,25},{9,17},{17,9},{25,1},{2,26},{10... | collective-permute-start | bytes 196616 | tf_op jit(solution)/shard_map/backward/ppermute | solution.py:30
  37.4 0.7 %collective-permute-start.14 = (bf16[128,256]{1,0:T(8,128)(2,1)S(1)}, bf16[128,256]{1,0:T(8,128)(2,1)S(1)}, u32[]{:S(2)}, u32[]{:S(2)}) collective-permute-start(bf16[128,256]{1,0:T(8,128)(2,1)S(1)} %get-tuple-element.39), channel_id=1, source_target_pairs={{0,8},{8,0},{16,24},{24,16},{1,9},{9,1},{17,25},{25,17},{2,10},{10... | collective-permute-start | bytes 196616 | tf_op jit(solution)/shard_map/backward/ppermute | solution.py:30
  38.1 0.9 %collective-permute-done.18 = bf16[128,256]{1,0:T(8,128)(2,1)S(1)} collective-permute-done((bf16[128,256]{1,0:T(8,128)(2,1)S(1)}, bf16[128,256]{1,0:T(8,128)(2,1)S(1)}, u32[]{:S(2)}, u32[]{:S(2)}) %collective-permute-start.18) | collective-permute-done | bytes 65568 | tf_op jit(solution)/shard_map/weight_levels/ppermute | solution.py:30
  39.4 1.1 %collective-permute-start.20 = (bf16[128,256]{1,0:T(8,128)(2,1)S(1)}, bf16[128,256]{1,0:T(8,128)(2,1)S(1)}, u32[]{:S(2)}, u32[]{:S(2)}) collective-permute-start(bf16[128,256]{1,0:T(8,128)(2,1)S(1)} %add_convert_fusion.2), channel_id=1, source_target_pairs={{0,3},{1,2},{2,1},{3,0},{4,7},{5,6},{6,5},{7,4},{8,11},{9,10},{10,... | collective-permute-start | bytes 196616 | tf_op jit(solution)/shard_map/weight_levels/ppermute | solution.py:30
  40.5 0.7 %collective-permute-start.21 = (bf16[128,256]{1,0:T(8,128)(2,1)S(1)}, bf16[128,256]{1,0:T(8,128)(2,1)S(1)}, u32[]{:S(2)}, u32[]{:S(2)}) collective-permute-start(bf16[128,256]{1,0:T(8,128)(2,1)S(1)} %add_convert_fusion.2), channel_id=1, source_target_pairs={{0,1},{1,0},{2,3},{3,2},{4,5},{5,4},{6,7},{7,6},{8,9},{9,8},{10,11... | collective-permute-start | bytes 196616 | tf_op jit(solution)/shard_map/weight_levels/ppermute | solution.py:30
  41.3 0.7 %activation.1 = bf16[128,256]{1,0:T(8,128)(2,1)} custom-call(f32[128,256]{1,0:T(8,128)S(1)} %get-tuple-element.34.preact_ref), custom_call_target="tpu_custom_call" | custom-call | flops 131072 | bytes 196608 | tf_op jit(solution)/shard_map/activation/pallas_call | solution.py:283
  41.9 0.8 %feature_gradient.1 = bf16[128,256]{1,0:T(8,128)(2,1)} custom-call(bf16[128,256]{1,0:T(8,128)(2,1)S(1)} %collective-permute-done.12.refs_0_, bf16[128,256]{1,0:T(8,128)(2,1)S(1)} %collective-permute-done.13.refs_1_, bf16[128,256]{1,0:T(8,128)(2,1)S(1)} %collective-permute-done.14.refs_2_, bf16[128,256]{1,0:T(8,128)(2,1)S(1)} %get-tuple-element.40.refs_3_, ...), custom_call_target="tpu_custom_call" | custom-call | flops 16777216 | bytes 393216 | tf_op jit(solution)/shard_map/backward/feature_gradient/pallas_call | solution.py:304
  42.8 1.1 %collective-permute-done.19 = bf16[128,256]{1,0:T(8,128)(2,1)S(1)} collective-permute-done((bf16[128,256]{1,0:T(8,128)(2,1)S(1)}, bf16[128,256]{1,0:T(8,128)(2,1)S(1)}, u32[]{:S(2)}, u32[]{:S(2)}) %collective-permute-start.19) | collective-permute-done | bytes 65568 | tf_op jit(solution)/shard_map/weight_levels/ppermute | solution.py:30
  43.9 0.7 %convert_multiply_fusion = f32[256,256]{1,0:T(8,128)} fusion(bf16[128,256]{1,0:T(8,128)(2,1)S(1)} %get-tuple-element.51, bf16[128,256]{1,0:T(8,128)(2,1)S(1)} %get-tuple-element.52, pred[]{:T(512)S(6)} %eq.3), kind=kLoop, calls=%fused_computation.1 | loop fusion | flops 720896 | bytes 393217 | tf_op jit(solution)/shard_map/weight_levels/mul | solution.py:395
  (38 shorter events, 5.5 us)
Async XLA Ops:
  0.6 7.7 %collective-permute-start = (bf16[128,256]{1,0:T(8,128)(2,1)}, bf16[128,256]{1,0:T(8,128)(2,1)S(1)}, u32[]{:S(2)}, u32[]{:S(2)}) collective-permute-start(bf16[128,256]{1,0:T(8,128)(2,1)} %refs_4_.3), channel_id=1, source_target_pairs={{0,24},{8,16},{16,8},{24,0},{1,25},{9,17},{17,9},{25,1},{2,26},{10... | collective-permute-start | bytes 196616 | tf_op jit(solution)/shard_map/gather_features/ppermute | solution.py:30
  4.6 4.5 %collective-permute-start.1 = (bf16[128,256]{1,0:T(8,128)(2,1)}, bf16[128,256]{1,0:T(8,128)(2,1)S(1)}, u32[]{:S(2)}, u32[]{:S(2)}) collective-permute-start(bf16[128,256]{1,0:T(8,128)(2,1)} %refs_4_.3), channel_id=1, source_target_pairs={{0,16},{8,24},{16,0},{24,8},{1,17},{9,25},{17,1},{25,9},{2,18},{10... | collective-permute-start | bytes 196616 | tf_op jit(solution)/shard_map/gather_features/ppermute | solution.py:30
  5.1 4.5 %collective-permute-start.2 = (bf16[128,256]{1,0:T(8,128)(2,1)}, bf16[128,256]{1,0:T(8,128)(2,1)S(1)}, u32[]{:S(2)}, u32[]{:S(2)}) collective-permute-start(bf16[128,256]{1,0:T(8,128)(2,1)} %refs_4_.3), channel_id=1, source_target_pairs={{0,8},{8,0},{16,24},{24,16},{1,9},{9,1},{17,25},{25,17},{2,10},{10... | collective-permute-start | bytes 196616 | tf_op jit(solution)/shard_map/gather_features/ppermute | solution.py:30
  5.9 3.7 %copy-start = (bf16[128,256]{1,0:T(8,128)(2,1)S(1)}, bf16[128,256]{1,0:T(8,128)(2,1)}, u32[]{:S(2)}) copy-start(bf16[128,256]{1,0:T(8,128)(2,1)} %refs_4_.3) | copy-start | bytes 196612
  9.8 1.4 %collective-permute-start.3 = (bf16[256,256]{1,0:T(8,128)(2,1)S(1)}, bf16[256,256]{1,0:T(8,128)(2,1)S(1)}, u32[]{:S(2)}, u32[]{:S(2)}) collective-permute-start(bf16[256,256]{1,0:T(8,128)(2,1)S(1)} %forward_far.1), channel_id=1, source_target_pairs={{0,1},{1,0},{2,3},{3,2},{4,5},{5,4},{6,7},{7,6},{8,9},{9,8},{10,11... | collective-permute-start | bytes 393224 | tf_op jit(solution)/shard_map/forward/ppermute | solution.py:30
  10.3 4.7 %collective-permute-start.6 = (bf16[256,256]{1,0:T(8,128)(2,1)S(1)}, bf16[256,256]{1,0:T(8,128)(2,1)S(1)}, u32[]{:S(2)}, u32[]{:S(2)}) collective-permute-start(bf16[256,256]{1,0:T(8,128)(2,1)S(1)} %get-tuple-element.29), channel_id=1, source_target_pairs={{0,1},{1,0},{2,3},{3,2},{4,5},{5,4},{6,7},{7,6},{8,9},{9,8},{10,11... | collective-permute-start | bytes 393224 | tf_op jit(solution)/shard_map/forward/ppermute | solution.py:30
  11.3 6.4 %collective-permute-start.4 = (bf16[128,256]{1,0:T(8,128)(2,1)S(1)}, bf16[128,256]{1,0:T(8,128)(2,1)S(1)}, u32[]{:S(2)}, u32[]{:S(2)}) collective-permute-start(bf16[128,256]{1,0:T(8,128)(2,1)S(1)} %get-tuple-element.50), channel_id=1, source_target_pairs={{0,6},{1,7},{2,4},{3,5},{4,2},{5,3},{6,0},{7,1},{8,14},{9,15},{10,... | collective-permute-start | bytes 196616 | tf_op jit(solution)/shard_map/forward/ppermute | solution.py:30
  14.9 5.9 %collective-permute-start.5 = (bf16[128,256]{1,0:T(8,128)(2,1)S(1)}, bf16[128,256]{1,0:T(8,128)(2,1)S(1)}, u32[]{:S(2)}, u32[]{:S(2)}) collective-permute-start(bf16[128,256]{1,0:T(8,128)(2,1)S(1)} %get-tuple-element.49), channel_id=1, source_target_pairs={{0,4},{1,5},{2,6},{3,7},{4,0},{5,1},{6,2},{7,3},{8,12},{9,13},{10,... | collective-permute-start | bytes 196616 | tf_op jit(solution)/shard_map/forward/ppermute | solution.py:30
  15.0 5.8 %collective-permute-start.7 = (bf16[128,256]{1,0:T(8,128)(2,1)S(1)}, bf16[128,256]{1,0:T(8,128)(2,1)S(1)}, u32[]{:S(2)}, u32[]{:S(2)}) collective-permute-start(bf16[128,256]{1,0:T(8,128)(2,1)S(1)} %get-tuple-element.48), channel_id=1, source_target_pairs={{0,2},{1,3},{2,0},{3,1},{4,6},{5,7},{6,4},{7,5},{8,10},{9,11},{10,... | collective-permute-start | bytes 196616 | tf_op jit(solution)/shard_map/forward/ppermute | solution.py:30
  21.3 1.3 %collective-permute-start.15 = (bf16[128,256]{1,0:T(8,128)(2,1)S(1)}, bf16[128,256]{1,0:T(8,128)(2,1)S(1)}, u32[]{:S(2)}, u32[]{:S(2)}) collective-permute-start(bf16[128,256]{1,0:T(8,128)(2,1)S(1)} %get-tuple-element.42), channel_id=1, source_target_pairs={{0,1},{1,0},{2,3},{3,2},{4,5},{5,4},{6,7},{7,6},{8,9},{9,8},{10,11... | collective-permute-start | bytes 196616 | tf_op jit(solution)/shard_map/weight_rows/ppermute | solution.py:30
  22.6 5.4 %collective-permute-start.16 = (bf16[128,256]{1,0:T(8,128)(2,1)S(1)}, bf16[128,256]{1,0:T(8,128)(2,1)S(1)}, u32[]{:S(2)}, u32[]{:S(2)}) collective-permute-start(bf16[128,256]{1,0:T(8,128)(2,1)S(1)} %add_convert_fusion.5), channel_id=1, source_target_pairs={{0,8},{8,0},{16,24},{24,16},{1,9},{9,1},{17,25},{25,17},{2,10},{10... | collective-permute-start | bytes 196616 | tf_op jit(solution)/shard_map/weight_rows/ppermute | solution.py:30
  23.7 6.5 %collective-permute-start.8 = (bf16[128,256]{1,0:T(8,128)(2,1)S(1)}, bf16[128,256]{1,0:T(8,128)(2,1)S(1)}, u32[]{:S(2)}, u32[]{:S(2)}) collective-permute-start(bf16[128,256]{1,0:T(8,128)(2,1)S(1)} %get-tuple-element.36.refs_4_), channel_id=1, source_target_pairs={{0,6},{1,7},{2,4},{3,5},{4,2},{5,3},{6,0},{7,1},{8,14},{9,15},{10,... | collective-permute-start | bytes 196616 | tf_op jit(solution)/shard_map/gather_slopes/ppermute | solution.py:30
  25.9 6.6 %collective-permute-start.9 = (bf16[128,256]{1,0:T(8,128)(2,1)S(1)}, bf16[128,256]{1,0:T(8,128)(2,1)S(1)}, u32[]{:S(2)}, u32[]{:S(2)}) collective-permute-start(bf16[128,256]{1,0:T(8,128)(2,1)S(1)} %get-tuple-element.36.refs_4_), channel_id=1, source_target_pairs={{0,4},{1,5},{2,6},{3,7},{4,0},{5,1},{6,2},{7,3},{8,12},{9,13},{10,... | collective-permute-start | bytes 196616 | tf_op jit(solution)/shard_map/gather_slopes/ppermute | solution.py:30
  26.0 6.5 %collective-permute-start.10 = (bf16[128,256]{1,0:T(8,128)(2,1)S(1)}, bf16[128,256]{1,0:T(8,128)(2,1)S(1)}, u32[]{:S(2)}, u32[]{:S(2)}) collective-permute-start(bf16[128,256]{1,0:T(8,128)(2,1)S(1)} %get-tuple-element.36.refs_4_), channel_id=1, source_target_pairs={{0,2},{1,3},{2,0},{3,1},{4,6},{5,7},{6,4},{7,5},{8,10},{9,11},{10,... | collective-permute-start | bytes 196616 | tf_op jit(solution)/shard_map/gather_slopes/ppermute | solution.py:30
  28.1 4.5 %collective-permute-start.17 = (bf16[128,256]{1,0:T(8,128)(2,1)S(1)}, bf16[128,256]{1,0:T(8,128)(2,1)S(1)}, u32[]{:S(2)}, u32[]{:S(2)}) collective-permute-start(bf16[128,256]{1,0:T(8,128)(2,1)S(1)} %add_convert_fusion.4), channel_id=1, source_target_pairs={{0,16},{8,24},{16,0},{24,8},{1,17},{9,25},{17,1},{25,9},{2,18},{10... | collective-permute-start | bytes 196616 | tf_op jit(solution)/shard_map/weight_rows/ppermute | solution.py:30
  32.5 1.6 %collective-permute-start.11 = (bf16[512,256]{1,0:T(8,128)(2,1)S(1)}, bf16[512,256]{1,0:T(8,128)(2,1)S(1)}, u32[]{:S(2)}, u32[]{:S(2)}) collective-permute-start(bf16[512,256]{1,0:T(8,128)(2,1)S(1)} %pad_maximum_fusion), channel_id=1, source_target_pairs={{0,1},{1,0},{2,3},{3,2},{4,5},{5,4},{6,7},{7,6},{8,9},{9,8},{10,11... | collective-permute-start | bytes 786440 | tf_op jit(solution)/shard_map/backward/ppermute | solution.py:30
  32.6 6.4 %collective-permute-start.18 = (bf16[128,256]{1,0:T(8,128)(2,1)S(1)}, bf16[128,256]{1,0:T(8,128)(2,1)S(1)}, u32[]{:S(2)}, u32[]{:S(2)}) collective-permute-start(bf16[128,256]{1,0:T(8,128)(2,1)S(1)} %add_convert_fusion.3), channel_id=1, source_target_pairs={{0,4},{1,5},{2,6},{3,7},{4,0},{5,1},{6,2},{7,3},{8,12},{9,13},{10,... | collective-permute-start | bytes 196616 | tf_op jit(solution)/shard_map/weight_levels/ppermute | solution.py:30
  34.5 6.0 %collective-permute-start.12 = (bf16[128,256]{1,0:T(8,128)(2,1)S(1)}, bf16[128,256]{1,0:T(8,128)(2,1)S(1)}, u32[]{:S(2)}, u32[]{:S(2)}) collective-permute-start(bf16[128,256]{1,0:T(8,128)(2,1)S(1)} %get-tuple-element.37), channel_id=1, source_target_pairs={{0,24},{8,16},{16,8},{24,0},{1,25},{9,17},{17,9},{25,1},{2,26},{10... | collective-permute-start | bytes 196616 | tf_op jit(solution)/shard_map/backward/ppermute | solution.py:30
  36.9 5.1 %collective-permute-start.13 = (bf16[128,256]{1,0:T(8,128)(2,1)S(1)}, bf16[128,256]{1,0:T(8,128)(2,1)S(1)}, u32[]{:S(2)}, u32[]{:S(2)}) collective-permute-start(bf16[128,256]{1,0:T(8,128)(2,1)S(1)} %get-tuple-element.38), channel_id=1, source_target_pairs={{0,16},{8,24},{16,0},{24,8},{1,17},{9,25},{17,1},{25,9},{2,18},{10... | collective-permute-start | bytes 196616 | tf_op jit(solution)/shard_map/backward/ppermute | solution.py:30
  37.4 4.6 %collective-permute-start.14 = (bf16[128,256]{1,0:T(8,128)(2,1)S(1)}, bf16[128,256]{1,0:T(8,128)(2,1)S(1)}, u32[]{:S(2)}, u32[]{:S(2)}) collective-permute-start(bf16[128,256]{1,0:T(8,128)(2,1)S(1)} %get-tuple-element.39), channel_id=1, source_target_pairs={{0,8},{8,0},{16,24},{24,16},{1,9},{9,1},{17,25},{25,17},{2,10},{10... | collective-permute-start | bytes 196616 | tf_op jit(solution)/shard_map/backward/ppermute | solution.py:30
  39.1 4.8 %collective-permute-start.19 = (bf16[128,256]{1,0:T(8,128)(2,1)S(1)}, bf16[128,256]{1,0:T(8,128)(2,1)S(1)}, u32[]{:S(2)}, u32[]{:S(2)}) collective-permute-start(bf16[128,256]{1,0:T(8,128)(2,1)S(1)} %add_convert_fusion.2), channel_id=1, source_target_pairs={{0,2},{1,3},{2,0},{3,1},{4,6},{5,7},{6,4},{7,5},{8,10},{9,11},{10,... | collective-permute-start | bytes 196616 | tf_op jit(solution)/shard_map/weight_levels/ppermute | solution.py:30
  39.4 4.5 %collective-permute-start.20 = (bf16[128,256]{1,0:T(8,128)(2,1)S(1)}, bf16[128,256]{1,0:T(8,128)(2,1)S(1)}, u32[]{:S(2)}, u32[]{:S(2)}) collective-permute-start(bf16[128,256]{1,0:T(8,128)(2,1)S(1)} %add_convert_fusion.2), channel_id=1, source_target_pairs={{0,3},{1,2},{2,1},{3,0},{4,7},{5,6},{6,5},{7,4},{8,11},{9,10},{10,... | collective-permute-start | bytes 196616 | tf_op jit(solution)/shard_map/weight_levels/ppermute | solution.py:30
  40.5 3.4 %collective-permute-start.21 = (bf16[128,256]{1,0:T(8,128)(2,1)S(1)}, bf16[128,256]{1,0:T(8,128)(2,1)S(1)}, u32[]{:S(2)}, u32[]{:S(2)}) collective-permute-start(bf16[128,256]{1,0:T(8,128)(2,1)S(1)} %add_convert_fusion.2), channel_id=1, source_target_pairs={{0,1},{1,0},{2,3},{3,2},{4,5},{5,4},{6,7},{7,6},{8,9},{9,8},{10,11... | collective-permute-start | bytes 196616 | tf_op jit(solution)/shard_map/weight_levels/ppermute | solution.py:30

commit v5 on v4

--- a/solution.py
+++ b/solution.py
@@ -30,6 +30,11 @@
     return lax.ppermute(value, axis, [(i, i ^ mask) for i in range(size)])
 
 
+def swap_by_core(value, mask0, mask1):
+    size = lax.axis_size("col")
+    return lax.ppermute(value, "col", [(i, i ^ (mask1 if i & 1 else mask0)) for i in range(size)])
+
+
 def exchange(values, axis, unit):
     out = list(values)
     for m in reversed(range(1, len(values))):
@@ -45,8 +50,12 @@
     return [values[i] for i in order]
 
 
+def run(part, index, size, place0, place1=None):
+    return (part, index * size, size, (place0 * size, (place0 if place1 is None else place1) * size))
+
+
 def runs_of(order, size):
-    return [(order.index(i), 0, size) for i in range(len(order))]
+    return [run(i, 0, size, place) for i, place in enumerate(order)]
 
 
 def tiled_dot(shape, store, lhs_rows, rhs_rows):
@@ -182,10 +191,10 @@
 
     @pl.when(pl.program_id(0) == 0)
     def _():
-        start = 0
-        for part, first, size in runs:
-            joined[start : start + size, :] = parts[part][first : first + size, :]
-            start += size
+        core = lax.axis_index("col") & 1
+        for part, first, size, places in runs:
+            start = jnp.where(core == 0, *places) if places[0] != places[1] else places[0]
+            joined[pl.ds(pl.multiple_of(start, size), size), :] = parts[part][first : first + size, :]
 
     rows = sum(out.shape[0] for out in outs)
     total = lax.dot_general(
@@ -314,6 +323,10 @@
     return (left.astype(F32) + right.astype(F32)).astype(BF16)
 
 
+def add_all(values):
+    return sum(value.astype(F32) for value in values).astype(BF16)
+
+
 def shards(
     features,
     weight,
@@ -332,7 +345,6 @@
     block = block_values.shape[3]
     row_blocks = node_count * col_devices // block
 
-    row_masks = [1 << i for i in range((row_devices - 1).bit_length())]
     level_masks = [2 << i for i in reversed(range((levels - 1).bit_length()))]
     row_order, level_order = far_first(row_devices), far_first(levels)
     with jax.named_scope("gather_features"):
@@ -357,24 +369,34 @@
     activations = activation(preact)
 
     with jax.named_scope("gather_slopes"):
-        slope_own = exchange([slopes] * levels, "col", 2)
+        arrived = swap(jnp.concatenate([slopes, weight_sent]), "col", 1)
+        both = jnp.concatenate([slopes, arrived[:node_count]])
+        far_pairs = [(m, m - 1) for m in range(levels - 1, 1, -2)]
+        far = [swap_by_core(both, 2 * m0, 2 * m1) for m0, m1 in far_pairs]
+        near = swap(slopes, "col", 2)
 
     with jax.named_scope("weight_rows"):
-        term = add(weight_kept, swap(weight_sent, "col", 1))
-        for mask in row_masks:
-            other = swap(term, "row", mask)
-            if mask == row_masks[-1]:
-                other, _ = lax.optimization_barrier((other, slope_own[1:]))
-            term = add(term, other)
+        term = add(weight_kept, arrived[node_count:])
+        step = 1
+        while step < row_devices:
+            wide = min(4, row_devices // step)
+            others = [swap(term, "row", m * step) for m in reversed(range(1, wide))]
+            step *= wide
+            if step == row_devices:
+                others, _ = lax.optimization_barrier((others, (far, near)))
+            term = add_all([term] + others)
 
     with jax.named_scope("backward"):
-        far = ordered(slope_own, level_order)
-        slope_other = swap(jnp.concatenate(far), "col", 1)
-        runs = runs_of(level_order, node_count)
+        handed = swap(jnp.concatenate(far + [near]), "col", 1)
+        runs = [run(0, 0, node_count, 0), run(1, 0, node_count, levels), run(2 + len(far), 0, node_count, 1)]
+        for i, (m0, m1) in enumerate(far_pairs):
+            runs += [run(2 + i, 0, node_count, m0, m1), run(2 + i, 1, node_count, levels + m0, levels + m1)]
+            runs += [run(3 + len(far), 2 * i, node_count, levels + m1, levels + m0), run(3 + len(far), 2 * i + 1, node_count, m1, m0)]
+        runs.append(run(3 + len(far), 2 * len(far), node_count, levels + 1))
         node_terms = product(
             tile_turned,
-            far + [slope_other],
-            runs + [(levels, part * node_count, node_count) for part, _, _ in runs],
+            [slopes, arrived] + far + [near, handed],
+            runs,
             [node_count] * row_devices,
             "backward_tile",
         )

time: 44.9 us -> 44.5 us (level)
  waiting for transfers between devices: 13.5 us -> 10.5 us
  starting transfers between devices: 23.4 us -> 25.8 us
    ppermute x22 -> x21, waiting for transfers between devices: 13.5 us -> 9.49 us  [swap(): return lax.ppermute(value, axis, [(i, i ^ mask) for i in range(size)])]
    ppermute x0 -> x1, starting transfers between devices: none -> 2.54 us  [swap_by_core(): lax.ppermute(value, 'col', [(i, i ^ (mask1 if i & 1 else mask0)) for i in...]
    ppermute x0 -> x1, waiting for transfers between devices: none -> 1.04 us  [swap_by_core(): lax.ppermute(value, 'col', [(i, i ^ (mask1 if i & 1 else mask0)) for i in...]
    ppermute x22 -> x21, starting transfers between devices: 23.4 us -> 23.3 us  [swap(): return lax.ppermute(value, axis, [(i, i ^ mask) for i in range(size)])]
  transfers between devices with their start and end apart: 22 -> 22, of which waited for: 11 -> 13; matrix products, arithmetic and copies ran while one was open for 0% -> 0% of each run, Pallas kernels for 11% -> 11%
where the time goes in v5:
time: 44.5 us; the launch traced here: 44.3 us
  starting transfers between devices  25.8 us (58%)
  waiting for transfers between devices  10.5 us (24%)
  Pallas kernels  5.58 us (13%)
  between operations  1.41 us (3%)
  other arithmetic  0.95 us (2%)
    ppermute x21, starting transfers between devices, swap(): return lax.ppermute(value, axis, [(i, i ^ mask) for i in range(size)])  23.3 us
    ppermute x21, waiting for transfers between devices, swap(): return lax.ppermute(value, axis, [(i, i ^ mask) for i in range(size)])  9.49 us
    pallas_call x1, Pallas kernels, prep(): pl.pallas_call(functools.partial(prep_kernel, per_step), grid=(row_blocks...  2.56 us
    ppermute x1, starting transfers between devices, swap_by_core(): lax.ppermute(value, 'col', [(i, i ^ (mask1 if i & 1 else mask0)) for i in...  2.54 us
    ppermute x1, waiting for transfers between devices, swap_by_core(): lax.ppermute(value, 'col', [(i, i ^ (mask1 if i & 1 else mask0)) for i in...  1.04 us
    pallas_call x3, Pallas kernels, product(): pl.pallas_call(functools.partial(product_kernel, len(parts), tuple(runs),...  1.04 us
  transfers between devices with their start and end apart: 22, of which 13 were waited for; matrix products, arithmetic and copies ran while one was open for 0% of the time, Pallas kernels for 11%

profile of v5, /device:TPU:0, one launch (start us, length us, event | category | flops | bytes accessed | tf_op | source)
XLA Modules:
  0.0 44.3 jit_solution(15982518164396383696)
XLA Ops:
  0.6 4.0 %collective-permute-start = (bf16[128,256]{1,0:T(8,128)(2,1)}, bf16[128,256]{1,0:T(8,128)(2,1)S(1)}, u32[]{:S(2)}, u32[]{:S(2)}) collective-permute-start(bf16[128,256]{1,0:T(8,128)(2,1)} %refs_4_.3), channel_id=1, source_target_pairs={{0,24},{8,16},{16,8},{24,0},{1,25},{9,17},{17,9},{25,1},{2,26},{10... | collective-permute-start | bytes 196616 | tf_op jit(solution)/shard_map/gather_features/ppermute | solution.py:30
  5.9 2.6 %prep.1 = (bf16[1024,512]{1,0:T(8,128)(2,1)S(1)}, bf16[512,1024]{1,0:T(8,128)(2,1)S(1)}, bf16[256,256]{1,0:T(8,128)(2,1)S(1)}, f32[1,256]{1,0:T(1,128)S(1)}, bf16[128,256]{1,0:T(8,128)(2,1)S(1)}) custom-call(s32[1,1]{1,0:T(1,128)S(6)} %copy.12.count, s32[1,1,16]{2,1,0:T(1,128)} %rows_hbm.1, s32[1,1,16]{2,1,0:T(1,128)} %cols_hbm.1, s32[4,128]{1,0:T(4,128)} %bitcast.4, ...), custom_call_target="tpu_custom_call" | custom-call | flops 1073741824 | bytes 524288 | tf_op jit(solution)/shard_map/prep/pallas_call | solution.py:160
  8.5 0.6 %collective-permute-done.1.refs_2_ = bf16[128,256]{1,0:T(8,128)(2,1)S(1)} collective-permute-done((bf16[128,256]{1,0:T(8,128)(2,1)}, bf16[128,256]{1,0:T(8,128)(2,1)S(1)}, u32[]{:S(2)}, u32[]{:S(2)}) %collective-permute-start.1) | collective-permute-done | bytes 65568 | tf_op jit(solution)/shard_map/gather_features/ppermute | solution.py:30
  10.3 0.6 %collective-permute-start.6 = (bf16[256,256]{1,0:T(8,128)(2,1)S(1)}, bf16[256,256]{1,0:T(8,128)(2,1)S(1)}, u32[]{:S(2)}, u32[]{:S(2)}) collective-permute-start(bf16[256,256]{1,0:T(8,128)(2,1)S(1)} %get-tuple-element.31), channel_id=1, source_target_pairs={{0,1},{1,0},{2,3},{3,2},{4,5},{5,4},{6,7},{7,6},{8,9},{9,8},{10,11... | collective-permute-start | bytes 393224 | tf_op jit(solution)/shard_map/forward/ppermute | solution.py:30
  11.3 3.7 %collective-permute-start.4 = (bf16[128,256]{1,0:T(8,128)(2,1)S(1)}, bf16[128,256]{1,0:T(8,128)(2,1)S(1)}, u32[]{:S(2)}, u32[]{:S(2)}) collective-permute-start(bf16[128,256]{1,0:T(8,128)(2,1)S(1)} %get-tuple-element.54), channel_id=1, source_target_pairs={{0,6},{1,7},{2,4},{3,5},{4,2},{5,3},{6,0},{7,1},{8,14},{9,15},{10,... | collective-permute-start | bytes 196616 | tf_op jit(solution)/shard_map/forward/ppermute | solution.py:30
  15.0 0.8 %collective-permute-start.7 = (bf16[128,256]{1,0:T(8,128)(2,1)S(1)}, bf16[128,256]{1,0:T(8,128)(2,1)S(1)}, u32[]{:S(2)}, u32[]{:S(2)}) collective-permute-start(bf16[128,256]{1,0:T(8,128)(2,1)S(1)} %get-tuple-element.52), channel_id=1, source_target_pairs={{0,2},{1,3},{2,0},{3,1},{4,6},{5,7},{6,4},{7,5},{8,10},{9,11},{10,... | collective-permute-start | bytes 196616 | tf_op jit(solution)/shard_map/forward/ppermute | solution.py:30
  15.8 1.8 %collective-permute-done.4.refs_0_ = bf16[128,256]{1,0:T(8,128)(2,1)S(1)} collective-permute-done((bf16[128,256]{1,0:T(8,128)(2,1)S(1)}, bf16[128,256]{1,0:T(8,128)(2,1)S(1)}, u32[]{:S(2)}, u32[]{:S(2)}) %collective-permute-start.4) | collective-permute-done | bytes 65568 | tf_op jit(solution)/shard_map/forward/ppermute | solution.py:30
  17.6 3.2 %collective-permute-done.5.refs_1_ = bf16[128,256]{1,0:T(8,128)(2,1)S(1)} collective-permute-done((bf16[128,256]{1,0:T(8,128)(2,1)S(1)}, bf16[128,256]{1,0:T(8,128)(2,1)S(1)}, u32[]{:S(2)}, u32[]{:S(2)}) %collective-permute-start.5) | collective-permute-done | bytes 65568 | tf_op jit(solution)/shard_map/forward/ppermute | solution.py:30
  21.4 1.2 %collective-permute-start.10 = (bf16[128,256]{1,0:T(8,128)(2,1)S(1)}, bf16[128,256]{1,0:T(8,128)(2,1)S(1)}, u32[]{:S(2)}, u32[]{:S(2)}) collective-permute-start(bf16[128,256]{1,0:T(8,128)(2,1)S(1)} %get-tuple-element.38.refs_1_), channel_id=1, source_target_pairs={{0,2},{1,3},{2,0},{3,1},{4,6},{5,7},{6,4},{7,5},{8,10},{9,11},{10,... | collective-permute-start | bytes 196616 | tf_op jit(solution)/shard_map/gather_slopes/ppermute | solution.py:30
  22.8 2.5 %collective-permute-start.9 = (bf16[256,256]{1,0:T(8,128)(2,1)S(1)}, bf16[256,256]{1,0:T(8,128)(2,1)S(1)}, u32[]{:S(2)}, u32[]{:S(2)}) collective-permute-start(bf16[256,256]{1,0:T(8,128)(2,1)S(1)} %pad_maximum_fusion.1), channel_id=1, source_target_pairs={{0,6},{1,5},{2,4},{3,7},{4,2},{5,1},{6,0},{7,3},{8,14},{9,13},{10,... | collective-permute-start | bytes 393224 | tf_op jit(solution)/shard_map/gather_slopes/ppermute | solution.py:35
  25.3 2.0 %collective-permute-start.15 = (bf16[128,256]{1,0:T(8,128)(2,1)S(1)}, bf16[128,256]{1,0:T(8,128)(2,1)S(1)}, u32[]{:S(2)}, u32[]{:S(2)}) collective-permute-start(bf16[128,256]{1,0:T(8,128)(2,1)S(1)} %add_convert_fusion.4), channel_id=1, source_target_pairs={{0,24},{8,16},{16,8},{24,0},{1,25},{9,17},{17,9},{25,1},{2,26},{10... | collective-permute-start | bytes 196616 | tf_op jit(solution)/shard_map/weight_rows/ppermute | solution.py:30
  27.7 1.2 %collective-permute-start.17 = (bf16[128,256]{1,0:T(8,128)(2,1)S(1)}, bf16[128,256]{1,0:T(8,128)(2,1)S(1)}, u32[]{:S(2)}, u32[]{:S(2)}) collective-permute-start(bf16[128,256]{1,0:T(8,128)(2,1)S(1)} %add_convert_fusion.4), channel_id=1, source_target_pairs={{0,8},{8,0},{16,24},{24,16},{1,9},{9,1},{17,25},{25,17},{2,10},{10... | collective-permute-start | bytes 196616 | tf_op jit(solution)/shard_map/weight_rows/ppermute | solution.py:30
  28.9 1.0 %collective-permute-done.9.refs_3_ = bf16[256,256]{1,0:T(8,128)(2,1)S(1)} collective-permute-done((bf16[256,256]{1,0:T(8,128)(2,1)S(1)}, bf16[256,256]{1,0:T(8,128)(2,1)S(1)}, u32[]{:S(2)}, u32[]{:S(2)}) %collective-permute-start.9) | collective-permute-done | bytes 131104 | tf_op jit(solution)/shard_map/gather_slopes/ppermute | solution.py:35
  29.9 1.7 %collective-permute-start.11 = (bf16[384,256]{1,0:T(8,128)(2,1)S(1)}, bf16[384,256]{1,0:T(8,128)(2,1)S(1)}, u32[]{:S(2)}, u32[]{:S(2)}) collective-permute-start(bf16[384,256]{1,0:T(8,128)(2,1)S(1)} %pad_maximum_fusion), channel_id=1, source_target_pairs={{0,1},{1,0},{2,3},{3,2},{4,5},{5,4},{6,7},{7,6},{8,9},{9,8},{10,11... | collective-permute-start | bytes 589832 | tf_op jit(solution)/shard_map/backward/ppermute | solution.py:30
  32.0 1.9 %collective-permute-start.18 = (bf16[128,256]{1,0:T(8,128)(2,1)S(1)}, bf16[128,256]{1,0:T(8,128)(2,1)S(1)}, u32[]{:S(2)}, u32[]{:S(2)}) collective-permute-start(bf16[128,256]{1,0:T(8,128)(2,1)S(1)} %add_convert_fusion.3), channel_id=1, source_target_pairs={{0,4},{1,5},{2,6},{3,7},{4,0},{5,1},{6,2},{7,3},{8,12},{9,13},{10,... | collective-permute-start | bytes 196616 | tf_op jit(solution)/shard_map/weight_levels/ppermute | solution.py:30
  34.3 2.0 %collective-permute-start.12 = (bf16[128,256]{1,0:T(8,128)(2,1)S(1)}, bf16[128,256]{1,0:T(8,128)(2,1)S(1)}, u32[]{:S(2)}, u32[]{:S(2)}) collective-permute-start(bf16[128,256]{1,0:T(8,128)(2,1)S(1)} %get-tuple-element.40), channel_id=1, source_target_pairs={{0,24},{8,16},{16,8},{24,0},{1,25},{9,17},{17,9},{25,1},{2,26},{10... | collective-permute-start | bytes 196616 | tf_op jit(solution)/shard_map/backward/ppermute | solution.py:30
  36.7 1.2 %collective-permute-start.14 = (bf16[128,256]{1,0:T(8,128)(2,1)S(1)}, bf16[128,256]{1,0:T(8,128)(2,1)S(1)}, u32[]{:S(2)}, u32[]{:S(2)}) collective-permute-start(bf16[128,256]{1,0:T(8,128)(2,1)S(1)} %get-tuple-element.42), channel_id=1, source_target_pairs={{0,8},{8,0},{16,24},{24,16},{1,9},{9,1},{17,25},{25,17},{2,10},{10... | collective-permute-start | bytes 196616 | tf_op jit(solution)/shard_map/backward/ppermute | solution.py:30
  38.4 0.7 %collective-permute-start.19 = (bf16[128,256]{1,0:T(8,128)(2,1)S(1)}, bf16[128,256]{1,0:T(8,128)(2,1)S(1)}, u32[]{:S(2)}, u32[]{:S(2)}) collective-permute-start(bf16[128,256]{1,0:T(8,128)(2,1)S(1)} %add_convert_fusion.2), channel_id=1, source_target_pairs={{0,2},{1,3},{2,0},{3,1},{4,6},{5,7},{6,4},{7,5},{8,10},{9,11},{10,... | collective-permute-start | bytes 196616 | tf_op jit(solution)/shard_map/weight_levels/ppermute | solution.py:30
  39.1 0.6 %collective-permute-done.12.refs_0_ = bf16[128,256]{1,0:T(8,128)(2,1)S(1)} collective-permute-done((bf16[128,256]{1,0:T(8,128)(2,1)S(1)}, bf16[128,256]{1,0:T(8,128)(2,1)S(1)}, u32[]{:S(2)}, u32[]{:S(2)}) %collective-permute-start.12) | collective-permute-done | bytes 65568 | tf_op jit(solution)/shard_map/backward/ppermute | solution.py:30
  39.7 0.9 %collective-permute-start.21 = (bf16[128,256]{1,0:T(8,128)(2,1)S(1)}, bf16[128,256]{1,0:T(8,128)(2,1)S(1)}, u32[]{:S(2)}, u32[]{:S(2)}) collective-permute-start(bf16[128,256]{1,0:T(8,128)(2,1)S(1)} %add_convert_fusion.2), channel_id=1, source_target_pairs={{0,1},{1,0},{2,3},{3,2},{4,5},{5,4},{6,7},{7,6},{8,9},{9,8},{10,11... | collective-permute-start | bytes 196616 | tf_op jit(solution)/shard_map/weight_levels/ppermute | solution.py:30
  40.6 0.7 %activation.1 = bf16[128,256]{1,0:T(8,128)(2,1)} custom-call(f32[128,256]{1,0:T(8,128)S(1)} %get-tuple-element.36.preact_ref), custom_call_target="tpu_custom_call" | custom-call | flops 131072 | bytes 196608 | tf_op jit(solution)/shard_map/activation/pallas_call | solution.py:292
  41.3 0.8 %feature_gradient.1 = bf16[128,256]{1,0:T(8,128)(2,1)} custom-call(bf16[128,256]{1,0:T(8,128)(2,1)S(1)} %collective-permute-done.12.refs_0_, bf16[128,256]{1,0:T(8,128)(2,1)S(1)} %collective-permute-done.13.refs_1_, bf16[128,256]{1,0:T(8,128)(2,1)S(1)} %collective-permute-done.14.refs_2_, bf16[128,256]{1,0:T(8,128)(2,1)S(1)} %get-tuple-element.43.refs_3_, ...), custom_call_target="tpu_custom_call" | custom-call | flops 16777216 | bytes 393216 | tf_op jit(solution)/shard_map/backward/feature_gradient/pallas_call | solution.py:313
  42.1 1.3 %collective-permute-done.19 = bf16[128,256]{1,0:T(8,128)(2,1)S(1)} collective-permute-done((bf16[128,256]{1,0:T(8,128)(2,1)S(1)}, bf16[128,256]{1,0:T(8,128)(2,1)S(1)}, u32[]{:S(2)}, u32[]{:S(2)}) %collective-permute-start.19) | collective-permute-done | bytes 65568 | tf_op jit(solution)/shard_map/weight_levels/ppermute | solution.py:30
  43.5 0.7 %convert_multiply_fusion = f32[256,256]{1,0:T(8,128)} fusion(bf16[128,256]{1,0:T(8,128)(2,1)S(1)} %get-tuple-element.55, bf16[128,256]{1,0:T(8,128)(2,1)S(1)} %get-tuple-element.56, pred[]{:T(512)S(6)} %eq.3), kind=kLoop, calls=%fused_computation | loop fusion | flops 720896 | bytes 393217 | tf_op jit(solution)/shard_map/weight_levels/mul | solution.py:417
  (40 shorter events, 5.5 us)
Async XLA Ops:
  0.6 7.8 %collective-permute-start = (bf16[128,256]{1,0:T(8,128)(2,1)}, bf16[128,256]{1,0:T(8,128)(2,1)S(1)}, u32[]{:S(2)}, u32[]{:S(2)}) collective-permute-start(bf16[128,256]{1,0:T(8,128)(2,1)} %refs_4_.3), channel_id=1, source_target_pairs={{0,24},{8,16},{16,8},{24,0},{1,25},{9,17},{17,9},{25,1},{2,26},{10... | collective-permute-start | bytes 196616 | tf_op jit(solution)/shard_map/gather_features/ppermute | solution.py:30
  4.6 4.5 %collective-permute-start.1 = (bf16[128,256]{1,0:T(8,128)(2,1)}, bf16[128,256]{1,0:T(8,128)(2,1)S(1)}, u32[]{:S(2)}, u32[]{:S(2)}) collective-permute-start(bf16[128,256]{1,0:T(8,128)(2,1)} %refs_4_.3), channel_id=1, source_target_pairs={{0,16},{8,24},{16,0},{24,8},{1,17},{9,25},{17,1},{25,9},{2,18},{10... | collective-permute-start | bytes 196616 | tf_op jit(solution)/shard_map/gather_features/ppermute | solution.py:30
  5.1 4.5 %collective-permute-start.2 = (bf16[128,256]{1,0:T(8,128)(2,1)}, bf16[128,256]{1,0:T(8,128)(2,1)S(1)}, u32[]{:S(2)}, u32[]{:S(2)}) collective-permute-start(bf16[128,256]{1,0:T(8,128)(2,1)} %refs_4_.3), channel_id=1, source_target_pairs={{0,8},{8,0},{16,24},{24,16},{1,9},{9,1},{17,25},{25,17},{2,10},{10... | collective-permute-start | bytes 196616 | tf_op jit(solution)/shard_map/gather_features/ppermute | solution.py:30
  5.9 3.7 %copy-start = (bf16[128,256]{1,0:T(8,128)(2,1)S(1)}, bf16[128,256]{1,0:T(8,128)(2,1)}, u32[]{:S(2)}) copy-start(bf16[128,256]{1,0:T(8,128)(2,1)} %refs_4_.3) | copy-start | bytes 196612
  9.8 1.4 %collective-permute-start.3 = (bf16[256,256]{1,0:T(8,128)(2,1)S(1)}, bf16[256,256]{1,0:T(8,128)(2,1)S(1)}, u32[]{:S(2)}, u32[]{:S(2)}) collective-permute-start(bf16[256,256]{1,0:T(8,128)(2,1)S(1)} %forward_far.1), channel_id=1, source_target_pairs={{0,1},{1,0},{2,3},{3,2},{4,5},{5,4},{6,7},{7,6},{8,9},{9,8},{10,11... | collective-permute-start | bytes 393224 | tf_op jit(solution)/shard_map/forward/ppermute | solution.py:30
  10.3 4.7 %collective-permute-start.6 = (bf16[256,256]{1,0:T(8,128)(2,1)S(1)}, bf16[256,256]{1,0:T(8,128)(2,1)S(1)}, u32[]{:S(2)}, u32[]{:S(2)}) collective-permute-start(bf16[256,256]{1,0:T(8,128)(2,1)S(1)} %get-tuple-element.31), channel_id=1, source_target_pairs={{0,1},{1,0},{2,3},{3,2},{4,5},{5,4},{6,7},{7,6},{8,9},{9,8},{10,11... | collective-permute-start | bytes 393224 | tf_op jit(solution)/shard_map/forward/ppermute | solution.py:30
  11.3 6.4 %collective-permute-start.4 = (bf16[128,256]{1,0:T(8,128)(2,1)S(1)}, bf16[128,256]{1,0:T(8,128)(2,1)S(1)}, u32[]{:S(2)}, u32[]{:S(2)}) collective-permute-start(bf16[128,256]{1,0:T(8,128)(2,1)S(1)} %get-tuple-element.54), channel_id=1, source_target_pairs={{0,6},{1,7},{2,4},{3,5},{4,2},{5,3},{6,0},{7,1},{8,14},{9,15},{10,... | collective-permute-start | bytes 196616 | tf_op jit(solution)/shard_map/forward/ppermute | solution.py:30
  14.9 5.9 %collective-permute-start.5 = (bf16[128,256]{1,0:T(8,128)(2,1)S(1)}, bf16[128,256]{1,0:T(8,128)(2,1)S(1)}, u32[]{:S(2)}, u32[]{:S(2)}) collective-permute-start(bf16[128,256]{1,0:T(8,128)(2,1)S(1)} %get-tuple-element.53), channel_id=1, source_target_pairs={{0,4},{1,5},{2,6},{3,7},{4,0},{5,1},{6,2},{7,3},{8,12},{9,13},{10,... | collective-permute-start | bytes 196616 | tf_op jit(solution)/shard_map/forward/ppermute | solution.py:30
  15.0 5.8 %collective-permute-start.7 = (bf16[128,256]{1,0:T(8,128)(2,1)S(1)}, bf16[128,256]{1,0:T(8,128)(2,1)S(1)}, u32[]{:S(2)}, u32[]{:S(2)}) collective-permute-start(bf16[128,256]{1,0:T(8,128)(2,1)S(1)} %get-tuple-element.52), channel_id=1, source_target_pairs={{0,2},{1,3},{2,0},{3,1},{4,6},{5,7},{6,4},{7,5},{8,10},{9,11},{10,... | collective-permute-start | bytes 196616 | tf_op jit(solution)/shard_map/forward/ppermute | solution.py:30
  21.3 1.4 %collective-permute-start.8 = (bf16[256,256]{1,0:T(8,128)(2,1)S(1)}, bf16[256,256]{1,0:T(8,128)(2,1)S(1)}, u32[]{:S(2)}, u32[]{:S(2)}) collective-permute-start(bf16[256,256]{1,0:T(8,128)(2,1)S(1)} %pad_maximum_fusion.2), channel_id=1, source_target_pairs={{0,1},{1,0},{2,3},{3,2},{4,5},{5,4},{6,7},{7,6},{8,9},{9,8},{10,11... | collective-permute-start | bytes 393224 | tf_op jit(solution)/shard_map/gather_slopes/ppermute | solution.py:30
  21.4 7.5 %collective-permute-start.10 = (bf16[128,256]{1,0:T(8,128)(2,1)S(1)}, bf16[128,256]{1,0:T(8,128)(2,1)S(1)}, u32[]{:S(2)}, u32[]{:S(2)}) collective-permute-start(bf16[128,256]{1,0:T(8,128)(2,1)S(1)} %get-tuple-element.38.refs_1_), channel_id=1, source_target_pairs={{0,2},{1,3},{2,0},{3,1},{4,6},{5,7},{6,4},{7,5},{8,10},{9,11},{10,... | collective-permute-start | bytes 196616 | tf_op jit(solution)/shard_map/gather_slopes/ppermute | solution.py:30
  22.8 7.2 %collective-permute-start.9 = (bf16[256,256]{1,0:T(8,128)(2,1)S(1)}, bf16[256,256]{1,0:T(8,128)(2,1)S(1)}, u32[]{:S(2)}, u32[]{:S(2)}) collective-permute-start(bf16[256,256]{1,0:T(8,128)(2,1)S(1)} %pad_maximum_fusion.1), channel_id=1, source_target_pairs={{0,6},{1,5},{2,4},{3,7},{4,2},{5,1},{6,0},{7,3},{8,14},{9,13},{10,... | collective-permute-start | bytes 393224 | tf_op jit(solution)/shard_map/gather_slopes/ppermute | solution.py:35
  25.3 6.3 %collective-permute-start.15 = (bf16[128,256]{1,0:T(8,128)(2,1)S(1)}, bf16[128,256]{1,0:T(8,128)(2,1)S(1)}, u32[]{:S(2)}, u32[]{:S(2)}) collective-permute-start(bf16[128,256]{1,0:T(8,128)(2,1)S(1)} %add_convert_fusion.4), channel_id=1, source_target_pairs={{0,24},{8,16},{16,8},{24,0},{1,25},{9,17},{17,9},{25,1},{2,26},{10... | collective-permute-start | bytes 196616 | tf_op jit(solution)/shard_map/weight_rows/ppermute | solution.py:30
  27.3 4.4 %collective-permute-start.16 = (bf16[128,256]{1,0:T(8,128)(2,1)S(1)}, bf16[128,256]{1,0:T(8,128)(2,1)S(1)}, u32[]{:S(2)}, u32[]{:S(2)}) collective-permute-start(bf16[128,256]{1,0:T(8,128)(2,1)S(1)} %add_convert_fusion.4), channel_id=1, source_target_pairs={{0,16},{8,24},{16,0},{24,8},{1,17},{9,25},{17,1},{25,9},{2,18},{10... | collective-permute-start | bytes 196616 | tf_op jit(solution)/shard_map/weight_rows/ppermute | solution.py:30
  27.7 4.3 %collective-permute-start.17 = (bf16[128,256]{1,0:T(8,128)(2,1)S(1)}, bf16[128,256]{1,0:T(8,128)(2,1)S(1)}, u32[]{:S(2)}, u32[]{:S(2)}) collective-permute-start(bf16[128,256]{1,0:T(8,128)(2,1)S(1)} %add_convert_fusion.4), channel_id=1, source_target_pairs={{0,8},{8,0},{16,24},{24,16},{1,9},{9,1},{17,25},{25,17},{2,10},{10... | collective-permute-start | bytes 196616 | tf_op jit(solution)/shard_map/weight_rows/ppermute | solution.py:30
  29.9 4.0 %collective-permute-start.11 = (bf16[384,256]{1,0:T(8,128)(2,1)S(1)}, bf16[384,256]{1,0:T(8,128)(2,1)S(1)}, u32[]{:S(2)}, u32[]{:S(2)}) collective-permute-start(bf16[384,256]{1,0:T(8,128)(2,1)S(1)} %pad_maximum_fusion), channel_id=1, source_target_pairs={{0,1},{1,0},{2,3},{3,2},{4,5},{5,4},{6,7},{7,6},{8,9},{9,8},{10,11... | collective-permute-start | bytes 589832 | tf_op jit(solution)/shard_map/backward/ppermute | solution.py:30
  32.0 6.4 %collective-permute-start.18 = (bf16[128,256]{1,0:T(8,128)(2,1)S(1)}, bf16[128,256]{1,0:T(8,128)(2,1)S(1)}, u32[]{:S(2)}, u32[]{:S(2)}) collective-permute-start(bf16[128,256]{1,0:T(8,128)(2,1)S(1)} %add_convert_fusion.3), channel_id=1, source_target_pairs={{0,4},{1,5},{2,6},{3,7},{4,0},{5,1},{6,2},{7,3},{8,12},{9,13},{10,... | collective-permute-start | bytes 196616 | tf_op jit(solution)/shard_map/weight_levels/ppermute | solution.py:30
  34.3 5.3 %collective-permute-start.12 = (bf16[128,256]{1,0:T(8,128)(2,1)S(1)}, bf16[128,256]{1,0:T(8,128)(2,1)S(1)}, u32[]{:S(2)}, u32[]{:S(2)}) collective-permute-start(bf16[128,256]{1,0:T(8,128)(2,1)S(1)} %get-tuple-element.40), channel_id=1, source_target_pairs={{0,24},{8,16},{16,8},{24,0},{1,25},{9,17},{17,9},{25,1},{2,26},{10... | collective-permute-start | bytes 196616 | tf_op jit(solution)/shard_map/backward/ppermute | solution.py:30
  36.3 5.0 %collective-permute-start.13 = (bf16[128,256]{1,0:T(8,128)(2,1)S(1)}, bf16[128,256]{1,0:T(8,128)(2,1)S(1)}, u32[]{:S(2)}, u32[]{:S(2)}) collective-permute-start(bf16[128,256]{1,0:T(8,128)(2,1)S(1)} %get-tuple-element.41), channel_id=1, source_target_pairs={{0,16},{8,24},{16,0},{24,8},{1,17},{9,25},{17,1},{25,9},{2,18},{10... | collective-permute-start | bytes 196616 | tf_op jit(solution)/shard_map/backward/ppermute | solution.py:30
  36.7 4.6 %collective-permute-start.14 = (bf16[128,256]{1,0:T(8,128)(2,1)S(1)}, bf16[128,256]{1,0:T(8,128)(2,1)S(1)}, u32[]{:S(2)}, u32[]{:S(2)}) collective-permute-start(bf16[128,256]{1,0:T(8,128)(2,1)S(1)} %get-tuple-element.42), channel_id=1, source_target_pairs={{0,8},{8,0},{16,24},{24,16},{1,9},{9,1},{17,25},{25,17},{2,10},{10... | collective-permute-start | bytes 196616 | tf_op jit(solution)/shard_map/backward/ppermute | solution.py:30
  38.4 5.0 %collective-permute-start.19 = (bf16[128,256]{1,0:T(8,128)(2,1)S(1)}, bf16[128,256]{1,0:T(8,128)(2,1)S(1)}, u32[]{:S(2)}, u32[]{:S(2)}) collective-permute-start(bf16[128,256]{1,0:T(8,128)(2,1)S(1)} %add_convert_fusion.2), channel_id=1, source_target_pairs={{0,2},{1,3},{2,0},{3,1},{4,6},{5,7},{6,4},{7,5},{8,10},{9,11},{10,... | collective-permute-start | bytes 196616 | tf_op jit(solution)/shard_map/weight_levels/ppermute | solution.py:30
  39.1 4.4 %collective-permute-start.20 = (bf16[128,256]{1,0:T(8,128)(2,1)S(1)}, bf16[128,256]{1,0:T(8,128)(2,1)S(1)}, u32[]{:S(2)}, u32[]{:S(2)}) collective-permute-start(bf16[128,256]{1,0:T(8,128)(2,1)S(1)} %add_convert_fusion.2), channel_id=1, source_target_pairs={{0,3},{1,2},{2,1},{3,0},{4,7},{5,6},{6,5},{7,4},{8,11},{9,10},{10,... | collective-permute-start | bytes 196616 | tf_op jit(solution)/shard_map/weight_levels/ppermute | solution.py:30
  39.7 3.8 %collective-permute-start.21 = (bf16[128,256]{1,0:T(8,128)(2,1)S(1)}, bf16[128,256]{1,0:T(8,128)(2,1)S(1)}, u32[]{:S(2)}, u32[]{:S(2)}) collective-permute-start(bf16[128,256]{1,0:T(8,128)(2,1)S(1)} %add_convert_fusion.2), channel_id=1, source_target_pairs={{0,1},{1,0},{2,3},{3,2},{4,5},{5,4},{6,7},{7,6},{8,9},{9,8},{10,11... | collective-permute-start | bytes 196616 | tf_op jit(solution)/shard_map/weight_levels/ppermute | solution.py:30

commit v6 on v5

--- a/solution.py
+++ b/solution.py
@@ -345,7 +345,7 @@
     block = block_values.shape[3]
     row_blocks = node_count * col_devices // block
 
-    level_masks = [2 << i for i in reversed(range((levels - 1).bit_length()))]
+    level_masks = [(4 << i) - 2 for i in reversed(range((levels - 1).bit_length()))]
     row_order, level_order = far_first(row_devices), far_first(levels)
     with jax.named_scope("gather_features"):
         pieces = exchange([features] * row_devices, "row", 1)
@@ -371,7 +371,7 @@
     with jax.named_scope("gather_slopes"):
         arrived = swap(jnp.concatenate([slopes, weight_sent]), "col", 1)
         both = jnp.concatenate([slopes, arrived[:node_count]])
-        far_pairs = [(m, m - 1) for m in range(levels - 1, 1, -2)]
+        far_pairs = [(m - 1, m) for m in range(levels - 1, 1, -2)]
         far = [swap_by_core(both, 2 * m0, 2 * m1) for m0, m1 in far_pairs]
         near = swap(slopes, "col", 2)
 

time: 44.5 us -> 43.8 us (0.984)
  starting transfers between devices: 25.8 us -> 24 us
  waiting for transfers between devices: 10.5 us -> 11.5 us
    ppermute x1, waiting for transfers between devices: 1.04 us -> 3.54 us  [swap_by_core(): lax.ppermute(value, 'col', [(i, i ^ (mask1 if i & 1 else mask0)) for i in...]
    ppermute x21, waiting for transfers between devices: 9.49 us -> 7.97 us  [swap(): return lax.ppermute(value, axis, [(i, i ^ mask) for i in range(size)])]
    ppermute x21, starting transfers between devices: 23.3 us -> 22.1 us  [swap(): return lax.ppermute(value, axis, [(i, i ^ mask) for i in range(size)])]
    ppermute x1, starting transfers between devices: 2.54 us -> 1.85 us  [swap_by_core(): lax.ppermute(value, 'col', [(i, i ^ (mask1 if i & 1 else mask0)) for i in...]
  transfers between devices with their start and end apart: 22 -> 22, of which waited for: 13 -> 11; matrix products, arithmetic and copies ran while one was open for 0% -> 0% of each run, Pallas kernels for 11% -> 11%
where the time goes in v6:
time: 43.8 us; the launch traced here: 43.6 us
  starting transfers between devices  24 us (55%)
  waiting for transfers between devices  11.5 us (26%)
  Pallas kernels  5.71 us (13%)
  between operations  1.45 us (3%)
  other arithmetic  0.95 us (2%)
    ppermute x21, starting transfers between devices, swap(): return lax.ppermute(value, axis, [(i, i ^ mask) for i in range(size)])  22.1 us
    ppermute x21, waiting for transfers between devices, swap(): return lax.ppermute(value, axis, [(i, i ^ mask) for i in range(size)])  7.97 us
    ppermute x1, waiting for transfers between devices, swap_by_core(): lax.ppermute(value, 'col', [(i, i ^ (mask1 if i & 1 else mask0)) for i in...  3.54 us
    pallas_call x1, Pallas kernels, prep(): pl.pallas_call(functools.partial(prep_kernel, per_step), grid=(row_blocks...  2.7 us
    ppermute x1, starting transfers between devices, swap_by_core(): lax.ppermute(value, 'col', [(i, i ^ (mask1 if i & 1 else mask0)) for i in...  1.85 us
    pallas_call x3, Pallas kernels, product(): pl.pallas_call(functools.partial(product_kernel, len(parts), tuple(runs),...  1.03 us
  transfers between devices with their start and end apart: 22, of which 11 were waited for; matrix products, arithmetic and copies ran while one was open for 0% of the time, Pallas kernels for 11%

profile of v6, /device:TPU:0, one launch (start us, length us, event | category | flops | bytes accessed | tf_op | source)
XLA Modules:
  0.0 43.6 jit_solution(615128038567258901)
XLA Ops:
  0.6 4.0 %collective-permute-start = (bf16[128,256]{1,0:T(8,128)(2,1)}, bf16[128,256]{1,0:T(8,128)(2,1)S(1)}, u32[]{:S(2)}, u32[]{:S(2)}) collective-permute-start(bf16[128,256]{1,0:T(8,128)(2,1)} %refs_4_.3), channel_id=1, source_target_pairs={{0,24},{8,16},{16,8},{24,0},{1,25},{9,17},{17,9},{25,1},{2,26},{10... | collective-permute-start | bytes 196616 | tf_op jit(solution)/shard_map/gather_features/ppermute | solution.py:30
  5.9 2.7 %prep.1 = (bf16[1024,512]{1,0:T(8,128)(2,1)S(1)}, bf16[512,1024]{1,0:T(8,128)(2,1)S(1)}, bf16[256,256]{1,0:T(8,128)(2,1)S(1)}, f32[1,256]{1,0:T(1,128)S(1)}, bf16[128,256]{1,0:T(8,128)(2,1)S(1)}) custom-call(s32[1,1]{1,0:T(1,128)S(6)} %copy.12.count, s32[1,1,16]{2,1,0:T(1,128)} %rows_hbm.1, s32[1,1,16]{2,1,0:T(1,128)} %cols_hbm.1, s32[4,128]{1,0:T(4,128)} %bitcast.4, ...), custom_call_target="tpu_custom_call" | custom-call | flops 1073741824 | bytes 524288 | tf_op jit(solution)/shard_map/prep/pallas_call | solution.py:160
  10.3 0.6 %collective-permute-start.6 = (bf16[256,256]{1,0:T(8,128)(2,1)S(1)}, bf16[256,256]{1,0:T(8,128)(2,1)S(1)}, u32[]{:S(2)}, u32[]{:S(2)}) collective-permute-start(bf16[256,256]{1,0:T(8,128)(2,1)S(1)} %get-tuple-element.31), channel_id=1, source_target_pairs={{0,1},{1,0},{2,3},{3,2},{4,5},{5,4},{6,7},{7,6},{8,9},{9,8},{10,11... | collective-permute-start | bytes 393224 | tf_op jit(solution)/shard_map/forward/ppermute | solution.py:30
  11.3 3.7 %collective-permute-start.4 = (bf16[128,256]{1,0:T(8,128)(2,1)S(1)}, bf16[128,256]{1,0:T(8,128)(2,1)S(1)}, u32[]{:S(2)}, u32[]{:S(2)}) collective-permute-start(bf16[128,256]{1,0:T(8,128)(2,1)S(1)} %get-tuple-element.54), channel_id=1, source_target_pairs={{0,6},{1,7},{2,4},{3,5},{4,2},{5,3},{6,0},{7,1},{8,14},{9,15},{10,... | collective-permute-start | bytes 196616 | tf_op jit(solution)/shard_map/forward/ppermute | solution.py:30
  15.0 0.8 %collective-permute-start.7 = (bf16[128,256]{1,0:T(8,128)(2,1)S(1)}, bf16[128,256]{1,0:T(8,128)(2,1)S(1)}, u32[]{:S(2)}, u32[]{:S(2)}) collective-permute-start(bf16[128,256]{1,0:T(8,128)(2,1)S(1)} %get-tuple-element.52), channel_id=1, source_target_pairs={{0,2},{1,3},{2,0},{3,1},{4,6},{5,7},{6,4},{7,5},{8,10},{9,11},{10,... | collective-permute-start | bytes 196616 | tf_op jit(solution)/shard_map/forward/ppermute | solution.py:30
  15.8 1.8 %collective-permute-done.4.refs_0_ = bf16[128,256]{1,0:T(8,128)(2,1)S(1)} collective-permute-done((bf16[128,256]{1,0:T(8,128)(2,1)S(1)}, bf16[128,256]{1,0:T(8,128)(2,1)S(1)}, u32[]{:S(2)}, u32[]{:S(2)}) %collective-permute-start.4) | collective-permute-done | bytes 65568 | tf_op jit(solution)/shard_map/forward/ppermute | solution.py:30
  17.6 3.2 %collective-permute-done.5.refs_1_ = bf16[128,256]{1,0:T(8,128)(2,1)S(1)} collective-permute-done((bf16[128,256]{1,0:T(8,128)(2,1)S(1)}, bf16[128,256]{1,0:T(8,128)(2,1)S(1)}, u32[]{:S(2)}, u32[]{:S(2)}) %collective-permute-start.5) | collective-permute-done | bytes 65568 | tf_op jit(solution)/shard_map/forward/ppermute | solution.py:30
  21.4 1.2 %collective-permute-start.10 = (bf16[128,256]{1,0:T(8,128)(2,1)S(1)}, bf16[128,256]{1,0:T(8,128)(2,1)S(1)}, u32[]{:S(2)}, u32[]{:S(2)}) collective-permute-start(bf16[128,256]{1,0:T(8,128)(2,1)S(1)} %get-tuple-element.38.refs_1_), channel_id=1, source_target_pairs={{0,2},{1,3},{2,0},{3,1},{4,6},{5,7},{6,4},{7,5},{8,10},{9,11},{10,... | collective-permute-start | bytes 196616 | tf_op jit(solution)/shard_map/gather_slopes/ppermute | solution.py:30
  22.8 1.8 %collective-permute-start.9 = (bf16[256,256]{1,0:T(8,128)(2,1)S(1)}, bf16[256,256]{1,0:T(8,128)(2,1)S(1)}, u32[]{:S(2)}, u32[]{:S(2)}) collective-permute-start(bf16[256,256]{1,0:T(8,128)(2,1)S(1)} %pad_maximum_fusion.1), channel_id=1, source_target_pairs={{0,4},{1,7},{2,6},{3,5},{4,0},{5,3},{6,2},{7,1},{8,12},{9,15},{10,... | collective-permute-start | bytes 393224 | tf_op jit(solution)/shard_map/gather_slopes/ppermute | solution.py:35
  24.6 1.7 %collective-permute-start.15 = (bf16[128,256]{1,0:T(8,128)(2,1)S(1)}, bf16[128,256]{1,0:T(8,128)(2,1)S(1)}, u32[]{:S(2)}, u32[]{:S(2)}) collective-permute-start(bf16[128,256]{1,0:T(8,128)(2,1)S(1)} %add_convert_fusion.4), channel_id=1, source_target_pairs={{0,24},{8,16},{16,8},{24,0},{1,25},{9,17},{17,9},{25,1},{2,26},{10... | collective-permute-start | bytes 196616 | tf_op jit(solution)/shard_map/weight_rows/ppermute | solution.py:30
  26.4 0.6 %collective-permute-start.16 = (bf16[128,256]{1,0:T(8,128)(2,1)S(1)}, bf16[128,256]{1,0:T(8,128)(2,1)S(1)}, u32[]{:S(2)}, u32[]{:S(2)}) collective-permute-start(bf16[128,256]{1,0:T(8,128)(2,1)S(1)} %add_convert_fusion.4), channel_id=1, source_target_pairs={{0,16},{8,24},{16,0},{24,8},{1,17},{9,25},{17,1},{25,9},{2,18},{10... | collective-permute-start | bytes 196616 | tf_op jit(solution)/shard_map/weight_rows/ppermute | solution.py:30
  27.0 1.2 %collective-permute-start.17 = (bf16[128,256]{1,0:T(8,128)(2,1)S(1)}, bf16[128,256]{1,0:T(8,128)(2,1)S(1)}, u32[]{:S(2)}, u32[]{:S(2)}) collective-permute-start(bf16[128,256]{1,0:T(8,128)(2,1)S(1)} %add_convert_fusion.4), channel_id=1, source_target_pairs={{0,8},{8,0},{16,24},{24,16},{1,9},{9,1},{17,25},{25,17},{2,10},{10... | collective-permute-start | bytes 196616 | tf_op jit(solution)/shard_map/weight_rows/ppermute | solution.py:30
  28.2 3.5 %collective-permute-done.9.refs_3_ = bf16[256,256]{1,0:T(8,128)(2,1)S(1)} collective-permute-done((bf16[256,256]{1,0:T(8,128)(2,1)S(1)}, bf16[256,256]{1,0:T(8,128)(2,1)S(1)}, u32[]{:S(2)}, u32[]{:S(2)}) %collective-permute-start.9) | collective-permute-done | bytes 131104 | tf_op jit(solution)/shard_map/gather_slopes/ppermute | solution.py:35
  31.9 2.3 %collective-permute-start.18 = (bf16[128,256]{1,0:T(8,128)(2,1)S(1)}, bf16[128,256]{1,0:T(8,128)(2,1)S(1)}, u32[]{:S(2)}, u32[]{:S(2)}) collective-permute-start(bf16[128,256]{1,0:T(8,128)(2,1)S(1)} %add_convert_fusion.3), channel_id=1, source_target_pairs={{0,6},{1,7},{2,4},{3,5},{4,2},{5,3},{6,0},{7,1},{8,14},{9,15},{10,... | collective-permute-start | bytes 196616 | tf_op jit(solution)/shard_map/weight_levels/ppermute | solution.py:30
  34.7 1.8 %collective-permute-start.12 = (bf16[128,256]{1,0:T(8,128)(2,1)S(1)}, bf16[128,256]{1,0:T(8,128)(2,1)S(1)}, u32[]{:S(2)}, u32[]{:S(2)}) collective-permute-start(bf16[128,256]{1,0:T(8,128)(2,1)S(1)} %get-tuple-element.40), channel_id=1, source_target_pairs={{0,24},{8,16},{16,8},{24,0},{1,25},{9,17},{17,9},{25,1},{2,26},{10... | collective-permute-start | bytes 196616 | tf_op jit(solution)/shard_map/backward/ppermute | solution.py:30
  36.4 0.6 %collective-permute-start.13 = (bf16[128,256]{1,0:T(8,128)(2,1)S(1)}, bf16[128,256]{1,0:T(8,128)(2,1)S(1)}, u32[]{:S(2)}, u32[]{:S(2)}) collective-permute-start(bf16[128,256]{1,0:T(8,128)(2,1)S(1)} %get-tuple-element.41), channel_id=1, source_target_pairs={{0,16},{8,24},{16,0},{24,8},{1,17},{9,25},{17,1},{25,9},{2,18},{10... | collective-permute-start | bytes 196616 | tf_op jit(solution)/shard_map/backward/ppermute | solution.py:30
  37.0 1.2 %collective-permute-start.14 = (bf16[128,256]{1,0:T(8,128)(2,1)S(1)}, bf16[128,256]{1,0:T(8,128)(2,1)S(1)}, u32[]{:S(2)}, u32[]{:S(2)}) collective-permute-start(bf16[128,256]{1,0:T(8,128)(2,1)S(1)} %get-tuple-element.42), channel_id=1, source_target_pairs={{0,8},{8,0},{16,24},{24,16},{1,9},{9,1},{17,25},{25,17},{2,10},{10... | collective-permute-start | bytes 196616 | tf_op jit(solution)/shard_map/backward/ppermute | solution.py:30
  38.3 1.0 %collective-permute-start.20 = (bf16[128,256]{1,0:T(8,128)(2,1)S(1)}, bf16[128,256]{1,0:T(8,128)(2,1)S(1)}, u32[]{:S(2)}, u32[]{:S(2)}) collective-permute-start(bf16[128,256]{1,0:T(8,128)(2,1)S(1)} %add_convert_fusion.2), channel_id=1, source_target_pairs={{0,3},{1,2},{2,1},{3,0},{4,7},{5,6},{6,5},{7,4},{8,11},{9,10},{10,... | collective-permute-start | bytes 196616 | tf_op jit(solution)/shard_map/weight_levels/ppermute | solution.py:30
  39.4 0.6 %collective-permute-done.12.refs_0_ = bf16[128,256]{1,0:T(8,128)(2,1)S(1)} collective-permute-done((bf16[128,256]{1,0:T(8,128)(2,1)S(1)}, bf16[128,256]{1,0:T(8,128)(2,1)S(1)}, u32[]{:S(2)}, u32[]{:S(2)}) %collective-permute-start.12) | collective-permute-done | bytes 65568 | tf_op jit(solution)/shard_map/backward/ppermute | solution.py:30
  39.9 0.5 %collective-permute-start.21 = (bf16[128,256]{1,0:T(8,128)(2,1)S(1)}, bf16[128,256]{1,0:T(8,128)(2,1)S(1)}, u32[]{:S(2)}, u32[]{:S(2)}) collective-permute-start(bf16[128,256]{1,0:T(8,128)(2,1)S(1)} %add_convert_fusion.2), channel_id=1, source_target_pairs={{0,1},{1,0},{2,3},{3,2},{4,5},{5,4},{6,7},{7,6},{8,9},{9,8},{10,11... | collective-permute-start | bytes 196616 | tf_op jit(solution)/shard_map/weight_levels/ppermute | solution.py:30
  40.5 0.7 %activation.1 = bf16[128,256]{1,0:T(8,128)(2,1)} custom-call(f32[128,256]{1,0:T(8,128)S(1)} %get-tuple-element.36.preact_ref), custom_call_target="tpu_custom_call" | custom-call | flops 131072 | bytes 196608 | tf_op jit(solution)/shard_map/activation/pallas_call | solution.py:292
  41.3 0.8 %feature_gradient.1 = bf16[128,256]{1,0:T(8,128)(2,1)} custom-call(bf16[128,256]{1,0:T(8,128)(2,1)S(1)} %collective-permute-done.12.refs_0_, bf16[128,256]{1,0:T(8,128)(2,1)S(1)} %collective-permute-done.13.refs_1_, bf16[128,256]{1,0:T(8,128)(2,1)S(1)} %collective-permute-done.14.refs_2_, bf16[128,256]{1,0:T(8,128)(2,1)S(1)} %get-tuple-element.43.refs_3_, ...), custom_call_target="tpu_custom_call" | custom-call | flops 16777216 | bytes 393216 | tf_op jit(solution)/shard_map/backward/feature_gradient/pallas_call | solution.py:313
  42.2 0.6 %collective-permute-done.19 = bf16[128,256]{1,0:T(8,128)(2,1)S(1)} collective-permute-done((bf16[128,256]{1,0:T(8,128)(2,1)S(1)}, bf16[128,256]{1,0:T(8,128)(2,1)S(1)}, u32[]{:S(2)}, u32[]{:S(2)}) %collective-permute-start.19) | collective-permute-done | bytes 65568 | tf_op jit(solution)/shard_map/weight_levels/ppermute | solution.py:30
  42.8 0.7 %convert_multiply_fusion = f32[256,256]{1,0:T(8,128)} fusion(bf16[128,256]{1,0:T(8,128)(2,1)S(1)} %get-tuple-element.55, bf16[128,256]{1,0:T(8,128)(2,1)S(1)} %get-tuple-element.56, pred[]{:T(512)S(6)} %eq.3), kind=kLoop, calls=%fused_computation | loop fusion | flops 720896 | bytes 393217 | tf_op jit(solution)/shard_map/weight_levels/mul | solution.py:417
  (40 shorter events, 4.4 us)
Async XLA Ops:
  0.6 8.0 %collective-permute-start = (bf16[128,256]{1,0:T(8,128)(2,1)}, bf16[128,256]{1,0:T(8,128)(2,1)S(1)}, u32[]{:S(2)}, u32[]{:S(2)}) collective-permute-start(bf16[128,256]{1,0:T(8,128)(2,1)} %refs_4_.3), channel_id=1, source_target_pairs={{0,24},{8,16},{16,8},{24,0},{1,25},{9,17},{17,9},{25,1},{2,26},{10... | collective-permute-start | bytes 196616 | tf_op jit(solution)/shard_map/gather_features/ppermute | solution.py:30
  4.6 4.5 %collective-permute-start.1 = (bf16[128,256]{1,0:T(8,128)(2,1)}, bf16[128,256]{1,0:T(8,128)(2,1)S(1)}, u32[]{:S(2)}, u32[]{:S(2)}) collective-permute-start(bf16[128,256]{1,0:T(8,128)(2,1)} %refs_4_.3), channel_id=1, source_target_pairs={{0,16},{8,24},{16,0},{24,8},{1,17},{9,25},{17,1},{25,9},{2,18},{10... | collective-permute-start | bytes 196616 | tf_op jit(solution)/shard_map/gather_features/ppermute | solution.py:30
  5.1 4.5 %collective-permute-start.2 = (bf16[128,256]{1,0:T(8,128)(2,1)}, bf16[128,256]{1,0:T(8,128)(2,1)S(1)}, u32[]{:S(2)}, u32[]{:S(2)}) collective-permute-start(bf16[128,256]{1,0:T(8,128)(2,1)} %refs_4_.3), channel_id=1, source_target_pairs={{0,8},{8,0},{16,24},{24,16},{1,9},{9,1},{17,25},{25,17},{2,10},{10... | collective-permute-start | bytes 196616 | tf_op jit(solution)/shard_map/gather_features/ppermute | solution.py:30
  5.9 3.7 %copy-start = (bf16[128,256]{1,0:T(8,128)(2,1)S(1)}, bf16[128,256]{1,0:T(8,128)(2,1)}, u32[]{:S(2)}) copy-start(bf16[128,256]{1,0:T(8,128)(2,1)} %refs_4_.3) | copy-start | bytes 196612
  9.8 1.4 %collective-permute-start.3 = (bf16[256,256]{1,0:T(8,128)(2,1)S(1)}, bf16[256,256]{1,0:T(8,128)(2,1)S(1)}, u32[]{:S(2)}, u32[]{:S(2)}) collective-permute-start(bf16[256,256]{1,0:T(8,128)(2,1)S(1)} %forward_far.1), channel_id=1, source_target_pairs={{0,1},{1,0},{2,3},{3,2},{4,5},{5,4},{6,7},{7,6},{8,9},{9,8},{10,11... | collective-permute-start | bytes 393224 | tf_op jit(solution)/shard_map/forward/ppermute | solution.py:30
  10.3 4.7 %collective-permute-start.6 = (bf16[256,256]{1,0:T(8,128)(2,1)S(1)}, bf16[256,256]{1,0:T(8,128)(2,1)S(1)}, u32[]{:S(2)}, u32[]{:S(2)}) collective-permute-start(bf16[256,256]{1,0:T(8,128)(2,1)S(1)} %get-tuple-element.31), channel_id=1, source_target_pairs={{0,1},{1,0},{2,3},{3,2},{4,5},{5,4},{6,7},{7,6},{8,9},{9,8},{10,11... | collective-permute-start | bytes 393224 | tf_op jit(solution)/shard_map/forward/ppermute | solution.py:30
  11.3 6.4 %collective-permute-start.4 = (bf16[128,256]{1,0:T(8,128)(2,1)S(1)}, bf16[128,256]{1,0:T(8,128)(2,1)S(1)}, u32[]{:S(2)}, u32[]{:S(2)}) collective-permute-start(bf16[128,256]{1,0:T(8,128)(2,1)S(1)} %get-tuple-element.54), channel_id=1, source_target_pairs={{0,6},{1,7},{2,4},{3,5},{4,2},{5,3},{6,0},{7,1},{8,14},{9,15},{10,... | collective-permute-start | bytes 196616 | tf_op jit(solution)/shard_map/forward/ppermute | solution.py:30
  14.9 5.9 %collective-permute-start.5 = (bf16[128,256]{1,0:T(8,128)(2,1)S(1)}, bf16[128,256]{1,0:T(8,128)(2,1)S(1)}, u32[]{:S(2)}, u32[]{:S(2)}) collective-permute-start(bf16[128,256]{1,0:T(8,128)(2,1)S(1)} %get-tuple-element.53), channel_id=1, source_target_pairs={{0,4},{1,5},{2,6},{3,7},{4,0},{5,1},{6,2},{7,3},{8,12},{9,13},{10,... | collective-permute-start | bytes 196616 | tf_op jit(solution)/shard_map/forward/ppermute | solution.py:30
  15.0 5.8 %collective-permute-start.7 = (bf16[128,256]{1,0:T(8,128)(2,1)S(1)}, bf16[128,256]{1,0:T(8,128)(2,1)S(1)}, u32[]{:S(2)}, u32[]{:S(2)}) collective-permute-start(bf16[128,256]{1,0:T(8,128)(2,1)S(1)} %get-tuple-element.52), channel_id=1, source_target_pairs={{0,2},{1,3},{2,0},{3,1},{4,6},{5,7},{6,4},{7,5},{8,10},{9,11},{10,... | collective-permute-start | bytes 196616 | tf_op jit(solution)/shard_map/forward/ppermute | solution.py:30
  21.3 1.4 %collective-permute-start.8 = (bf16[256,256]{1,0:T(8,128)(2,1)S(1)}, bf16[256,256]{1,0:T(8,128)(2,1)S(1)}, u32[]{:S(2)}, u32[]{:S(2)}) collective-permute-start(bf16[256,256]{1,0:T(8,128)(2,1)S(1)} %pad_maximum_fusion.2), channel_id=1, source_target_pairs={{0,1},{1,0},{2,3},{3,2},{4,5},{5,4},{6,7},{7,6},{8,9},{9,8},{10,11... | collective-permute-start | bytes 393224 | tf_op jit(solution)/shard_map/gather_slopes/ppermute | solution.py:30
  21.4 6.8 %collective-permute-start.10 = (bf16[128,256]{1,0:T(8,128)(2,1)S(1)}, bf16[128,256]{1,0:T(8,128)(2,1)S(1)}, u32[]{:S(2)}, u32[]{:S(2)}) collective-permute-start(bf16[128,256]{1,0:T(8,128)(2,1)S(1)} %get-tuple-element.38.refs_1_), channel_id=1, source_target_pairs={{0,2},{1,3},{2,0},{3,1},{4,6},{5,7},{6,4},{7,5},{8,10},{9,11},{10,... | collective-permute-start | bytes 196616 | tf_op jit(solution)/shard_map/gather_slopes/ppermute | solution.py:30
  22.8 9.0 %collective-permute-start.9 = (bf16[256,256]{1,0:T(8,128)(2,1)S(1)}, bf16[256,256]{1,0:T(8,128)(2,1)S(1)}, u32[]{:S(2)}, u32[]{:S(2)}) collective-permute-start(bf16[256,256]{1,0:T(8,128)(2,1)S(1)} %pad_maximum_fusion.1), channel_id=1, source_target_pairs={{0,4},{1,7},{2,6},{3,5},{4,0},{5,3},{6,2},{7,1},{8,12},{9,15},{10,... | collective-permute-start | bytes 393224 | tf_op jit(solution)/shard_map/gather_slopes/ppermute | solution.py:35
  24.6 7.2 %collective-permute-start.15 = (bf16[128,256]{1,0:T(8,128)(2,1)S(1)}, bf16[128,256]{1,0:T(8,128)(2,1)S(1)}, u32[]{:S(2)}, u32[]{:S(2)}) collective-permute-start(bf16[128,256]{1,0:T(8,128)(2,1)S(1)} %add_convert_fusion.4), channel_id=1, source_target_pairs={{0,24},{8,16},{16,8},{24,0},{1,25},{9,17},{17,9},{25,1},{2,26},{10... | collective-permute-start | bytes 196616 | tf_op jit(solution)/shard_map/weight_rows/ppermute | solution.py:30
  26.4 5.5 %collective-permute-start.16 = (bf16[128,256]{1,0:T(8,128)(2,1)S(1)}, bf16[128,256]{1,0:T(8,128)(2,1)S(1)}, u32[]{:S(2)}, u32[]{:S(2)}) collective-permute-start(bf16[128,256]{1,0:T(8,128)(2,1)S(1)} %add_convert_fusion.4), channel_id=1, source_target_pairs={{0,16},{8,24},{16,0},{24,8},{1,17},{9,25},{17,1},{25,9},{2,18},{10... | collective-permute-start | bytes 196616 | tf_op jit(solution)/shard_map/weight_rows/ppermute | solution.py:30
  27.0 4.9 %collective-permute-start.17 = (bf16[128,256]{1,0:T(8,128)(2,1)S(1)}, bf16[128,256]{1,0:T(8,128)(2,1)S(1)}, u32[]{:S(2)}, u32[]{:S(2)}) collective-permute-start(bf16[128,256]{1,0:T(8,128)(2,1)S(1)} %add_convert_fusion.4), channel_id=1, source_target_pairs={{0,8},{8,0},{16,24},{24,16},{1,9},{9,1},{17,25},{25,17},{2,10},{10... | collective-permute-start | bytes 196616 | tf_op jit(solution)/shard_map/weight_rows/ppermute | solution.py:30
  31.7 2.5 %collective-permute-start.11 = (bf16[384,256]{1,0:T(8,128)(2,1)S(1)}, bf16[384,256]{1,0:T(8,128)(2,1)S(1)}, u32[]{:S(2)}, u32[]{:S(2)}) collective-permute-start(bf16[384,256]{1,0:T(8,128)(2,1)S(1)} %pad_maximum_fusion), channel_id=1, source_target_pairs={{0,1},{1,0},{2,3},{3,2},{4,5},{5,4},{6,7},{7,6},{8,9},{9,8},{10,11... | collective-permute-start | bytes 589832 | tf_op jit(solution)/shard_map/backward/ppermute | solution.py:30
  31.9 6.3 %collective-permute-start.18 = (bf16[128,256]{1,0:T(8,128)(2,1)S(1)}, bf16[128,256]{1,0:T(8,128)(2,1)S(1)}, u32[]{:S(2)}, u32[]{:S(2)}) collective-permute-start(bf16[128,256]{1,0:T(8,128)(2,1)S(1)} %add_convert_fusion.3), channel_id=1, source_target_pairs={{0,6},{1,7},{2,4},{3,5},{4,2},{5,3},{6,0},{7,1},{8,14},{9,15},{10,... | collective-permute-start | bytes 196616 | tf_op jit(solution)/shard_map/weight_levels/ppermute | solution.py:30
  34.7 5.3 %collective-permute-start.12 = (bf16[128,256]{1,0:T(8,128)(2,1)S(1)}, bf16[128,256]{1,0:T(8,128)(2,1)S(1)}, u32[]{:S(2)}, u32[]{:S(2)}) collective-permute-start(bf16[128,256]{1,0:T(8,128)(2,1)S(1)} %get-tuple-element.40), channel_id=1, source_target_pairs={{0,24},{8,16},{16,8},{24,0},{1,25},{9,17},{17,9},{25,1},{2,26},{10... | collective-permute-start | bytes 196616 | tf_op jit(solution)/shard_map/backward/ppermute | solution.py:30
  36.4 4.8 %collective-permute-start.13 = (bf16[128,256]{1,0:T(8,128)(2,1)S(1)}, bf16[128,256]{1,0:T(8,128)(2,1)S(1)}, u32[]{:S(2)}, u32[]{:S(2)}) collective-permute-start(bf16[128,256]{1,0:T(8,128)(2,1)S(1)} %get-tuple-element.41), channel_id=1, source_target_pairs={{0,16},{8,24},{16,0},{24,8},{1,17},{9,25},{17,1},{25,9},{2,18},{10... | collective-permute-start | bytes 196616 | tf_op jit(solution)/shard_map/backward/ppermute | solution.py:30
  37.0 4.3 %collective-permute-start.14 = (bf16[128,256]{1,0:T(8,128)(2,1)S(1)}, bf16[128,256]{1,0:T(8,128)(2,1)S(1)}, u32[]{:S(2)}, u32[]{:S(2)}) collective-permute-start(bf16[128,256]{1,0:T(8,128)(2,1)S(1)} %get-tuple-element.42), channel_id=1, source_target_pairs={{0,8},{8,0},{16,24},{24,16},{1,9},{9,1},{17,25},{25,17},{2,10},{10... | collective-permute-start | bytes 196616 | tf_op jit(solution)/shard_map/backward/ppermute | solution.py:30
  38.3 4.5 %collective-permute-start.19 = (bf16[128,256]{1,0:T(8,128)(2,1)S(1)}, bf16[128,256]{1,0:T(8,128)(2,1)S(1)}, u32[]{:S(2)}, u32[]{:S(2)}) collective-permute-start(bf16[128,256]{1,0:T(8,128)(2,1)S(1)} %add_convert_fusion.2), channel_id=1, source_target_pairs={{0,2},{1,3},{2,0},{3,1},{4,6},{5,7},{6,4},{7,5},{8,10},{9,11},{10,... | collective-permute-start | bytes 196616 | tf_op jit(solution)/shard_map/weight_levels/ppermute | solution.py:30
  38.3 4.5 %collective-permute-start.20 = (bf16[128,256]{1,0:T(8,128)(2,1)S(1)}, bf16[128,256]{1,0:T(8,128)(2,1)S(1)}, u32[]{:S(2)}, u32[]{:S(2)}) collective-permute-start(bf16[128,256]{1,0:T(8,128)(2,1)S(1)} %add_convert_fusion.2), channel_id=1, source_target_pairs={{0,3},{1,2},{2,1},{3,0},{4,7},{5,6},{6,5},{7,4},{8,11},{9,10},{10,... | collective-permute-start | bytes 196616 | tf_op jit(solution)/shard_map/weight_levels/ppermute | solution.py:30
  39.9 2.9 %collective-permute-start.21 = (bf16[128,256]{1,0:T(8,128)(2,1)S(1)}, bf16[128,256]{1,0:T(8,128)(2,1)S(1)}, u32[]{:S(2)}, u32[]{:S(2)}) collective-permute-start(bf16[128,256]{1,0:T(8,128)(2,1)S(1)} %add_convert_fusion.2), channel_id=1, source_target_pairs={{0,1},{1,0},{2,3},{3,2},{4,5},{5,4},{6,7},{7,6},{8,9},{9,8},{10,11... | collective-permute-start | bytes 196616 | tf_op jit(solution)/shard_map/weight_levels/ppermute | solution.py:30
